TPU v7x, 256 devices: a whole 4x4x8 slice. The times are simulated.
256 devices in a mesh: dp: 4 (over x), owner: 64 (over z, y, core).
Axes of the slice: x: 4, y: 4, z: 8, core: 2. Of those that a mesh axis runs over, the one named last changes fastest.
Arguments:
- tokens: bfloat16 [32768, 2048], P(('dp', 'owner')), may hold values from -6 to 6
- grads: bfloat16 [32768, 8, 768], P(('dp', 'owner')), may hold values from -0.19921875 to 0.19921875
- routing: int32 [32768, 8], P(('dp', 'owner')), may hold values from 0 to 127, as said below
- basis_in: bfloat16 [64, 2048, 2048], P('owner'), may hold values from -0.125 to 0.125
- basis_out: bfloat16 [64, 768, 768], P('owner'), may hold values from -0.21875 to 0.21875
Outputs:
- eigenvalues: float32 [2048, 64, 768], P('dp', 'owner')
Inputs may be any that keep to these rules, and one draw needn't show every extreme that they name: `routing`: in each device's block of 128 tokens no expert is chosen by more than 16 tokens, and some expert below 64 is chosen by exactly 16 tokens of every block. The 8 experts of one token differ.
All inputs are finite; a program needn't handle non-finite values.
Results may differ from a plain program's by a relative error of at most 0.00048.
Values may be sent and summed in bfloat16 or wider, within the bound.
No kernel may reach another device: no remote copies, remote signals or barrier semaphores. Data moves between devices by JAX's collectives and lax.ppermute only.
A program may use at most 128 MiB of HBM per device.

v0:
```python
import functools

import jax
import jax.numpy as jnp
from jax import lax
from jax.experimental import pallas as pl
from jax.experimental.pallas import tpu as pltpu
from jax.sharding import Mesh
from jax.sharding import PartitionSpec as P

CAP = 16
N_X, N_Z, N_Y, N_C = 4, 8, 4, 2
N_YC = N_Y * N_C
FIRST = (0, 1, 7, 2, 6, 3, 5)
SECOND = (4,)
ORDER = FIRST + SECOND
TOK = 128
TOP = 8
D = 2048
WIDE = D // 2
FF = 768
EXPERTS = 64
ROWS = EXPERTS * CAP
QUARTER = D // N_X
HALF = QUARTER // 2
CODE_ROWS = HALF + 16
BF = jnp.bfloat16
F32 = jnp.float32
I32 = jnp.int32
MIB = 1024 * 1024
IN_SMEM = pl.BlockSpec(memory_space=pltpu.SMEM)
IN_VMEM = pl.BlockSpec(memory_space=pltpu.VMEM)


def iota(shape, dim):
    return lax.broadcasted_iota(I32, shape, dim)


def params(mib):
    return pltpu.CompilerParams(vmem_limit_bytes=mib * MIB)


def ones_where(mask):
    return jnp.where(mask, 1.0, 0.0).astype(BF)


def earlier(n):
    return ones_where(iota((n, n), 0) < iota((n, n), 1))


def stage_kernel(tokens_ref, routing_ref, left_ref, right_ref):
    left_ref[0:TOK, :] = tokens_ref[:, 0:WIDE]
    left_ref[TOK:, :] = jnp.zeros((TOP, WIDE), BF)
    left_ref[TOK:, 0:TOK] = routing_ref[...].astype(F32).astype(BF)
    right_ref[...] = tokens_ref[:, WIDE:]


def stage(tokens, routing):
    return pl.pallas_call(
        stage_kernel,
        out_shape=(
            jax.ShapeDtypeStruct((TOK + TOP, WIDE), BF),
            jax.ShapeDtypeStruct((TOK, WIDE), BF),
        ),
        compiler_params=params(60),
    )(tokens, routing)


def pack_grads_kernel(here_ref, flat_ref, grads_ref, out_ref):
    pairs = TOK * TOP
    flat = flat_ref[...]
    hit = iota((EXPERTS, pairs), 0) == flat
    before = jnp.dot(ones_where(hit), earlier(pairs), preferred_element_type=F32)
    rank = jnp.sum(jnp.where(hit, before, 0.0), axis=0, keepdims=True).astype(I32)
    along_z = (flat // N_YC + N_Z - here_ref[0]) % N_Z
    slot = jnp.where(flat < EXPERTS, (flat % N_YC) * TOK + along_z * CAP + rank, -1)
    grads = grads_ref[...]
    for k in range(N_YC):
        pick = ones_where(iota((TOK, pairs), 0) + k * TOK == slot)
        out_ref[k] = jnp.dot(pick, grads, preferred_element_type=F32).astype(BF)


def pack_grads(here, flat, grads):
    return pl.pallas_call(
        pack_grads_kernel,
        out_shape=jax.ShapeDtypeStruct((N_YC, N_Z * CAP, FF), BF),
        in_specs=[IN_SMEM] + [IN_VMEM] * 2,
        out_specs=IN_VMEM,
        compiler_params=params(60),
        cost_estimate=pl.CostEstimate(
            flops=2 * ROWS * ROWS * FF, bytes_accessed=4 * ROWS * FF, transcendentals=0
        ),
    )(here, flat, grads)


def regroup_kernel(*refs):
    in_ref, out_refs = refs[0], refs[-N_Z:]
    for k, out_ref in enumerate(out_refs):
        for i in range(N_YC):
            out_ref[i * CAP : (i + 1) * CAP, :] = in_ref[i, k * CAP : (k + 1) * CAP, :]


def regroup(blocks, others):
    return pl.pallas_call(
        regroup_kernel,
        out_shape=[jax.ShapeDtypeStruct((N_YC * CAP, FF), BF)] * N_Z,
        in_specs=[IN_VMEM] + [pl.BlockSpec(memory_space=pl.ANY)] * len(others),
        out_specs=[IN_VMEM] * N_Z,
        compiler_params=params(60),
    )(blocks, *others)


def pack_tokens_kernel(n, here_ref, *refs):
    lefts, rights, out_ref = refs[:n], refs[n : 2 * n], refs[-1]
    expert = iota((N_YC, TOK), 0) + here_ref[0] * N_YC
    rank = iota((CAP, TOK), 0)
    ahead = earlier(TOK)
    for b, (left, right) in enumerate(zip(lefts, rights)):
        routing = left[TOK:, 0:TOK].astype(F32).astype(I32)
        member = jnp.zeros((N_YC, TOK), F32)
        for j in range(TOP):
            member += jnp.where(routing[j : j + 1, :] == expert, 1.0, 0.0)
        before = jnp.dot(member.astype(BF), ahead, preferred_element_type=F32)
        slot = jnp.where(member > 0, before, -1.0).astype(I32)
        pick = jnp.concatenate([ones_where(slot[k : k + 1, :] == rank) for k in range(N_YC)], axis=0)
        for at, rows_ref in ((0, left), (WIDE, right)):
            rows = jnp.dot(pick, rows_ref[0:TOK, :], preferred_element_type=F32).astype(BF)
            out_ref[:, b * CAP : (b + 1) * CAP, at : at + WIDE] = rows.reshape(N_YC, CAP, WIDE)


def pack_tokens(here, lefts, rights, gates):
    n = len(lefts)
    return pl.pallas_call(
        functools.partial(pack_tokens_kernel, n),
        out_shape=jax.ShapeDtypeStruct((N_YC, n * CAP, D), BF),
        in_specs=[IN_SMEM] + [IN_VMEM] * (2 * n) + [pl.BlockSpec(memory_space=pl.ANY)] * len(gates),
        out_specs=IN_VMEM,
        compiler_params=params(60),
        cost_estimate=pl.CostEstimate(
            flops=2 * n * TOK * TOK * D, bytes_accessed=4 * n * TOK * D, transcendentals=0
        ),
    )(here, *lefts, *rights, *gates)


STRIP = 512


def rotate_kernel(parts_ref, basis_ref, out_ref, rows_ref):
    @pl.when(pl.program_id(0) == 0)
    def _():
        for k in range(N_YC):
            for b in range(rows_ref.shape[0] // TOK):
                start = b * TOK + k * CAP
                rows_ref[start : start + CAP, :] = parts_ref[k, b * CAP : (b + 1) * CAP, :]

    rotated = jnp.dot(rows_ref[...], basis_ref[0], preferred_element_type=F32)
    out_ref[...] = jnp.transpose(rotated * rotated).astype(BF)


def rotate_inputs(parts, basis_in):
    rows = parts.shape[1] * N_YC
    return pl.pallas_call(
        rotate_kernel,
        out_shape=jax.ShapeDtypeStruct((D, rows), BF),
        grid=(D // STRIP,),
        in_specs=[
            pl.BlockSpec(parts.shape, lambda i: (0, 0, 0)),
            pl.BlockSpec((1, D, STRIP), lambda i: (0, 0, i)),
        ],
        out_specs=pl.BlockSpec((STRIP, rows), lambda i: (i, 0)),
        scratch_shapes=[pltpu.VMEM((rows, D), BF)],
        compiler_params=params(50),
        cost_estimate=pl.CostEstimate(
            flops=2 * rows * D * D, bytes_accessed=2 * D * D + 4 * rows * D, transcendentals=0
        ),
    )(parts, basis_in)


def encode(values, out_ref):
    most = jnp.max(values, axis=0, keepdims=True)
    power = jnp.clip(jnp.ceil(jnp.log2(jnp.maximum(most, 1e-37))), -126.0, 126.0)
    scaled = (values * jnp.exp2(-power)) * 65535.0 + 0.5
    code = jnp.minimum(scaled.astype(I32), 65535) - 32768
    out_ref[0:HALF, :] = code.astype(jnp.int16)
    out_ref[HALF:CODE_ROWS, :] = jnp.broadcast_to(power.astype(I32), (16, FF)).astype(jnp.int16)


def decode(code_ref):
    power = code_ref[HALF:CODE_ROWS, :].astype(I32)[0:1, :].astype(F32)
    value = (code_ref[0:HALF, :].astype(I32) + 32768).astype(F32)
    return value * (jnp.exp2(power) * (1.0 / 65535.0))


CODE = jax.ShapeDtypeStruct((CODE_ROWS, FF), jnp.int16)
BLOCK = jax.ShapeDtypeStruct((HALF, FF), F32)


N_FIRST = len(FIRST) * TOK


def block_sum(a_refs, g_ref, quarter, half):
    start = pl.multiple_of(quarter * QUARTER + half * HALF, HALF)
    first, second = a_refs
    return jnp.dot(
        first[pl.ds(start, HALF), :], g_ref[0:N_FIRST, :], preferred_element_type=F32
    ) + jnp.dot(second[pl.ds(start, HALF), :], g_ref[N_FIRST:, :], preferred_element_type=F32)


def far_kernel(place_ref, *refs):
    rows_refs, (basis_ref, first, second, g_ref, up_ref, down_ref) = refs[:N_Z], refs[N_Z:]
    for k, rows_ref in enumerate(rows_refs):
        rotated = jnp.dot(rows_ref[...], basis_ref[0], preferred_element_type=F32)
        g_ref[k * TOK : (k + 1) * TOK, :] = (rotated * rotated).astype(BF)
    encode(block_sum((first, second), g_ref, place_ref[0], 0), up_ref)
    encode(block_sum((first, second), g_ref, place_ref[0], 1), down_ref)


def far_blocks(place, rows, basis_out, a_sq):
    return pl.pallas_call(
        far_kernel,
        out_shape=(jax.ShapeDtypeStruct((ROWS, FF), BF), CODE, CODE),
        in_specs=[IN_SMEM] + [IN_VMEM] * (N_Z + 3),
        out_specs=[IN_VMEM] * 3,
        compiler_params=params(8),
        cost_estimate=pl.CostEstimate(
            flops=2 * ROWS * FF * (FF + QUARTER), bytes_accessed=12 << 20, transcendentals=0
        ),
    )(place, *rows, basis_out, *a_sq)


def near_kernel(place_ref, first, second, g_ref, up_ref, down_ref):
    encode(block_sum((first, second), g_ref, place_ref[1], 1), up_ref)
    encode(block_sum((first, second), g_ref, place_ref[2], 0), down_ref)


def near_blocks(place, a_sq, g_sq):
    return pl.pallas_call(
        near_kernel,
        out_shape=(CODE, CODE),
        in_specs=[IN_SMEM] + [IN_VMEM] * 3,
        out_specs=[IN_VMEM] * 2,
        compiler_params=params(4),
        cost_estimate=pl.CostEstimate(
            flops=2 * ROWS * FF * QUARTER, bytes_accessed=4 << 20, transcendentals=0
        ),
    )(place, *a_sq, g_sq)


def rest_kernel(place_ref, first, second, g_ref, up_ref, down_ref, own_ref):
    a_refs = (first, second)
    up_ref[...] = block_sum(a_refs, g_ref, place_ref[1], 0)
    down_ref[...] = block_sum(a_refs, g_ref, place_ref[2], 1)
    own_ref[0:HALF, :] = block_sum(a_refs, g_ref, place_ref[3], 0)
    own_ref[HALF:QUARTER, :] = block_sum(a_refs, g_ref, place_ref[3], 1)


def rest_blocks(place, a_sq, g_sq):
    return pl.pallas_call(
        rest_kernel,
        out_shape=(BLOCK, BLOCK, jax.ShapeDtypeStruct((QUARTER, FF), F32)),
        in_specs=[IN_SMEM] + [IN_VMEM] * 3,
        out_specs=[IN_VMEM] * 3,
        compiler_params=params(4),
        cost_estimate=pl.CostEstimate(
            flops=4 * ROWS * FF * QUARTER, bytes_accessed=8 << 20, transcendentals=0
        ),
    )(place, *a_sq, g_sq)


def pass_on_kernel(up_ref, down_ref, got_up_ref, got_down_ref, out_up_ref, out_down_ref):
    encode(up_ref[...] + decode(got_up_ref), out_up_ref)
    encode(down_ref[...] + decode(got_down_ref), out_down_ref)


def pass_on(up, down, got_up, got_down):
    return pl.pallas_call(
        pass_on_kernel,
        out_shape=(CODE, CODE),
        in_specs=[IN_VMEM] * 4,
        out_specs=[IN_VMEM] * 2,
        compiler_params=params(4),
    )(up, down, got_up, got_down)


LANES = 128
SPLIT = FF // LANES


def finish_kernel(own_ref, top_a_ref, top_b_ref, bottom_a_ref, bottom_b_ref, out_ref):
    top = own_ref[0:HALF, :] + decode(top_a_ref) + decode(top_b_ref)
    bottom = own_ref[HALF:QUARTER, :] + decode(bottom_a_ref) + decode(bottom_b_ref)
    for k in range(SPLIT):
        lanes = slice(k * LANES, (k + 1) * LANES)
        out_ref[pl.ds(k, HALF, stride=SPLIT), :] = top[:, lanes]
        out_ref[pl.ds(HALF * SPLIT + k, HALF, stride=SPLIT), :] = bottom[:, lanes]


def finish(own, top_a, top_b, bottom_a, bottom_b):
    return pl.pallas_call(
        finish_kernel,
        out_shape=jax.ShapeDtypeStruct((QUARTER * SPLIT, LANES), F32),
        in_specs=[IN_VMEM] * 5,
        out_specs=IN_VMEM,
        compiler_params=params(4),
    )(own, top_a, top_b, bottom_a, bottom_b)


def shift(value, axis, by):
    n = lax.axis_size(axis)
    return lax.ppermute(value, axis, [(i, (i + by) % n) for i in range(n)])


def to_owners(value):
    return lax.all_to_all(value, ("y", "c"), split_axis=0, concat_axis=0, tiled=True)


def z_ring(left, right):
    up, down = {0: (left, right)}, {0: (left, right)}
    for step in (1, 2, 3):
        up[step] = tuple(shift(v, "z", 1) for v in up[step - 1])
        down[step] = tuple(shift(v, "z", -1) for v in down[step - 1])
    ring = {**up, **{N_Z - step: down[step] for step in (1, 2, 3)}}
    ring[4] = (shift(up[3][0], "z", 1), shift(down[3][1], "z", -1))
    return ring


def on_device(tokens, grads, routing, basis_in, basis_out):
    x, z = lax.axis_index("x"), lax.axis_index("z")
    place = jnp.stack([x ^ 2, (x + 1) & 3, (x + 3) & 3, x]).astype(I32)
    here = z.astype(I32).reshape(1)

    ring = z_ring(*stage(tokens, routing.T))
    packed = pack_grads(here, routing.reshape(1, TOK * TOP), grads.reshape(TOK * TOP, FF))
    grads_in = to_owners(packed)
    by_z = regroup(grads_in, [*ring[3], *ring[5]])
    rows_out = [by_z[k] if k == 0 else shift(by_z[k], "z", k) for k in ORDER]

    a_sq, gates = [], [grads_in]
    for senders in (FIRST, SECOND):
        rows_in = pack_tokens(
            here, [ring[k][0] for k in senders], [ring[k][1] for k in senders], gates
        )
        rows_in = to_owners(rows_in)
        gates = [rows_in, by_z[0], rows_out[ORDER.index(3)], rows_out[ORDER.index(5)]]
        a_sq.append(rotate_inputs(rows_in, basis_in))

    g_sq, far_up, far_down = far_blocks(place, rows_out, basis_out, a_sq)
    got_far_up, got_far_down = shift(far_up, "x", 1), shift(far_down, "x", -1)
    near_up, near_down = near_blocks(place, a_sq, g_sq)
    got_near_up, got_near_down = shift(near_up, "x", 1), shift(near_down, "x", -1)
    up, down, own = rest_blocks(place, a_sq, g_sq)
    up, down = pass_on(up, down, got_far_up, got_far_down)
    got_up, got_down = shift(up, "x", 1), shift(down, "x", -1)
    values = finish(own, got_up, got_near_down, got_near_up, got_down)
    return values.reshape(QUARTER, 1, FF)


def solution(mesh):
    split = Mesh(mesh.devices.reshape(N_X, N_Z, N_Y, N_C), ("x", "z", "y", "c"))
    owner = ("z", "y", "c")
    everywhere = ("x", "z", "y", "c")
    return jax.shard_map(
        on_device,
        mesh=split,
        in_specs=(
            P(everywhere, None),
            P(everywhere, None, None),
            P(everywhere, None),
            P(owner, None, None),
            P(owner, None, None),
        ),
        out_specs=P("x", owner, None),
        check_vma=False,
    )
```

profile of v0, /device:TPU:6, one launch (start us, length us, event | category | flops | bytes accessed | tf_op | source)
XLA Modules:
  0.0 175.4 jit_solution(8047463743823035368)
XLA Ops:
  0.0 0.8 copy.8
  0.8 0.7 reshape.13.flat_ref
  1.5 4.8 %shard_map.56 = bf16[8,128,768]{2,1,0:T(8,128)(2,1)} custom-call(s32[1]{0:T(128)} %bitcast.4.here_ref, s32[1,1024]{1,0:T(1,128)} %reshape.13.flat_ref, bf16[1024,768]{1,0:T(8,128)(2,1)} %bitcast.9), custom_call_target="tpu_custom_call" | custom-call | flops 1610612736 | bytes 3145728 | tf_op jit(solution)/shard_map/pallas_call | solution.py:84
  6.3 4.5 %all-to-all-start = ((bf16[8,128,768]{2,1,0:T(8,128)(2,1)}), bf16[8,128,768]{2,1,0:T(8,128)(2,1)S(1)}, u32[]{:S(2)}, u32[]{:S(2)}) async-start(bf16[8,128,768]{2,1,0:T(8,128)(2,1)} %shard_map.56), calls=%async_computation | async-start | bytes 3145728 | tf_op jit(solution)/shard_map/all_to_all | solution.py:314
  10.7 1.9 %shard_map.55 = (bf16[136,1024]{1,0:T(8,128)(2,1)}, bf16[128,1024]{1,0:T(8,128)(2,1)}) custom-call(bf16[128,2048]{1,0:T(8,128)(2,1)} %tokens_ref.1, s32[8,128]{1,0:T(8,128)} %bitcast.8), custom_call_target="tpu_custom_call" | custom-call | tf_op jit(solution)/shard_map/pallas_call | solution.py:59
  12.6 5.9 %collective-permute-start.1 = (bf16[136,1024]{1,0:T(8,128)(2,1)}, bf16[136,1024]{1,0:T(8,128)(2,1)S(1)}, u32[]{:S(2)}, u32[]{:S(2)}) collective-permute-start(bf16[136,1024]{1,0:T(8,128)(2,1)} %get-tuple-element.25.refs_0_), channel_id=1, source_target_pairs={{0,56},{8,0},{16,8},{24,16},{32,24},{40,32},{48,40},{56,48},{1,57}... | collective-permute-start | bytes 835592 | tf_op jit(solution)/shard_map/ppermute | solution.py:310
  18.5 3.2 %collective-permute-start.7 = (bf16[128,1024]{1,0:T(8,128)(2,1)}, bf16[128,1024]{1,0:T(8,128)(2,1)S(1)}, u32[]{:S(2)}, u32[]{:S(2)}) collective-permute-start(bf16[128,1024]{1,0:T(8,128)(2,1)} %get-tuple-element.26.refs_7_), channel_id=1, source_target_pairs={{0,56},{8,0},{16,8},{24,16},{32,24},{40,32},{48,40},{56,48},{1,57}... | collective-permute-start | bytes 786440 | tf_op jit(solution)/shard_map/ppermute | solution.py:310
  21.7 4.0 %collective-permute-done.1.refs_2_ = bf16[136,1024]{1,0:T(8,128)(2,1)S(1)} collective-permute-done((bf16[136,1024]{1,0:T(8,128)(2,1)}, bf16[136,1024]{1,0:T(8,128)(2,1)S(1)}, u32[]{:S(2)}, u32[]{:S(2)}) %collective-permute-start.1) | collective-permute-done | bytes 278560 | tf_op jit(solution)/shard_map/ppermute | solution.py:310
  25.7 3.6 %collective-permute-start.3 = (bf16[136,1024]{1,0:T(8,128)(2,1)S(1)}, bf16[136,1024]{1,0:T(8,128)(2,1)S(1)}, u32[]{:S(2)}, u32[]{:S(2)}) collective-permute-start(bf16[136,1024]{1,0:T(8,128)(2,1)S(1)} %collective-permute-done.1.refs_2_), channel_id=1, source_target_pairs={{0,56},{8,0},{16,8},{24,16},{32,24},{40,32},{48,40},{56,48},{1,57}... | collective-permute-start | bytes 835592 | tf_op jit(solution)/shard_map/ppermute | solution.py:310
  29.4 2.0 %collective-permute-done.7.refs_9_ = bf16[128,1024]{1,0:T(8,128)(2,1)S(1)} collective-permute-done((bf16[128,1024]{1,0:T(8,128)(2,1)}, bf16[128,1024]{1,0:T(8,128)(2,1)S(1)}, u32[]{:S(2)}, u32[]{:S(2)}) %collective-permute-start.7) | collective-permute-done | bytes 262176 | tf_op jit(solution)/shard_map/ppermute | solution.py:310
  31.4 3.6 %collective-permute-start.9 = (bf16[128,1024]{1,0:T(8,128)(2,1)S(1)}, bf16[128,1024]{1,0:T(8,128)(2,1)S(1)}, u32[]{:S(2)}, u32[]{:S(2)}) collective-permute-start(bf16[128,1024]{1,0:T(8,128)(2,1)S(1)} %collective-permute-done.7.refs_9_), channel_id=1, source_target_pairs={{0,56},{8,0},{16,8},{24,16},{32,24},{40,32},{48,40},{56,48},{1,57}... | collective-permute-start | bytes 786440 | tf_op jit(solution)/shard_map/ppermute | solution.py:310
  35.0 2.2 %collective-permute-done.3.refs_4_ = bf16[136,1024]{1,0:T(8,128)(2,1)S(1)} collective-permute-done((bf16[136,1024]{1,0:T(8,128)(2,1)S(1)}, bf16[136,1024]{1,0:T(8,128)(2,1)S(1)}, u32[]{:S(2)}, u32[]{:S(2)}) %collective-permute-start.3) | collective-permute-done | bytes 278560 | tf_op jit(solution)/shard_map/ppermute | solution.py:310
  37.2 3.7 %collective-permute-start.5 = (bf16[136,1024]{1,0:T(8,128)(2,1)S(1)}, bf16[136,1024]{1,0:T(8,128)(2,1)S(1)}, u32[]{:S(2)}, u32[]{:S(2)}) collective-permute-start(bf16[136,1024]{1,0:T(8,128)(2,1)S(1)} %collective-permute-done.3.refs_4_), channel_id=1, source_target_pairs={{0,56},{8,0},{16,8},{24,16},{32,24},{40,32},{48,40},{56,48},{1,57}... | collective-permute-start | bytes 835592 | tf_op jit(solution)/shard_map/ppermute | solution.py:310
  41.0 1.9 %collective-permute-done.9.refs_11_ = bf16[128,1024]{1,0:T(8,128)(2,1)S(1)} collective-permute-done((bf16[128,1024]{1,0:T(8,128)(2,1)S(1)}, bf16[128,1024]{1,0:T(8,128)(2,1)S(1)}, u32[]{:S(2)}, u32[]{:S(2)}) %collective-permute-start.9) | collective-permute-done | bytes 262176 | tf_op jit(solution)/shard_map/ppermute | solution.py:310
  42.8 3.7 %collective-permute-start.11 = (bf16[128,1024]{1,0:T(8,128)(2,1)S(1)}, bf16[128,1024]{1,0:T(8,128)(2,1)S(1)}, u32[]{:S(2)}, u32[]{:S(2)}) collective-permute-start(bf16[128,1024]{1,0:T(8,128)(2,1)S(1)} %collective-permute-done.9.refs_11_), channel_id=1, source_target_pairs={{0,56},{8,0},{16,8},{24,16},{32,24},{40,32},{48,40},{56,48},{1,57}... | collective-permute-start | bytes 786440 | tf_op jit(solution)/shard_map/ppermute | solution.py:310
  46.8 7.2 %collective-permute-done.11.refs_13_.refs_4_ = bf16[128,1024]{1,0:T(8,128)(2,1)S(1)} collective-permute-done((bf16[128,1024]{1,0:T(8,128)(2,1)S(1)}, bf16[128,1024]{1,0:T(8,128)(2,1)S(1)}, u32[]{:S(2)}, u32[]{:S(2)}) %collective-permute-start.11) | collective-permute-done | bytes 262176 | tf_op jit(solution)/shard_map/ppermute | solution.py:310
  54.0 3.4 %collective-permute-done.10.refs_12_.refs_2_ = bf16[128,1024]{1,0:T(8,128)(2,1)S(1)} collective-permute-done((bf16[128,1024]{1,0:T(8,128)(2,1)S(1)}, bf16[128,1024]{1,0:T(8,128)(2,1)S(1)}, u32[]{:S(2)}, u32[]{:S(2)}) %collective-permute-start.10) | collective-permute-done | bytes 262176 | tf_op jit(solution)/shard_map/ppermute | solution.py:310
  57.6 0.6 copy-done.14
  58.4 1.1 copy-done.8
  59.5 5.9 %shard_map.57 = bf16[8,112,2048]{2,1,0:T(8,128)(2,1)} custom-call(s32[1]{0:T(128)} %bitcast.4.here_ref, bf16[136,1024]{1,0:T(8,128)(2,1)} %get-tuple-element.25.refs_0_, bf16[136,1024]{1,0:T(8,128)(2,1)} %copy-done.17, bf16[136,1024]{1,0:T(8,128)(2,1)} %copy-done.16, bf16[136,1024]{1,0:T(8,128)(2,1)} %copy-done.19, bf16[136,1024]{1,0:T(8,128)(2,1)} %copy-done.18, ...), custom_call_target="tpu_custom_call" | custom-call | flops 469762048 | bytes 7340032 | tf_op jit(solution)/shard_map/pallas_call | solution.py:133
  65.4 4.7 %all-to-all-start.1 = ((bf16[8,112,2048]{2,1,0:T(8,128)(2,1)}), bf16[8,112,2048]{2,1,0:T(8,128)(2,1)}, u32[]{:S(2)}, u32[]{:S(2)}) async-start(bf16[8,112,2048]{2,1,0:T(8,128)(2,1)} %shard_map.57), calls=%async_computation.1 | async-start | bytes 7340032 | tf_op jit(solution)/shard_map/all_to_all | solution.py:314
  70.2 3.2 %collective-permute-start.13 = (bf16[128,1024]{1,0:T(8,128)(2,1)S(1)}, bf16[128,1024]{1,0:T(8,128)(2,1)S(1)}, u32[]{:S(2)}, u32[]{:S(2)}) collective-permute-start(bf16[128,1024]{1,0:T(8,128)(2,1)S(1)} %copy-done.13), channel_id=1, source_target_pairs={{0,56},{8,0},{16,8},{24,16},{32,24},{40,32},{48,40},{56,48},{1,57}... | collective-permute-start | bytes 786440 | tf_op jit(solution)/shard_map/ppermute | solution.py:310
  73.4 2.6 %shard_map.59 = (bf16[128,768]{1,0:T(8,128)(2,1)}, bf16[128,768]{1,0:T(8,128)(2,1)}, bf16[128,768]{1,0:T(8,128)(2,1)}, bf16[128,768]{1,0:T(8,128)(2,1)}, bf16[12...) custom-call(bf16[8,128,768]{2,1,0:T(8,128)(2,1)} %copy-done.8, ...), custom_call_target="tpu_custom_call" | custom-call | tf_op jit(solution)/shard_map/pallas_call | solution.py:104
  76.0 5.0 %collective-permute-start.15 = (bf16[128,768]{1,0:T(8,128)(2,1)}, bf16[128,768]{1,0:T(8,128)(2,1)S(1)}, u32[]{:S(2)}, u32[]{:S(2)}) collective-permute-start(bf16[128,768]{1,0:T(8,128)(2,1)} %get-tuple-element.29), channel_id=1, source_target_pairs={{0,40},{8,48},{16,56},{24,0},{32,8},{40,16},{48,24},{56,32},{1,41}... | collective-permute-start | bytes 589832 | tf_op jit(solution)/shard_map/ppermute | solution.py:310
  81.1 3.2 %collective-permute-start.17 = (bf16[128,768]{1,0:T(8,128)(2,1)}, bf16[128,768]{1,0:T(8,128)(2,1)S(1)}, u32[]{:S(2)}, u32[]{:S(2)}) collective-permute-start(bf16[128,768]{1,0:T(8,128)(2,1)} %get-tuple-element.31), channel_id=1, source_target_pairs={{0,56},{8,0},{16,8},{24,16},{32,24},{40,32},{48,40},{56,48},{1,57}... | collective-permute-start | bytes 589832 | tf_op jit(solution)/shard_map/ppermute | solution.py:310
  84.4 10.4 %collective-permute-done.14.refs_4_.refs_5_ = bf16[128,768]{1,0:T(8,128)(2,1)S(1)} collective-permute-done((bf16[128,768]{1,0:T(8,128)(2,1)}, bf16[128,768]{1,0:T(8,128)(2,1)S(1)}, u32[]{:S(2)}, u32[]{:S(2)}) %collective-permute-start.14) | collective-permute-done | bytes 196640 | tf_op jit(solution)/shard_map/ppermute | solution.py:310
  95.1 3.6 %collective-permute-start.20 = (bf16[128,768]{1,0:T(8,128)(2,1)}, bf16[128,768]{1,0:T(8,128)(2,1)S(1)}, u32[]{:S(2)}, u32[]{:S(2)}) collective-permute-start(bf16[128,768]{1,0:T(8,128)(2,1)} %get-tuple-element.34), channel_id=1, source_target_pairs={{0,32},{8,40},{16,48},{24,56},{32,0},{40,8},{48,16},{56,24},{1,33}... | collective-permute-start | bytes 589832 | tf_op jit(solution)/shard_map/ppermute | solution.py:310
  98.7 15.4 %all-to-all-done.1.parts_ref.refs_2_ = bf16[8,112,2048]{2,1,0:T(8,128)(2,1)} async-done(((bf16[8,112,2048]{2,1,0:T(8,128)(2,1)}), bf16[8,112,2048]{2,1,0:T(8,128)(2,1)}, u32[]{:S(2)}, u32[]{:S(2)}) %all-to-all-start.1) | async-done | bytes 3670048 | tf_op jit(solution)/shard_map/all_to_all | solution.py:314
  114.2 2.2 %shard_map.60 = bf16[8,16,2048]{2,1,0:T(8,128)(2,1)} custom-call(s32[1]{0:T(128)} %bitcast.4.here_ref, bf16[136,1024]{1,0:T(8,128)(2,1)} %copy-done.15, bf16[128,1024]{1,0:T(8,128)(2,1)} %copy-done.20, bf16[8,112,2048]{2,1,0:T(8,128)(2,1)} %all-to-all-done.1.parts_ref.refs_2_, bf16[128,768]{1,0:T(8,128)(2,1)} %get-tuple-element.27.refs_3_.refs_0_, ...), custom_call_target="tpu_custom_call" | custom-call | flops 67108864 | bytes 1048576 | tf_op jit(solution)/shard_map/pallas_call | solution.py:133
  116.4 3.7 %all-to-all-start.2 = ((bf16[8,16,2048]{2,1,0:T(8,128)(2,1)}), bf16[8,16,2048]{2,1,0:T(8,128)(2,1)S(1)}, u32[]{:S(2)}, u32[]{:S(2)}) async-start(bf16[8,16,2048]{2,1,0:T(8,128)(2,1)} %shard_map.60), calls=%async_computation.2 | async-start | bytes 1048576 | tf_op jit(solution)/shard_map/all_to_all | solution.py:314
  120.1 11.5 %shard_map.58.refs_9_.first = bf16[2048,896]{1,0:T(8,128)(2,1)S(1)} custom-call(bf16[8,112,2048]{2,1,0:T(8,128)(2,1)} %all-to-all-done.1.parts_ref.refs_2_, bf16[1,2048,2048]{2,1,0:T(8,128)(2,1)} %basis_ref.3), custom_call_target="tpu_custom_call" | custom-call | flops 7516192768 | bytes 15728640 | tf_op jit(solution)/shard_map/pallas_call | solution.py:162
  131.7 1.8 %copy-done = bf16[2048,896]{1,0:T(8,128)(2,1)} copy-done((bf16[2048,896]{1,0:T(8,128)(2,1)}, bf16[2048,896]{1,0:T(8,128)(2,1)S(1)}, u32[]{:S(2)}) %copy-start) | copy-done | bytes 3670040
  133.5 5.8 %shard_map.61.refs_10_.second = bf16[2048,128]{1,0:T(8,128)(2,1)S(1)} custom-call(bf16[8,16,2048]{2,1,0:T(8,128)(2,1)S(1)} %all-to-all-done.2.parts_ref, bf16[1,2048,2048]{2,1,0:T(8,128)(2,1)} %basis_ref.3), custom_call_target="tpu_custom_call" | custom-call | flops 1073741824 | bytes 9437184 | tf_op jit(solution)/shard_map/pallas_call | solution.py:162
  139.4 3.2 %shard_map.62 = (bf16[1024,768]{1,0:T(8,128)(2,1)S(1)}, s16[272,768]{1,0:T(8,128)(2,1)S(1)}, s16[272,768]{1,0:T(8,128)(2,1)S(1)}) custom-call(s32[4]{0:T(128)S(1)} %pad_add_fusion.place_ref, bf16[128,768]{1,0:T(8,128)(2,1)S(1)} %copy-done.2, bf16[128,768]{1,0:T(8,128)(2,1)S(1)} %collective-permute-done.16.refs_1_, ...), custom_call_target="tpu_custom_call" | custom-call | flops 2013265920 | bytes 12582912 | tf_op jit(solution)/shard_map/pallas_call | solution.py:219
  142.6 0.6 collective-permute-start.21
  143.2 1.5 collective-permute-start.22
  144.7 2.2 %shard_map.65 = (s16[272,768]{1,0:T(8,128)(2,1)S(1)}, s16[272,768]{1,0:T(8,128)(2,1)S(1)}) custom-call(s32[4]{0:T(128)S(1)} %pad_add_fusion.place_ref, bf16[2048,896]{1,0:T(8,128)(2,1)S(1)} %copy-done.1, bf16[2048,128]{1,0:T(8,128)(2,1)S(1)} %shard_map.61.refs_10_.second, bf16[1024,768]{1,0:T(8,128)(2,1)S(1)} %get-tuple-element.35.g_ref), custom_call_target="tpu_custom_call" | custom-call | flops 805306368 | bytes 4194304 | tf_op jit(solution)/shard_map/pallas_call | solution.py:237
  146.9 0.9 collective-permute-start.24
  147.8 2.4 %collective-permute-start.25 = (s16[272,768]{1,0:T(8,128)(2,1)S(1)}, s16[272,768]{1,0:T(8,128)(2,1)S(1)}, u32[]{:S(2)}, u32[]{:S(2)}) collective-permute-start(s16[272,768]{1,0:T(8,128)(2,1)S(1)} %get-tuple-element.43), channel_id=1, source_target_pairs={{0,64},{64,128},{128,192},{192,0},{1,65},{65,129},{129,193},{193,1... | collective-permute-start | bytes 1253384 | tf_op jit(solution)/shard_map/ppermute | solution.py:310
  150.2 2.7 %shard_map.63 = (f32[256,768]{1,0:T(8,128)S(1)}, f32[256,768]{1,0:T(8,128)S(1)}, f32[512,768]{1,0:T(8,128)S(1)}) custom-call(s32[4]{0:T(128)S(1)} %pad_add_fusion.place_ref, bf16[2048,896]{1,0:T(8,128)(2,1)S(1)} %copy-done.1, bf16[2048,128]{1,0:T(8,128)(2,1)S(1)} %shard_map.61.refs_10_.second, bf16[1024,768]{1,0:T(8,128)(2,1)S(1)} %get-tuple-element.35.g_ref), custom_call_target="tpu_custom_call" | custom-call | flops 1610612736 | bytes 8388608 | tf_op jit(solution)/shard_map/pallas_call | solution.py:258
  153.0 2.2 %collective-permute-done.21.got_up_ref = s16[272,768]{1,0:T(8,128)(2,1)S(1)} collective-permute-done((s16[272,768]{1,0:T(8,128)(2,1)S(1)}, s16[272,768]{1,0:T(8,128)(2,1)S(1)}, u32[]{:S(2)}, u32[]{:S(2)}) %collective-permute-start.21) | collective-permute-done | bytes 417824 | tf_op jit(solution)/shard_map/ppermute | solution.py:310
  155.2 1.7 collective-permute-done.22.got_down_ref
  156.9 0.9 shard_map.64
  158.2 1.7 collective-permute-start.26
  159.9 5.9 %collective-permute-done.24.top_b_ref = s16[272,768]{1,0:T(8,128)(2,1)S(1)} collective-permute-done((s16[272,768]{1,0:T(8,128)(2,1)S(1)}, s16[272,768]{1,0:T(8,128)(2,1)S(1)}, u32[]{:S(2)}, u32[]{:S(2)}) %collective-permute-start.24) | collective-permute-done | bytes 417824 | tf_op jit(solution)/shard_map/ppermute | solution.py:310
  165.9 6.5 %collective-permute-done.23.top_a_ref = s16[272,768]{1,0:T(8,128)(2,1)S(1)} collective-permute-done((s16[272,768]{1,0:T(8,128)(2,1)S(1)}, s16[272,768]{1,0:T(8,128)(2,1)S(1)}, u32[]{:S(2)}, u32[]{:S(2)}) %collective-permute-start.23) | collective-permute-done | bytes 417824 | tf_op jit(solution)/shard_map/ppermute | solution.py:310
  172.3 1.4 collective-permute-done.26.bottom_b_ref
  173.7 1.7 shard_map.66
  (77 shorter events, 1.6 us)
Async XLA Ops:
  6.3 51.3 %all-to-all-start = ((bf16[8,128,768]{2,1,0:T(8,128)(2,1)}), bf16[8,128,768]{2,1,0:T(8,128)(2,1)S(1)}, u32[]{:S(2)}, u32[]{:S(2)}) async-start(bf16[8,128,768]{2,1,0:T(8,128)(2,1)} %shard_map.56), calls=%async_computation | async-start | bytes 3145728 | tf_op jit(solution)/shard_map/all_to_all | solution.py:314
  12.6 13.1 %collective-permute-start.1 = (bf16[136,1024]{1,0:T(8,128)(2,1)}, bf16[136,1024]{1,0:T(8,128)(2,1)S(1)}, u32[]{:S(2)}, u32[]{:S(2)}) collective-permute-start(bf16[136,1024]{1,0:T(8,128)(2,1)} %get-tuple-element.25.refs_0_), channel_id=1, source_target_pairs={{0,56},{8,0},{16,8},{24,16},{32,24},{40,32},{48,40},{56,48},{1,57}... | collective-permute-start | bytes 835592 | tf_op jit(solution)/shard_map/ppermute | solution.py:310
  18.5 10.9 %collective-permute-start = (bf16[136,1024]{1,0:T(8,128)(2,1)}, bf16[136,1024]{1,0:T(8,128)(2,1)S(1)}, u32[]{:S(2)}, u32[]{:S(2)}) collective-permute-start(bf16[136,1024]{1,0:T(8,128)(2,1)} %get-tuple-element.25.refs_0_), channel_id=1, source_target_pairs={{0,8},{8,16},{16,24},{24,32},{32,40},{40,48},{48,56},{56,0},{1,9},... | collective-permute-start | bytes 835592 | tf_op jit(solution)/shard_map/ppermute | solution.py:310
  18.5 12.9 %collective-permute-start.7 = (bf16[128,1024]{1,0:T(8,128)(2,1)}, bf16[128,1024]{1,0:T(8,128)(2,1)S(1)}, u32[]{:S(2)}, u32[]{:S(2)}) collective-permute-start(bf16[128,1024]{1,0:T(8,128)(2,1)} %get-tuple-element.26.refs_7_), channel_id=1, source_target_pairs={{0,56},{8,0},{16,8},{24,16},{32,24},{40,32},{48,40},{56,48},{1,57}... | collective-permute-start | bytes 786440 | tf_op jit(solution)/shard_map/ppermute | solution.py:310
  21.7 13.3 %collective-permute-start.6 = (bf16[128,1024]{1,0:T(8,128)(2,1)}, bf16[128,1024]{1,0:T(8,128)(2,1)S(1)}, u32[]{:S(2)}, u32[]{:S(2)}) collective-permute-start(bf16[128,1024]{1,0:T(8,128)(2,1)} %get-tuple-element.26.refs_7_), channel_id=1, source_target_pairs={{0,8},{8,16},{16,24},{24,32},{32,40},{40,48},{48,56},{56,0},{1,9},... | collective-permute-start | bytes 786440 | tf_op jit(solution)/shard_map/ppermute | solution.py:310
  25.7 31.8 %copy-start.16 = (bf16[136,1024]{1,0:T(8,128)(2,1)}, bf16[136,1024]{1,0:T(8,128)(2,1)S(1)}, u32[]{:S(2)}) copy-start(bf16[136,1024]{1,0:T(8,128)(2,1)S(1)} %collective-permute-done.1.refs_2_) | copy-start | bytes 835588
  25.7 11.5 %collective-permute-start.3 = (bf16[136,1024]{1,0:T(8,128)(2,1)S(1)}, bf16[136,1024]{1,0:T(8,128)(2,1)S(1)}, u32[]{:S(2)}, u32[]{:S(2)}) collective-permute-start(bf16[136,1024]{1,0:T(8,128)(2,1)S(1)} %collective-permute-done.1.refs_2_), channel_id=1, source_target_pairs={{0,56},{8,0},{16,8},{24,16},{32,24},{40,32},{48,40},{56,48},{1,57}... | collective-permute-start | bytes 835592 | tf_op jit(solution)/shard_map/ppermute | solution.py:310
  29.4 28.2 %copy-start.17 = (bf16[136,1024]{1,0:T(8,128)(2,1)}, bf16[136,1024]{1,0:T(8,128)(2,1)S(1)}, u32[]{:S(2)}) copy-start(bf16[136,1024]{1,0:T(8,128)(2,1)S(1)} %collective-permute-done.refs_1_) | copy-start | bytes 835588
  29.4 11.6 %collective-permute-start.2 = (bf16[136,1024]{1,0:T(8,128)(2,1)S(1)}, bf16[136,1024]{1,0:T(8,128)(2,1)S(1)}, u32[]{:S(2)}, u32[]{:S(2)}) collective-permute-start(bf16[136,1024]{1,0:T(8,128)(2,1)S(1)} %collective-permute-done.refs_1_), channel_id=1, source_target_pairs={{0,8},{8,16},{16,24},{24,32},{32,40},{40,48},{48,56},{56,0},{1,9},... | collective-permute-start | bytes 835592 | tf_op jit(solution)/shard_map/ppermute | solution.py:310
  31.4 9.6 %copy-start.21 = (bf16[128,1024]{1,0:T(8,128)(2,1)}, bf16[128,1024]{1,0:T(8,128)(2,1)S(1)}, u32[]{:S(2)}) copy-start(bf16[128,1024]{1,0:T(8,128)(2,1)S(1)} %collective-permute-done.7.refs_9_) | copy-start | bytes 786436
  31.4 11.5 %collective-permute-start.9 = (bf16[128,1024]{1,0:T(8,128)(2,1)S(1)}, bf16[128,1024]{1,0:T(8,128)(2,1)S(1)}, u32[]{:S(2)}, u32[]{:S(2)}) collective-permute-start(bf16[128,1024]{1,0:T(8,128)(2,1)S(1)} %collective-permute-done.7.refs_9_), channel_id=1, source_target_pairs={{0,56},{8,0},{16,8},{24,16},{32,24},{40,32},{48,40},{56,48},{1,57}... | collective-permute-start | bytes 786440 | tf_op jit(solution)/shard_map/ppermute | solution.py:310
  35.0 11.6 %copy-start.22 = (bf16[128,1024]{1,0:T(8,128)(2,1)}, bf16[128,1024]{1,0:T(8,128)(2,1)S(1)}, u32[]{:S(2)}) copy-start(bf16[128,1024]{1,0:T(8,128)(2,1)S(1)} %collective-permute-done.6.refs_8_) | copy-start | bytes 786436
  35.0 11.6 %collective-permute-start.8 = (bf16[128,1024]{1,0:T(8,128)(2,1)S(1)}, bf16[128,1024]{1,0:T(8,128)(2,1)S(1)}, u32[]{:S(2)}, u32[]{:S(2)}) collective-permute-start(bf16[128,1024]{1,0:T(8,128)(2,1)S(1)} %collective-permute-done.6.refs_8_), channel_id=1, source_target_pairs={{0,8},{8,16},{16,24},{24,32},{32,40},{40,48},{48,56},{56,0},{1,9},... | collective-permute-start | bytes 786440 | tf_op jit(solution)/shard_map/ppermute | solution.py:310
  37.2 20.3 %copy-start.18 = (bf16[136,1024]{1,0:T(8,128)(2,1)}, bf16[136,1024]{1,0:T(8,128)(2,1)S(1)}, u32[]{:S(2)}) copy-start(bf16[136,1024]{1,0:T(8,128)(2,1)S(1)} %collective-permute-done.3.refs_4_) | copy-start | bytes 835588
  37.2 20.2 %collective-permute-start.5 = (bf16[136,1024]{1,0:T(8,128)(2,1)S(1)}, bf16[136,1024]{1,0:T(8,128)(2,1)S(1)}, u32[]{:S(2)}, u32[]{:S(2)}) collective-permute-start(bf16[136,1024]{1,0:T(8,128)(2,1)S(1)} %collective-permute-done.3.refs_4_), channel_id=1, source_target_pairs={{0,56},{8,0},{16,8},{24,16},{32,24},{40,32},{48,40},{56,48},{1,57}... | collective-permute-start | bytes 835592 | tf_op jit(solution)/shard_map/ppermute | solution.py:310
  41.0 16.5 %copy-start.19 = (bf16[136,1024]{1,0:T(8,128)(2,1)}, bf16[136,1024]{1,0:T(8,128)(2,1)S(1)}, u32[]{:S(2)}) copy-start(bf16[136,1024]{1,0:T(8,128)(2,1)S(1)} %collective-permute-done.2.refs_3_) | copy-start | bytes 835588
  41.0 16.5 %collective-permute-start.4 = (bf16[136,1024]{1,0:T(8,128)(2,1)S(1)}, bf16[136,1024]{1,0:T(8,128)(2,1)S(1)}, u32[]{:S(2)}, u32[]{:S(2)}) collective-permute-start(bf16[136,1024]{1,0:T(8,128)(2,1)S(1)} %collective-permute-done.2.refs_3_), channel_id=1, source_target_pairs={{0,8},{8,16},{16,24},{24,32},{32,40},{40,48},{48,56},{56,0},{1,9},... | collective-permute-start | bytes 835592 | tf_op jit(solution)/shard_map/ppermute | solution.py:310
  42.8 14.6 %copy-start.23 = (bf16[128,1024]{1,0:T(8,128)(2,1)}, bf16[128,1024]{1,0:T(8,128)(2,1)S(1)}, u32[]{:S(2)}) copy-start(bf16[128,1024]{1,0:T(8,128)(2,1)S(1)} %collective-permute-done.9.refs_11_) | copy-start | bytes 786436
  42.8 11.2 %collective-permute-start.11 = (bf16[128,1024]{1,0:T(8,128)(2,1)S(1)}, bf16[128,1024]{1,0:T(8,128)(2,1)S(1)}, u32[]{:S(2)}, u32[]{:S(2)}) collective-permute-start(bf16[128,1024]{1,0:T(8,128)(2,1)S(1)} %collective-permute-done.9.refs_11_), channel_id=1, source_target_pairs={{0,56},{8,0},{16,8},{24,16},{32,24},{40,32},{48,40},{56,48},{1,57}... | collective-permute-start | bytes 786440 | tf_op jit(solution)/shard_map/ppermute | solution.py:310
  46.6 10.9 %copy-start.24 = (bf16[128,1024]{1,0:T(8,128)(2,1)}, bf16[128,1024]{1,0:T(8,128)(2,1)S(1)}, u32[]{:S(2)}) copy-start(bf16[128,1024]{1,0:T(8,128)(2,1)S(1)} %collective-permute-done.8.refs_10_) | copy-start | bytes 786436
  46.6 10.9 %collective-permute-start.10 = (bf16[128,1024]{1,0:T(8,128)(2,1)S(1)}, bf16[128,1024]{1,0:T(8,128)(2,1)S(1)}, u32[]{:S(2)}, u32[]{:S(2)}) collective-permute-start(bf16[128,1024]{1,0:T(8,128)(2,1)S(1)} %collective-permute-done.8.refs_10_), channel_id=1, source_target_pairs={{0,8},{8,16},{16,24},{24,32},{32,40},{40,48},{48,56},{56,0},{1,9},... | collective-permute-start | bytes 786440 | tf_op jit(solution)/shard_map/ppermute | solution.py:310
  65.4 4.8 %copy-start.13 = (bf16[128,1024]{1,0:T(8,128)(2,1)S(1)}, bf16[128,1024]{1,0:T(8,128)(2,1)}, u32[]{:S(2)}) copy-start(bf16[128,1024]{1,0:T(8,128)(2,1)} %copy-done.12) | copy-start | bytes 786436
  65.4 48.7 %all-to-all-start.1 = ((bf16[8,112,2048]{2,1,0:T(8,128)(2,1)}), bf16[8,112,2048]{2,1,0:T(8,128)(2,1)}, u32[]{:S(2)}, u32[]{:S(2)}) async-start(bf16[8,112,2048]{2,1,0:T(8,128)(2,1)} %shard_map.57), calls=%async_computation.1 | async-start | bytes 7340032 | tf_op jit(solution)/shard_map/all_to_all | solution.py:314
  70.1 14.3 %collective-permute-start.12 = (bf16[136,1024]{1,0:T(8,128)(2,1)S(1)}, bf16[136,1024]{1,0:T(8,128)(2,1)S(1)}, u32[]{:S(2)}, u32[]{:S(2)}) collective-permute-start(bf16[136,1024]{1,0:T(8,128)(2,1)S(1)} %copy-done.10), channel_id=1, source_target_pairs={{0,8},{8,16},{16,24},{24,32},{32,40},{40,48},{48,56},{56,0},{1,9},... | collective-permute-start | bytes 835592 | tf_op jit(solution)/shard_map/ppermute | solution.py:310
  70.2 10.9 %collective-permute-start.13 = (bf16[128,1024]{1,0:T(8,128)(2,1)S(1)}, bf16[128,1024]{1,0:T(8,128)(2,1)S(1)}, u32[]{:S(2)}, u32[]{:S(2)}) collective-permute-start(bf16[128,1024]{1,0:T(8,128)(2,1)S(1)} %copy-done.13), channel_id=1, source_target_pairs={{0,56},{8,0},{16,8},{24,16},{32,24},{40,32},{48,40},{56,48},{1,57}... | collective-permute-start | bytes 786440 | tf_op jit(solution)/shard_map/ppermute | solution.py:310
  76.0 18.8 %collective-permute-start.14 = (bf16[128,768]{1,0:T(8,128)(2,1)}, bf16[128,768]{1,0:T(8,128)(2,1)S(1)}, u32[]{:S(2)}, u32[]{:S(2)}) collective-permute-start(bf16[128,768]{1,0:T(8,128)(2,1)} %get-tuple-element.28), channel_id=1, source_target_pairs={{0,24},{8,32},{16,40},{24,48},{32,56},{40,0},{48,8},{56,16},{1,25}... | collective-permute-start | bytes 589832 | tf_op jit(solution)/shard_map/ppermute | solution.py:310
  76.0 19.1 %collective-permute-start.15 = (bf16[128,768]{1,0:T(8,128)(2,1)}, bf16[128,768]{1,0:T(8,128)(2,1)S(1)}, u32[]{:S(2)}, u32[]{:S(2)}) collective-permute-start(bf16[128,768]{1,0:T(8,128)(2,1)} %get-tuple-element.29), channel_id=1, source_target_pairs={{0,40},{8,48},{16,56},{24,0},{32,8},{40,16},{48,24},{56,32},{1,41}... | collective-permute-start | bytes 589832 | tf_op jit(solution)/shard_map/ppermute | solution.py:310
  81.1 58.2 %collective-permute-start.16 = (bf16[128,768]{1,0:T(8,128)(2,1)}, bf16[128,768]{1,0:T(8,128)(2,1)S(1)}, u32[]{:S(2)}, u32[]{:S(2)}) collective-permute-start(bf16[128,768]{1,0:T(8,128)(2,1)} %get-tuple-element.30), channel_id=1, source_target_pairs={{0,8},{8,16},{16,24},{24,32},{32,40},{40,48},{48,56},{56,0},{1,9},... | collective-permute-start | bytes 589832 | tf_op jit(solution)/shard_map/ppermute | solution.py:310
  81.1 33.0 %copy-start.20 = (bf16[128,1024]{1,0:T(8,128)(2,1)}, bf16[128,1024]{1,0:T(8,128)(2,1)S(1)}, u32[]{:S(2)}) copy-start(bf16[128,1024]{1,0:T(8,128)(2,1)S(1)} %collective-permute-done.13.refs_1_) | copy-start | bytes 786436
  81.1 58.2 %collective-permute-start.17 = (bf16[128,768]{1,0:T(8,128)(2,1)}, bf16[128,768]{1,0:T(8,128)(2,1)S(1)}, u32[]{:S(2)}, u32[]{:S(2)}) collective-permute-start(bf16[128,768]{1,0:T(8,128)(2,1)} %get-tuple-element.31), channel_id=1, source_target_pairs={{0,56},{8,0},{16,8},{24,16},{32,24},{40,32},{48,40},{56,48},{1,57}... | collective-permute-start | bytes 589832 | tf_op jit(solution)/shard_map/ppermute | solution.py:310
  84.4 29.8 %copy-start.15 = (bf16[136,1024]{1,0:T(8,128)(2,1)}, bf16[136,1024]{1,0:T(8,128)(2,1)S(1)}, u32[]{:S(2)}) copy-start(bf16[136,1024]{1,0:T(8,128)(2,1)S(1)} %collective-permute-done.12.refs_0_) | copy-start | bytes 835588
  84.4 54.9 %collective-permute-start.18 = (bf16[128,768]{1,0:T(8,128)(2,1)}, bf16[128,768]{1,0:T(8,128)(2,1)S(1)}, u32[]{:S(2)}, u32[]{:S(2)}) collective-permute-start(bf16[128,768]{1,0:T(8,128)(2,1)} %get-tuple-element.32), channel_id=1, source_target_pairs={{0,16},{8,24},{16,32},{24,40},{32,48},{40,56},{48,0},{56,8},{1,17}... | collective-permute-start | bytes 589832 | tf_op jit(solution)/shard_map/ppermute | solution.py:310
  94.8 19.4 %copy-start.3 = (bf16[128,768]{1,0:T(8,128)(2,1)}, bf16[128,768]{1,0:T(8,128)(2,1)S(1)}, u32[]{:S(2)}) copy-start(bf16[128,768]{1,0:T(8,128)(2,1)S(1)} %collective-permute-done.14.refs_4_.refs_5_) | copy-start | bytes 589828
  94.8 44.5 %collective-permute-start.19 = (bf16[128,768]{1,0:T(8,128)(2,1)}, bf16[128,768]{1,0:T(8,128)(2,1)S(1)}, u32[]{:S(2)}, u32[]{:S(2)}) collective-permute-start(bf16[128,768]{1,0:T(8,128)(2,1)} %get-tuple-element.33), channel_id=1, source_target_pairs={{0,48},{8,56},{16,0},{24,8},{32,16},{40,24},{48,32},{56,40},{1,49}... | collective-permute-start | bytes 589832 | tf_op jit(solution)/shard_map/ppermute | solution.py:310
  95.1 19.1 %copy-start.5 = (bf16[128,768]{1,0:T(8,128)(2,1)}, bf16[128,768]{1,0:T(8,128)(2,1)S(1)}, u32[]{:S(2)}) copy-start(bf16[128,768]{1,0:T(8,128)(2,1)S(1)} %collective-permute-done.15.refs_5_.refs_6_) | copy-start | bytes 589828
  95.1 44.2 %collective-permute-start.20 = (bf16[128,768]{1,0:T(8,128)(2,1)}, bf16[128,768]{1,0:T(8,128)(2,1)S(1)}, u32[]{:S(2)}, u32[]{:S(2)}) collective-permute-start(bf16[128,768]{1,0:T(8,128)(2,1)} %get-tuple-element.34), channel_id=1, source_target_pairs={{0,32},{8,40},{16,48},{24,56},{32,0},{40,8},{48,16},{56,24},{1,33}... | collective-permute-start | bytes 589832 | tf_op jit(solution)/shard_map/ppermute | solution.py:310
  116.4 17.1 %all-to-all-start.2 = ((bf16[8,16,2048]{2,1,0:T(8,128)(2,1)}), bf16[8,16,2048]{2,1,0:T(8,128)(2,1)S(1)}, u32[]{:S(2)}, u32[]{:S(2)}) async-start(bf16[8,16,2048]{2,1,0:T(8,128)(2,1)} %shard_map.60), calls=%async_computation.2 | async-start | bytes 1048576 | tf_op jit(solution)/shard_map/all_to_all | solution.py:314
  133.5 5.8 %copy-start.2 = (bf16[128,768]{1,0:T(8,128)(2,1)S(1)}, bf16[128,768]{1,0:T(8,128)(2,1)}, u32[]{:S(2)}) copy-start(bf16[128,768]{1,0:T(8,128)(2,1)} %get-tuple-element.27.refs_3_.refs_0_) | copy-start | bytes 589828
  133.5 5.9 %copy-start.4 = (bf16[128,768]{1,0:T(8,128)(2,1)S(1)}, bf16[128,768]{1,0:T(8,128)(2,1)}, u32[]{:S(2)}) copy-start(bf16[128,768]{1,0:T(8,128)(2,1)} %copy-done.3) | copy-start | bytes 589828
  133.5 5.9 %copy-start.6 = (bf16[128,768]{1,0:T(8,128)(2,1)S(1)}, bf16[128,768]{1,0:T(8,128)(2,1)}, u32[]{:S(2)}) copy-start(bf16[128,768]{1,0:T(8,128)(2,1)} %copy-done.5) | copy-start | bytes 589828
  133.5 5.9 %copy-start.7 = (bf16[1,768,768]{2,1,0:T(8,128)(2,1)S(1)}, bf16[1,768,768]{2,1,0:T(8,128)(2,1)}, u32[]{:S(2)}) copy-start(bf16[1,768,768]{2,1,0:T(8,128)(2,1)} %refs_8_.1) | copy-start | bytes 3538948
  133.5 5.9 %copy-start.1 = (bf16[2048,896]{1,0:T(8,128)(2,1)S(1)}, bf16[2048,896]{1,0:T(8,128)(2,1)}, u32[]{:S(2)}) copy-start(bf16[2048,896]{1,0:T(8,128)(2,1)} %copy-done) | copy-start | bytes 11010052
  142.6 12.6 %collective-permute-start.21 = (s16[272,768]{1,0:T(8,128)(2,1)S(1)}, s16[272,768]{1,0:T(8,128)(2,1)S(1)}, u32[]{:S(2)}, u32[]{:S(2)}) collective-permute-start(s16[272,768]{1,0:T(8,128)(2,1)S(1)} %get-tuple-element.39), channel_id=1, source_target_pairs={{0,64},{64,128},{128,192},{192,0},{1,65},{65,129},{129,193},{193,1... | collective-permute-start | bytes 1253384 | tf_op jit(solution)/shard_map/ppermute | solution.py:310
  143.2 13.7 %collective-permute-start.22 = (s16[272,768]{1,0:T(8,128)(2,1)S(1)}, s16[272,768]{1,0:T(8,128)(2,1)S(1)}, u32[]{:S(2)}, u32[]{:S(2)}) collective-permute-start(s16[272,768]{1,0:T(8,128)(2,1)S(1)} %get-tuple-element.40), channel_id=1, source_target_pairs={{0,192},{64,0},{128,64},{192,128},{1,193},{65,1},{129,65},{193,129... | collective-permute-start | bytes 1253384 | tf_op jit(solution)/shard_map/ppermute | solution.py:310
  146.9 19.0 %collective-permute-start.24 = (s16[272,768]{1,0:T(8,128)(2,1)S(1)}, s16[272,768]{1,0:T(8,128)(2,1)S(1)}, u32[]{:S(2)}, u32[]{:S(2)}) collective-permute-start(s16[272,768]{1,0:T(8,128)(2,1)S(1)} %get-tuple-element.42), channel_id=1, source_target_pairs={{0,192},{64,0},{128,64},{192,128},{1,193},{65,1},{129,65},{193,129... | collective-permute-start | bytes 1253384 | tf_op jit(solution)/shard_map/ppermute | solution.py:310
  147.8 18.1 %collective-permute-start.25 = (s16[272,768]{1,0:T(8,128)(2,1)S(1)}, s16[272,768]{1,0:T(8,128)(2,1)S(1)}, u32[]{:S(2)}, u32[]{:S(2)}) collective-permute-start(s16[272,768]{1,0:T(8,128)(2,1)S(1)} %get-tuple-element.43), channel_id=1, source_target_pairs={{0,64},{64,128},{128,192},{192,0},{1,65},{65,129},{129,193},{193,1... | collective-permute-start | bytes 1253384 | tf_op jit(solution)/shard_map/ppermute | solution.py:310
  157.8 14.5 %collective-permute-start.23 = (s16[272,768]{1,0:T(8,128)(2,1)S(1)}, s16[272,768]{1,0:T(8,128)(2,1)S(1)}, u32[]{:S(2)}, u32[]{:S(2)}) collective-permute-start(s16[272,768]{1,0:T(8,128)(2,1)S(1)} %get-tuple-element.41), channel_id=1, source_target_pairs={{0,64},{64,128},{128,192},{192,0},{1,65},{65,129},{129,193},{193,1... | collective-permute-start | bytes 1253384 | tf_op jit(solution)/shard_map/ppermute | solution.py:310
  158.2 15.6 %collective-permute-start.26 = (s16[272,768]{1,0:T(8,128)(2,1)S(1)}, s16[272,768]{1,0:T(8,128)(2,1)S(1)}, u32[]{:S(2)}, u32[]{:S(2)}) collective-permute-start(s16[272,768]{1,0:T(8,128)(2,1)S(1)} %get-tuple-element.44), channel_id=1, source_target_pairs={{0,192},{64,0},{128,64},{192,128},{1,193},{65,1},{129,65},{193,129... | collective-permute-start | bytes 1253384 | tf_op jit(solution)/shard_map/ppermute | solution.py:310
  (7 other events, 13.5 us)
where the time goes:
time: 176 us; the launch traced here: 175 us
  waiting for transfers between devices  64.6 us (37%)
  starting transfers between devices  59.7 us (34%)
  Pallas kernels  45.4 us (26%)
  local copies, waits for them, and re-layouts  5.31 us (3%)
    ppermute x27, waiting for transfers between devices, shift(): return lax.ppermute(value, axis, [(i, (i + by) % n) for i in range(n)])  49.2 us
    ppermute x27, starting transfers between devices, shift(): return lax.ppermute(value, axis, [(i, (i + by) % n) for i in range(n)])  46.9 us
    pallas_call x2, Pallas kernels, rotate_inputs(): pl.pallas_call(rotate_kernel, out_shape=jax.ShapeDtypeStruct((D, rows), B...  17.3 us
    all_to_all x3, waiting for transfers between devices, to_owners(): lax.all_to_all(value, ('y', 'c'), split_axis=0, concat_axis=0, tiled=True)  15.4 us
    all_to_all x3, starting transfers between devices, to_owners(): lax.all_to_all(value, ('y', 'c'), split_axis=0, concat_axis=0, tiled=True)  12.8 us
    pallas_call x2, Pallas kernels, pack_tokens(): pl.pallas_call(functools.partial(pack_tokens_kernel, n), out_shape=jax.Sh...  8.11 us
    pallas_call x1, Pallas kernels, pack_grads(): pl.pallas_call(pack_grads_kernel, out_shape=jax.ShapeDtypeStruct((N_YC, N...  4.78 us
    unnamed x51, local copies, waits for them, and re-layouts  4.62 us
  transfers between devices with their start and end apart: 30, of which 13 were waited for; matrix products, arithmetic and copies ran while one was open for 0% of the time, Pallas kernels for 17%

commit v1 on v0

--- a/solution.py
+++ b/solution.py
@@ -11,8 +11,8 @@
 CAP = 16
 N_X, N_Z, N_Y, N_C = 4, 8, 4, 2
 N_YC = N_Y * N_C
-FIRST = (0, 1, 7, 2, 6, 3, 5)
-SECOND = (4,)
+FIRST = (0, 1, 7, 2, 6)
+SECOND = (3, 5, 4)
 ORDER = FIRST + SECOND
 TOK = 128
 TOP = 8
@@ -66,9 +66,13 @@
     )(tokens, routing)
 
 
-def pack_grads_kernel(here_ref, flat_ref, grads_ref, out_ref):
+def pack_grads_kernel(here_ref, routing_ref, grads_ref, *refs):
+    out_ref = refs[-1]
     pairs = TOK * TOP
-    flat = flat_ref[...]
+    token = ones_where(iota((TOK, pairs), 1) // TOP == iota((TOK, pairs), 0))
+    spread = jnp.dot(routing_ref[...].astype(F32).astype(BF), token, preferred_element_type=F32)
+    choice = iota((TOP, pairs), 1) % TOP == iota((TOP, pairs), 0)
+    flat = jnp.sum(jnp.where(choice, spread, 0.0), axis=0, keepdims=True).astype(I32)
     hit = iota((EXPERTS, pairs), 0) == flat
     before = jnp.dot(ones_where(hit), earlier(pairs), preferred_element_type=F32)
     rank = jnp.sum(jnp.where(hit, before, 0.0), axis=0, keepdims=True).astype(I32)
@@ -80,17 +84,17 @@
         out_ref[k] = jnp.dot(pick, grads, preferred_element_type=F32).astype(BF)
 
 
-def pack_grads(here, flat, grads):
+def pack_grads(here, routing, grads, gates):
     return pl.pallas_call(
         pack_grads_kernel,
         out_shape=jax.ShapeDtypeStruct((N_YC, N_Z * CAP, FF), BF),
-        in_specs=[IN_SMEM] + [IN_VMEM] * 2,
+        in_specs=[IN_SMEM] + [IN_VMEM] * 2 + [pl.BlockSpec(memory_space=pl.ANY)] * len(gates),
         out_specs=IN_VMEM,
         compiler_params=params(60),
         cost_estimate=pl.CostEstimate(
             flops=2 * ROWS * ROWS * FF, bytes_accessed=4 * ROWS * FF, transcendentals=0
         ),
-    )(here, flat, grads)
+    )(here, routing, grads, *gates)
 
 
 def regroup_kernel(*refs):
@@ -145,7 +149,9 @@
 STRIP = 512
 
 
-def rotate_kernel(parts_ref, basis_ref, out_ref, rows_ref):
+def rotate_kernel(parts_ref, basis_ref, *refs):
+    out_ref, rows_ref = refs[-2:]
+
     @pl.when(pl.program_id(0) == 0)
     def _():
         for k in range(N_YC):
@@ -154,10 +160,10 @@
                 rows_ref[start : start + CAP, :] = parts_ref[k, b * CAP : (b + 1) * CAP, :]
 
     rotated = jnp.dot(rows_ref[...], basis_ref[0], preferred_element_type=F32)
-    out_ref[...] = jnp.transpose(rotated * rotated).astype(BF)
-
-
-def rotate_inputs(parts, basis_in):
+    out_ref[...] = jnp.transpose((rotated * rotated).astype(BF))
+
+
+def rotate_inputs(parts, basis_in, gates):
     rows = parts.shape[1] * N_YC
     return pl.pallas_call(
         rotate_kernel,
@@ -166,14 +172,15 @@
         in_specs=[
             pl.BlockSpec(parts.shape, lambda i: (0, 0, 0)),
             pl.BlockSpec((1, D, STRIP), lambda i: (0, 0, i)),
-        ],
+        ]
+        + [pl.BlockSpec(memory_space=pl.ANY)] * len(gates),
         out_specs=pl.BlockSpec((STRIP, rows), lambda i: (i, 0)),
         scratch_shapes=[pltpu.VMEM((rows, D), BF)],
         compiler_params=params(50),
         cost_estimate=pl.CostEstimate(
             flops=2 * rows * D * D, bytes_accessed=2 * D * D + 4 * rows * D, transcendentals=0
         ),
-    )(parts, basis_in)
+    )(parts, basis_in, *gates)
 
 
 def encode(values, out_ref):
@@ -330,19 +337,18 @@
     here = z.astype(I32).reshape(1)
 
     ring = z_ring(*stage(tokens, routing.T))
-    packed = pack_grads(here, routing.reshape(1, TOK * TOP), grads.reshape(TOK * TOP, FF))
+    packed = pack_grads(here, routing.T, grads.reshape(TOK * TOP, FF), [])
     grads_in = to_owners(packed)
     by_z = regroup(grads_in, [*ring[3], *ring[5]])
     rows_out = [by_z[k] if k == 0 else shift(by_z[k], "z", k) for k in ORDER]
 
-    a_sq, gates = [], [grads_in]
+    a_sq, gates = [], [grads_in, *ring[3], *ring[5]]
     for senders in (FIRST, SECOND):
-        rows_in = pack_tokens(
+        packed = pack_tokens(
             here, [ring[k][0] for k in senders], [ring[k][1] for k in senders], gates
         )
-        rows_in = to_owners(rows_in)
-        gates = [rows_in, by_z[0], rows_out[ORDER.index(3)], rows_out[ORDER.index(5)]]
-        a_sq.append(rotate_inputs(rows_in, basis_in))
+        gates = [packed] + [rows_out[ORDER.index(k)] for k in (3, 5, 2, 6)]
+        a_sq.append(rotate_inputs(to_owners(packed), basis_in, a_sq))
 
     g_sq, far_up, far_down = far_blocks(place, rows_out, basis_out, a_sq)
     got_far_up, got_far_down = shift(far_up, "x", 1), shift(far_down, "x", -1)

time: 176 us -> 175 us (level)
  waiting for transfers between devices: 64.6 us -> 62.5 us
    all_to_all x3, waiting for transfers between devices: 15.4 us -> 5.29 us  [to_owners(): lax.all_to_all(value, ('y', 'c'), split_axis=0, concat_axis=0, tiled=True)]
    ppermute x27, waiting for transfers between devices: 49.2 us -> 57.2 us  [shift(): return lax.ppermute(value, axis, [(i, (i + by) % n) for i in range(n)])]
    unnamed x51 -> x56, local copies, waits for them, and re-layouts: 4.62 us -> 5.69 us
  transfers between devices with their start and end apart: 30 -> 30, of which waited for: 13 -> 16; matrix products, arithmetic and copies ran while one was open for 0% -> 0% of each run, Pallas kernels for 17% -> 17%
where the time goes in v1:
time: 175 us; the launch traced here: 174 us
  waiting for transfers between devices  62.5 us (36%)
  starting transfers between devices  61.1 us (35%)
  Pallas kernels  44.4 us (25%)
  local copies, waits for them, and re-layouts  5.69 us (3%)
    ppermute x27, waiting for transfers between devices, shift(): return lax.ppermute(value, axis, [(i, (i + by) % n) for i in range(n)])  57.2 us
    ppermute x27, starting transfers between devices, shift(): return lax.ppermute(value, axis, [(i, (i + by) % n) for i in range(n)])  47.6 us
    pallas_call x2, Pallas kernels, rotate_inputs(): pl.pallas_call(rotate_kernel, out_shape=jax.ShapeDtypeStruct((D, rows), B...  15.7 us
    all_to_all x3, starting transfers between devices, to_owners(): lax.all_to_all(value, ('y', 'c'), split_axis=0, concat_axis=0, tiled=True)  13.5 us
    pallas_call x2, Pallas kernels, pack_tokens(): pl.pallas_call(functools.partial(pack_tokens_kernel, n), out_shape=jax.Sh...  8.14 us
    unnamed x56, local copies, waits for them, and re-layouts  5.69 us
    all_to_all x3, waiting for transfers between devices, to_owners(): lax.all_to_all(value, ('y', 'c'), split_axis=0, concat_axis=0, tiled=True)  5.29 us
    pallas_call x1, Pallas kernels, pack_grads(): pl.pallas_call(pack_grads_kernel, out_shape=jax.ShapeDtypeStruct((N_YC, N...  4.8 us
  transfers between devices with their start and end apart: 30, of which 16 were waited for; matrix products, arithmetic and copies ran while one was open for 0% of the time, Pallas kernels for 17%

profile of v1, /device:TPU:6, one launch (start us, length us, event | category | flops | bytes accessed | tf_op | source)
XLA Modules:
  0.0 174.1 jit_solution(5440772588502587307)
XLA Ops:
  0.0 4.8 %shard_map.56 = bf16[8,128,768]{2,1,0:T(8,128)(2,1)} custom-call(s32[1]{0:T(128)} %bitcast.4.here_ref, s32[8,128]{1,0:T(8,128)} %bitcast.8, bf16[1024,768]{1,0:T(8,128)(2,1)} %bitcast.10), custom_call_target="tpu_custom_call" | custom-call | flops 1610612736 | bytes 3145728 | tf_op jit(solution)/shard_map/pallas_call | solution.py:88
  4.8 4.5 %all-to-all-start = ((bf16[8,128,768]{2,1,0:T(8,128)(2,1)}), bf16[8,128,768]{2,1,0:T(8,128)(2,1)S(1)}, u32[]{:S(2)}, u32[]{:S(2)}) async-start(bf16[8,128,768]{2,1,0:T(8,128)(2,1)} %shard_map.56), calls=%async_computation | async-start | bytes 3145728 | tf_op jit(solution)/shard_map/all_to_all | solution.py:321
  9.3 1.9 %shard_map.55 = (bf16[136,1024]{1,0:T(8,128)(2,1)}, bf16[128,1024]{1,0:T(8,128)(2,1)}) custom-call(bf16[128,2048]{1,0:T(8,128)(2,1)} %tokens_ref.1, s32[8,128]{1,0:T(8,128)} %bitcast.9), custom_call_target="tpu_custom_call" | custom-call | tf_op jit(solution)/shard_map/pallas_call | solution.py:59
  11.1 1.9 %collective-permute-start = (bf16[136,1024]{1,0:T(8,128)(2,1)}, bf16[136,1024]{1,0:T(8,128)(2,1)S(1)}, u32[]{:S(2)}, u32[]{:S(2)}) collective-permute-start(bf16[136,1024]{1,0:T(8,128)(2,1)} %get-tuple-element.25.refs_0_), channel_id=1, source_target_pairs={{0,8},{8,16},{16,24},{24,32},{32,40},{40,48},{48,56},{56,0},{1,9},... | collective-permute-start | bytes 835592 | tf_op jit(solution)/shard_map/ppermute | solution.py:317
  13.1 3.9 %collective-permute-start.1 = (bf16[136,1024]{1,0:T(8,128)(2,1)}, bf16[136,1024]{1,0:T(8,128)(2,1)S(1)}, u32[]{:S(2)}, u32[]{:S(2)}) collective-permute-start(bf16[136,1024]{1,0:T(8,128)(2,1)} %get-tuple-element.25.refs_0_), channel_id=1, source_target_pairs={{0,56},{8,0},{16,8},{24,16},{32,24},{40,32},{48,40},{56,48},{1,57}... | collective-permute-start | bytes 835592 | tf_op jit(solution)/shard_map/ppermute | solution.py:317
  17.0 3.2 %collective-permute-start.5 = (bf16[128,1024]{1,0:T(8,128)(2,1)}, bf16[128,1024]{1,0:T(8,128)(2,1)S(1)}, u32[]{:S(2)}, u32[]{:S(2)}) collective-permute-start(bf16[128,1024]{1,0:T(8,128)(2,1)} %get-tuple-element.26.refs_5_), channel_id=1, source_target_pairs={{0,56},{8,0},{16,8},{24,16},{32,24},{40,32},{48,40},{56,48},{1,57}... | collective-permute-start | bytes 786440 | tf_op jit(solution)/shard_map/ppermute | solution.py:317
  20.2 4.5 %collective-permute-done.refs_1_ = bf16[136,1024]{1,0:T(8,128)(2,1)S(1)} collective-permute-done((bf16[136,1024]{1,0:T(8,128)(2,1)}, bf16[136,1024]{1,0:T(8,128)(2,1)S(1)}, u32[]{:S(2)}, u32[]{:S(2)}) %collective-permute-start) | collective-permute-done | bytes 278560 | tf_op jit(solution)/shard_map/ppermute | solution.py:317
  24.7 3.2 %collective-permute-start.3 = (bf16[136,1024]{1,0:T(8,128)(2,1)S(1)}, bf16[136,1024]{1,0:T(8,128)(2,1)S(1)}, u32[]{:S(2)}, u32[]{:S(2)}) collective-permute-start(bf16[136,1024]{1,0:T(8,128)(2,1)S(1)} %collective-permute-done.1.refs_2_), channel_id=1, source_target_pairs={{0,56},{8,0},{16,8},{24,16},{32,24},{40,32},{48,40},{56,48},{1,57}... | collective-permute-start | bytes 835592 | tf_op jit(solution)/shard_map/ppermute | solution.py:317
  28.0 2.4 %collective-permute-done.4.refs_6_ = bf16[128,1024]{1,0:T(8,128)(2,1)S(1)} collective-permute-done((bf16[128,1024]{1,0:T(8,128)(2,1)}, bf16[128,1024]{1,0:T(8,128)(2,1)S(1)}, u32[]{:S(2)}, u32[]{:S(2)}) %collective-permute-start.4) | collective-permute-done | bytes 262176 | tf_op jit(solution)/shard_map/ppermute | solution.py:317
  30.4 3.2 %collective-permute-start.7 = (bf16[128,1024]{1,0:T(8,128)(2,1)S(1)}, bf16[128,1024]{1,0:T(8,128)(2,1)S(1)}, u32[]{:S(2)}, u32[]{:S(2)}) collective-permute-start(bf16[128,1024]{1,0:T(8,128)(2,1)S(1)} %collective-permute-done.5.refs_7_), channel_id=1, source_target_pairs={{0,56},{8,0},{16,8},{24,16},{32,24},{40,32},{48,40},{56,48},{1,57}... | collective-permute-start | bytes 786440 | tf_op jit(solution)/shard_map/ppermute | solution.py:317
  33.6 2.7 %collective-permute-done.2.refs_3_ = bf16[136,1024]{1,0:T(8,128)(2,1)S(1)} collective-permute-done((bf16[136,1024]{1,0:T(8,128)(2,1)S(1)}, bf16[136,1024]{1,0:T(8,128)(2,1)S(1)}, u32[]{:S(2)}, u32[]{:S(2)}) %collective-permute-start.2) | collective-permute-done | bytes 278560 | tf_op jit(solution)/shard_map/ppermute | solution.py:317
  36.3 3.2 %collective-permute-start.10 = (bf16[136,1024]{1,0:T(8,128)(2,1)S(1)}, bf16[136,1024]{1,0:T(8,128)(2,1)S(1)}, u32[]{:S(2)}, u32[]{:S(2)}) collective-permute-start(bf16[136,1024]{1,0:T(8,128)(2,1)S(1)} %collective-permute-done.3.refs_4_), channel_id=1, source_target_pairs={{0,56},{8,0},{16,8},{24,16},{32,24},{40,32},{48,40},{56,48},{1,57}... | collective-permute-start | bytes 835592 | tf_op jit(solution)/shard_map/ppermute | solution.py:317
  39.5 2.4 %collective-permute-done.6.refs_8_ = bf16[128,1024]{1,0:T(8,128)(2,1)S(1)} collective-permute-done((bf16[128,1024]{1,0:T(8,128)(2,1)S(1)}, bf16[128,1024]{1,0:T(8,128)(2,1)S(1)}, u32[]{:S(2)}, u32[]{:S(2)}) %collective-permute-start.6) | collective-permute-done | bytes 262176 | tf_op jit(solution)/shard_map/ppermute | solution.py:317
  42.0 3.5 %collective-permute-start.11 = (bf16[128,1024]{1,0:T(8,128)(2,1)S(1)}, bf16[128,1024]{1,0:T(8,128)(2,1)S(1)}, u32[]{:S(2)}, u32[]{:S(2)}) collective-permute-start(bf16[128,1024]{1,0:T(8,128)(2,1)S(1)} %collective-permute-done.7.refs_9_), channel_id=1, source_target_pairs={{0,56},{8,0},{16,8},{24,16},{32,24},{40,32},{48,40},{56,48},{1,57}... | collective-permute-start | bytes 786440 | tf_op jit(solution)/shard_map/ppermute | solution.py:317
  45.4 7.9 %collective-permute-done.9.refs_12_.refs_2_.refs_3_ = bf16[128,1024]{1,0:T(8,128)(2,1)S(1)} collective-permute-done((bf16[128,1024]{1,0:T(8,128)(2,1)S(1)}, bf16[128,1024]{1,0:T(8,128)(2,1)S(1)}, u32[]{:S(2)}, u32[]{:S(2)}) %collective-permute-start.9) | collective-permute-done | bytes 262176 | tf_op jit(solution)/shard_map/ppermute | solution.py:317
  55.5 4.7 %shard_map.57.refs_6_ = bf16[8,80,2048]{2,1,0:T(8,128)(2,1)} custom-call(s32[1]{0:T(128)} %bitcast.4.here_ref, bf16[136,1024]{1,0:T(8,128)(2,1)} %get-tuple-element.25.refs_0_, bf16[136,1024]{1,0:T(8,128)(2,1)} %copy-done.20, bf16[136,1024]{1,0:T(8,128)(2,1)} %copy-done.21, bf16[136,1024]{1,0:T(8,128)(2,1)} %copy-done.22, bf16[136,1024]{1,0:T(8,128)(2,1)} %copy-done.23, ...), custom_call_target="tpu_custom_call" | custom-call | flops 335544320 | bytes 5242880 | tf_op jit(solution)/shard_map/pallas_call | solution.py:137
  60.1 4.6 %all-to-all-start.1 = ((bf16[8,80,2048]{2,1,0:T(8,128)(2,1)}), bf16[8,80,2048]{2,1,0:T(8,128)(2,1)S(1)}, u32[]{:S(2)}, u32[]{:S(2)}) async-start(bf16[8,80,2048]{2,1,0:T(8,128)(2,1)} %shard_map.57.refs_6_), calls=%async_computation.1 | async-start | bytes 5242880 | tf_op jit(solution)/shard_map/all_to_all | solution.py:321
  64.7 2.9 %collective-permute-start.13 = (bf16[128,1024]{1,0:T(8,128)(2,1)S(1)}, bf16[128,1024]{1,0:T(8,128)(2,1)}, u32[]{:S(2)}, u32[]{:S(2)}) collective-permute-start(bf16[128,1024]{1,0:T(8,128)(2,1)S(1)} %copy-done.19), channel_id=1, source_target_pairs={{0,56},{8,0},{16,8},{24,16},{32,24},{40,32},{48,40},{56,48},{1,57}... | collective-permute-start | bytes 786440 | tf_op jit(solution)/shard_map/ppermute | solution.py:317
  67.6 2.6 %shard_map.59 = (bf16[128,768]{1,0:T(8,128)(2,1)}, bf16[128,768]{1,0:T(8,128)(2,1)}, bf16[128,768]{1,0:T(8,128)(2,1)}, bf16[128,768]{1,0:T(8,128)(2,1)}, bf16[12...) custom-call(bf16[8,128,768]{2,1,0:T(8,128)(2,1)} %copy-done.12, ...), custom_call_target="tpu_custom_call" | custom-call | tf_op jit(solution)/shard_map/pallas_call | solution.py:108
  70.2 4.8 %collective-permute-start.14 = (bf16[128,768]{1,0:T(8,128)(2,1)}, bf16[128,768]{1,0:T(8,128)(2,1)S(1)}, u32[]{:S(2)}, u32[]{:S(2)}) collective-permute-start(bf16[128,768]{1,0:T(8,128)(2,1)} %get-tuple-element.27), channel_id=1, source_target_pairs={{0,24},{8,32},{16,40},{24,48},{32,56},{40,0},{48,8},{56,16},{1,25}... | collective-permute-start | bytes 589832 | tf_op jit(solution)/shard_map/ppermute | solution.py:317
  75.3 2.3 %collective-permute-start.16 = (bf16[128,768]{1,0:T(8,128)(2,1)}, bf16[128,768]{1,0:T(8,128)(2,1)S(1)}, u32[]{:S(2)}, u32[]{:S(2)}) collective-permute-start(bf16[128,768]{1,0:T(8,128)(2,1)} %get-tuple-element.29), channel_id=1, source_target_pairs={{0,16},{8,24},{16,32},{24,40},{32,48},{40,56},{48,0},{56,8},{1,17}... | collective-permute-start | bytes 589832 | tf_op jit(solution)/shard_map/ppermute | solution.py:317
  77.6 1.9 %collective-permute-start.17 = (bf16[128,768]{1,0:T(8,128)(2,1)}, bf16[128,768]{1,0:T(8,128)(2,1)S(1)}, u32[]{:S(2)}, u32[]{:S(2)}) collective-permute-start(bf16[128,768]{1,0:T(8,128)(2,1)} %get-tuple-element.30), channel_id=1, source_target_pairs={{0,48},{8,56},{16,0},{24,8},{32,16},{40,24},{48,32},{56,40},{1,49}... | collective-permute-start | bytes 589832 | tf_op jit(solution)/shard_map/ppermute | solution.py:317
  79.4 2.1 %collective-permute-done.12.refs_2_ = bf16[136,1024]{1,0:T(8,128)(2,1)} collective-permute-done((bf16[136,1024]{1,0:T(8,128)(2,1)S(1)}, bf16[136,1024]{1,0:T(8,128)(2,1)}, u32[]{:S(2)}, u32[]{:S(2)}) %collective-permute-start.12) | collective-permute-done | bytes 278560 | tf_op jit(solution)/shard_map/ppermute | solution.py:317
  81.5 6.4 %collective-permute-done.14.refs_7_.refs_5_ = bf16[128,768]{1,0:T(8,128)(2,1)S(1)} collective-permute-done((bf16[128,768]{1,0:T(8,128)(2,1)}, bf16[128,768]{1,0:T(8,128)(2,1)S(1)}, u32[]{:S(2)}, u32[]{:S(2)}) %collective-permute-start.14) | collective-permute-done | bytes 196640 | tf_op jit(solution)/shard_map/ppermute | solution.py:317
  87.9 2.5 %collective-permute-done.15.refs_8_.refs_6_ = bf16[128,768]{1,0:T(8,128)(2,1)S(1)} collective-permute-done((bf16[128,768]{1,0:T(8,128)(2,1)}, bf16[128,768]{1,0:T(8,128)(2,1)S(1)}, u32[]{:S(2)}, u32[]{:S(2)}) %collective-permute-start.15) | collective-permute-done | bytes 196640 | tf_op jit(solution)/shard_map/ppermute | solution.py:317
  90.4 5.8 %collective-permute-done.16.refs_9_.refs_3_ = bf16[128,768]{1,0:T(8,128)(2,1)S(1)} collective-permute-done((bf16[128,768]{1,0:T(8,128)(2,1)}, bf16[128,768]{1,0:T(8,128)(2,1)S(1)}, u32[]{:S(2)}, u32[]{:S(2)}) %collective-permute-start.16) | collective-permute-done | bytes 196640 | tf_op jit(solution)/shard_map/ppermute | solution.py:317
  96.3 3.1 %collective-permute-done.17.refs_10_.refs_4_ = bf16[128,768]{1,0:T(8,128)(2,1)S(1)} collective-permute-done((bf16[128,768]{1,0:T(8,128)(2,1)}, bf16[128,768]{1,0:T(8,128)(2,1)S(1)}, u32[]{:S(2)}, u32[]{:S(2)}) %collective-permute-start.17) | collective-permute-done | bytes 196640 | tf_op jit(solution)/shard_map/ppermute | solution.py:317
  100.1 3.5 %shard_map.60 = bf16[8,48,2048]{2,1,0:T(8,128)(2,1)} custom-call(s32[1]{0:T(128)} %bitcast.4.here_ref, bf16[136,1024]{1,0:T(8,128)(2,1)} %copy-done.14, bf16[136,1024]{1,0:T(8,128)(2,1)} %copy-done.16, bf16[136,1024]{1,0:T(8,128)(2,1)} %collective-permute-done.12.refs_2_, bf16[128,1024]{1,0:T(8,128)(2,1)} %copy-done.17, bf16[128,1024]{1,0:T(8,128)(2,1)} %copy-done.18, ...), custom_call_target="tpu_custom_call" | custom-call | flops 201326592 | bytes 3145728 | tf_op jit(solution)/shard_map/pallas_call | solution.py:137
  103.6 1.5 copy-done.13
  105.1 4.4 %all-to-all-start.2 = ((bf16[8,48,2048]{2,1,0:T(8,128)(2,1)}), bf16[8,48,2048]{2,1,0:T(8,128)(2,1)S(1)}, u32[]{:S(2)}, u32[]{:S(2)}) async-start(bf16[8,48,2048]{2,1,0:T(8,128)(2,1)} %shard_map.60), calls=%async_computation.2 | async-start | bytes 3145728 | tf_op jit(solution)/shard_map/all_to_all | solution.py:321
  110.9 1.9 %collective-permute-start.19 = (bf16[128,768]{1,0:T(8,128)(2,1)}, bf16[128,768]{1,0:T(8,128)(2,1)}, u32[]{:S(2)}, u32[]{:S(2)}) collective-permute-start(bf16[128,768]{1,0:T(8,128)(2,1)} %get-tuple-element.33), channel_id=1, source_target_pairs={{0,56},{8,0},{16,8},{24,16},{32,24},{40,32},{48,40},{56,48},{1,57}... | collective-permute-start | bytes 589832 | tf_op jit(solution)/shard_map/ppermute | solution.py:317
  112.8 2.5 %collective-permute-start.20 = (bf16[128,768]{1,0:T(8,128)(2,1)}, bf16[128,768]{1,0:T(8,128)(2,1)}, u32[]{:S(2)}, u32[]{:S(2)}) collective-permute-start(bf16[128,768]{1,0:T(8,128)(2,1)} %get-tuple-element.34), channel_id=1, source_target_pairs={{0,32},{8,40},{16,48},{24,56},{32,0},{40,8},{48,16},{56,24},{1,33}... | collective-permute-start | bytes 589832 | tf_op jit(solution)/shard_map/ppermute | solution.py:317
  115.3 9.0 %shard_map.58.refs_0_.refs_9_.first = bf16[2048,640]{1,0:T(8,128)(2,1)S(1)} custom-call(bf16[8,80,2048]{2,1,0:T(8,128)(2,1)} %copy-done.13, bf16[1,2048,2048]{2,1,0:T(8,128)(2,1)} %basis_ref.3), custom_call_target="tpu_custom_call" | custom-call | flops 5368709120 | bytes 13631488 | tf_op jit(solution)/shard_map/pallas_call | solution.py:168
  124.3 1.5 copy-done
  125.8 5.3 %all-to-all-done.2.parts_ref = bf16[8,48,2048]{2,1,0:T(8,128)(2,1)S(1)} async-done(((bf16[8,48,2048]{2,1,0:T(8,128)(2,1)}), bf16[8,48,2048]{2,1,0:T(8,128)(2,1)S(1)}, u32[]{:S(2)}, u32[]{:S(2)}) %all-to-all-start.2) | async-done | bytes 1572896 | tf_op jit(solution)/shard_map/all_to_all | solution.py:321
  131.1 6.8 %shard_map.61.refs_10_.second = bf16[2048,384]{1,0:T(8,128)(2,1)S(1)} custom-call(bf16[8,48,2048]{2,1,0:T(8,128)(2,1)S(1)} %all-to-all-done.2.parts_ref, bf16[1,2048,2048]{2,1,0:T(8,128)(2,1)} %basis_ref.3, bf16[2048,640]{1,0:T(8,128)(2,1)} %copy-done), custom_call_target="tpu_custom_call" | custom-call | flops 3221225472 | bytes 11534336 | tf_op jit(solution)/shard_map/pallas_call | solution.py:168
  137.9 3.8 %shard_map.62 = (bf16[1024,768]{1,0:T(8,128)(2,1)S(1)}, s16[272,768]{1,0:T(8,128)(2,1)S(1)}, s16[272,768]{1,0:T(8,128)(2,1)S(1)}) custom-call(s32[4]{0:T(128)S(1)} %pad_add_fusion.place_ref, bf16[128,768]{1,0:T(8,128)(2,1)S(1)} %copy-done.11, bf16[128,768]{1,0:T(8,128)(2,1)} %collective-permute-done.18.refs_1_, ...), custom_call_target="tpu_custom_call" | custom-call | flops 2013265920 | bytes 12582912 | tf_op jit(solution)/shard_map/pallas_call | solution.py:226
  142.3 1.6 collective-permute-start.22
  143.9 2.0 %shard_map.65 = (s16[272,768]{1,0:T(8,128)(2,1)S(1)}, s16[272,768]{1,0:T(8,128)(2,1)S(1)}) custom-call(s32[4]{0:T(128)S(1)} %pad_add_fusion.place_ref, bf16[2048,640]{1,0:T(8,128)(2,1)S(1)} %copy-done.1, bf16[2048,384]{1,0:T(8,128)(2,1)S(1)} %shard_map.61.refs_10_.second, bf16[1024,768]{1,0:T(8,128)(2,1)S(1)} %get-tuple-element.35.g_ref), custom_call_target="tpu_custom_call" | custom-call | flops 805306368 | bytes 4194304 | tf_op jit(solution)/shard_map/pallas_call | solution.py:244
  146.8 2.4 %collective-permute-start.25 = (s16[272,768]{1,0:T(8,128)(2,1)S(1)}, s16[272,768]{1,0:T(8,128)(2,1)S(1)}, u32[]{:S(2)}, u32[]{:S(2)}) collective-permute-start(s16[272,768]{1,0:T(8,128)(2,1)S(1)} %get-tuple-element.43), channel_id=1, source_target_pairs={{0,64},{64,128},{128,192},{192,0},{1,65},{65,129},{129,193},{193,1... | collective-permute-start | bytes 1253384 | tf_op jit(solution)/shard_map/ppermute | solution.py:317
  149.2 2.8 %shard_map.63 = (f32[256,768]{1,0:T(8,128)S(1)}, f32[256,768]{1,0:T(8,128)S(1)}, f32[512,768]{1,0:T(8,128)S(1)}) custom-call(s32[4]{0:T(128)S(1)} %pad_add_fusion.place_ref, bf16[2048,640]{1,0:T(8,128)(2,1)S(1)} %copy-done.1, bf16[2048,384]{1,0:T(8,128)(2,1)S(1)} %shard_map.61.refs_10_.second, bf16[1024,768]{1,0:T(8,128)(2,1)S(1)} %get-tuple-element.35.g_ref), custom_call_target="tpu_custom_call" | custom-call | flops 1610612736 | bytes 8388608 | tf_op jit(solution)/shard_map/pallas_call | solution.py:265
  152.0 2.4 %collective-permute-done.21.got_up_ref = s16[272,768]{1,0:T(8,128)(2,1)S(1)} collective-permute-done((s16[272,768]{1,0:T(8,128)(2,1)S(1)}, s16[272,768]{1,0:T(8,128)(2,1)S(1)}, u32[]{:S(2)}, u32[]{:S(2)}) %collective-permute-start.21) | collective-permute-done | bytes 417824 | tf_op jit(solution)/shard_map/ppermute | solution.py:317
  154.4 1.7 collective-permute-done.22.got_down_ref
  157.4 1.7 collective-permute-start.26
  159.1 5.9 %collective-permute-done.24.top_b_ref = s16[272,768]{1,0:T(8,128)(2,1)S(1)} collective-permute-done((s16[272,768]{1,0:T(8,128)(2,1)S(1)}, s16[272,768]{1,0:T(8,128)(2,1)S(1)}, u32[]{:S(2)}, u32[]{:S(2)}) %collective-permute-start.24) | collective-permute-done | bytes 417824 | tf_op jit(solution)/shard_map/ppermute | solution.py:317
  165.1 5.9 %collective-permute-done.23.top_a_ref = s16[272,768]{1,0:T(8,128)(2,1)S(1)} collective-permute-done((s16[272,768]{1,0:T(8,128)(2,1)S(1)}, s16[272,768]{1,0:T(8,128)(2,1)S(1)}, u32[]{:S(2)}, u32[]{:S(2)}) %collective-permute-start.23) | collective-permute-done | bytes 417824 | tf_op jit(solution)/shard_map/ppermute | solution.py:317
  170.9 1.4 collective-permute-done.26.bottom_b_ref
  172.4 1.7 shard_map.66
  (81 shorter events, 7.2 us)
Async XLA Ops:
  4.8 48.6 %all-to-all-start = ((bf16[8,128,768]{2,1,0:T(8,128)(2,1)}), bf16[8,128,768]{2,1,0:T(8,128)(2,1)S(1)}, u32[]{:S(2)}, u32[]{:S(2)}) async-start(bf16[8,128,768]{2,1,0:T(8,128)(2,1)} %shard_map.56), calls=%async_computation | async-start | bytes 3145728 | tf_op jit(solution)/shard_map/all_to_all | solution.py:321
  11.1 13.6 %collective-permute-start = (bf16[136,1024]{1,0:T(8,128)(2,1)}, bf16[136,1024]{1,0:T(8,128)(2,1)S(1)}, u32[]{:S(2)}, u32[]{:S(2)}) collective-permute-start(bf16[136,1024]{1,0:T(8,128)(2,1)} %get-tuple-element.25.refs_0_), channel_id=1, source_target_pairs={{0,8},{8,16},{16,24},{24,32},{32,40},{40,48},{48,56},{56,0},{1,9},... | collective-permute-start | bytes 835592 | tf_op jit(solution)/shard_map/ppermute | solution.py:317
  13.1 11.7 %collective-permute-start.1 = (bf16[136,1024]{1,0:T(8,128)(2,1)}, bf16[136,1024]{1,0:T(8,128)(2,1)S(1)}, u32[]{:S(2)}, u32[]{:S(2)}) collective-permute-start(bf16[136,1024]{1,0:T(8,128)(2,1)} %get-tuple-element.25.refs_0_), channel_id=1, source_target_pairs={{0,56},{8,0},{16,8},{24,16},{32,24},{40,32},{48,40},{56,48},{1,57}... | collective-permute-start | bytes 835592 | tf_op jit(solution)/shard_map/ppermute | solution.py:317
  17.0 13.3 %collective-permute-start.4 = (bf16[128,1024]{1,0:T(8,128)(2,1)}, bf16[128,1024]{1,0:T(8,128)(2,1)S(1)}, u32[]{:S(2)}, u32[]{:S(2)}) collective-permute-start(bf16[128,1024]{1,0:T(8,128)(2,1)} %get-tuple-element.26.refs_5_), channel_id=1, source_target_pairs={{0,8},{8,16},{16,24},{24,32},{32,40},{40,48},{48,56},{56,0},{1,9},... | collective-permute-start | bytes 786440 | tf_op jit(solution)/shard_map/ppermute | solution.py:317
  17.0 13.3 %collective-permute-start.5 = (bf16[128,1024]{1,0:T(8,128)(2,1)}, bf16[128,1024]{1,0:T(8,128)(2,1)S(1)}, u32[]{:S(2)}, u32[]{:S(2)}) collective-permute-start(bf16[128,1024]{1,0:T(8,128)(2,1)} %get-tuple-element.26.refs_5_), channel_id=1, source_target_pairs={{0,56},{8,0},{16,8},{24,16},{32,24},{40,32},{48,40},{56,48},{1,57}... | collective-permute-start | bytes 786440 | tf_op jit(solution)/shard_map/ppermute | solution.py:317
  24.7 28.7 %copy-start.20 = (bf16[136,1024]{1,0:T(8,128)(2,1)}, bf16[136,1024]{1,0:T(8,128)(2,1)S(1)}, u32[]{:S(2)}) copy-start(bf16[136,1024]{1,0:T(8,128)(2,1)S(1)} %collective-permute-done.refs_1_) | copy-start | bytes 835588
  24.7 11.6 %collective-permute-start.2 = (bf16[136,1024]{1,0:T(8,128)(2,1)S(1)}, bf16[136,1024]{1,0:T(8,128)(2,1)S(1)}, u32[]{:S(2)}, u32[]{:S(2)}) collective-permute-start(bf16[136,1024]{1,0:T(8,128)(2,1)S(1)} %collective-permute-done.refs_1_), channel_id=1, source_target_pairs={{0,8},{8,16},{16,24},{24,32},{32,40},{40,48},{48,56},{56,0},{1,9},... | collective-permute-start | bytes 835592 | tf_op jit(solution)/shard_map/ppermute | solution.py:317
  24.7 28.7 %copy-start.21 = (bf16[136,1024]{1,0:T(8,128)(2,1)}, bf16[136,1024]{1,0:T(8,128)(2,1)S(1)}, u32[]{:S(2)}) copy-start(bf16[136,1024]{1,0:T(8,128)(2,1)S(1)} %collective-permute-done.1.refs_2_) | copy-start | bytes 835588
  24.7 11.6 %collective-permute-start.3 = (bf16[136,1024]{1,0:T(8,128)(2,1)S(1)}, bf16[136,1024]{1,0:T(8,128)(2,1)S(1)}, u32[]{:S(2)}, u32[]{:S(2)}) collective-permute-start(bf16[136,1024]{1,0:T(8,128)(2,1)S(1)} %collective-permute-done.1.refs_2_), channel_id=1, source_target_pairs={{0,56},{8,0},{16,8},{24,16},{32,24},{40,32},{48,40},{56,48},{1,57}... | collective-permute-start | bytes 835592 | tf_op jit(solution)/shard_map/ppermute | solution.py:317
  30.3 9.2 %copy-start.24 = (bf16[128,1024]{1,0:T(8,128)(2,1)}, bf16[128,1024]{1,0:T(8,128)(2,1)S(1)}, u32[]{:S(2)}) copy-start(bf16[128,1024]{1,0:T(8,128)(2,1)S(1)} %collective-permute-done.4.refs_6_) | copy-start | bytes 786436
  30.3 11.6 %collective-permute-start.6 = (bf16[128,1024]{1,0:T(8,128)(2,1)S(1)}, bf16[128,1024]{1,0:T(8,128)(2,1)S(1)}, u32[]{:S(2)}, u32[]{:S(2)}) collective-permute-start(bf16[128,1024]{1,0:T(8,128)(2,1)S(1)} %collective-permute-done.4.refs_6_), channel_id=1, source_target_pairs={{0,8},{8,16},{16,24},{24,32},{32,40},{40,48},{48,56},{56,0},{1,9},... | collective-permute-start | bytes 786440 | tf_op jit(solution)/shard_map/ppermute | solution.py:317
  30.3 11.6 %copy-start.25 = (bf16[128,1024]{1,0:T(8,128)(2,1)}, bf16[128,1024]{1,0:T(8,128)(2,1)S(1)}, u32[]{:S(2)}) copy-start(bf16[128,1024]{1,0:T(8,128)(2,1)S(1)} %collective-permute-done.5.refs_7_) | copy-start | bytes 786436
  30.4 11.6 %collective-permute-start.7 = (bf16[128,1024]{1,0:T(8,128)(2,1)S(1)}, bf16[128,1024]{1,0:T(8,128)(2,1)S(1)}, u32[]{:S(2)}, u32[]{:S(2)}) collective-permute-start(bf16[128,1024]{1,0:T(8,128)(2,1)S(1)} %collective-permute-done.5.refs_7_), channel_id=1, source_target_pairs={{0,56},{8,0},{16,8},{24,16},{32,24},{40,32},{48,40},{56,48},{1,57}... | collective-permute-start | bytes 786440 | tf_op jit(solution)/shard_map/ppermute | solution.py:317
  36.3 17.1 %copy-start.22 = (bf16[136,1024]{1,0:T(8,128)(2,1)}, bf16[136,1024]{1,0:T(8,128)(2,1)S(1)}, u32[]{:S(2)}) copy-start(bf16[136,1024]{1,0:T(8,128)(2,1)S(1)} %collective-permute-done.2.refs_3_) | copy-start | bytes 835588
  36.3 17.0 %collective-permute-start.8 = (bf16[136,1024]{1,0:T(8,128)(2,1)S(1)}, bf16[136,1024]{1,0:T(8,128)(2,1)S(1)}, u32[]{:S(2)}, u32[]{:S(2)}) collective-permute-start(bf16[136,1024]{1,0:T(8,128)(2,1)S(1)} %collective-permute-done.2.refs_3_), channel_id=1, source_target_pairs={{0,8},{8,16},{16,24},{24,32},{32,40},{40,48},{48,56},{56,0},{1,9},... | collective-permute-start | bytes 835592 | tf_op jit(solution)/shard_map/ppermute | solution.py:317
  36.3 17.0 %copy-start.23 = (bf16[136,1024]{1,0:T(8,128)(2,1)}, bf16[136,1024]{1,0:T(8,128)(2,1)S(1)}, u32[]{:S(2)}) copy-start(bf16[136,1024]{1,0:T(8,128)(2,1)S(1)} %collective-permute-done.3.refs_4_) | copy-start | bytes 835588
  36.3 17.1 %collective-permute-start.10 = (bf16[136,1024]{1,0:T(8,128)(2,1)S(1)}, bf16[136,1024]{1,0:T(8,128)(2,1)S(1)}, u32[]{:S(2)}, u32[]{:S(2)}) collective-permute-start(bf16[136,1024]{1,0:T(8,128)(2,1)S(1)} %collective-permute-done.3.refs_4_), channel_id=1, source_target_pairs={{0,56},{8,0},{16,8},{24,16},{32,24},{40,32},{48,40},{56,48},{1,57}... | collective-permute-start | bytes 835592 | tf_op jit(solution)/shard_map/ppermute | solution.py:317
  41.9 11.4 %copy-start.26 = (bf16[128,1024]{1,0:T(8,128)(2,1)}, bf16[128,1024]{1,0:T(8,128)(2,1)S(1)}, u32[]{:S(2)}) copy-start(bf16[128,1024]{1,0:T(8,128)(2,1)S(1)} %collective-permute-done.6.refs_8_) | copy-start | bytes 786436
  41.9 11.4 %collective-permute-start.9 = (bf16[128,1024]{1,0:T(8,128)(2,1)S(1)}, bf16[128,1024]{1,0:T(8,128)(2,1)S(1)}, u32[]{:S(2)}, u32[]{:S(2)}) collective-permute-start(bf16[128,1024]{1,0:T(8,128)(2,1)S(1)} %collective-permute-done.6.refs_8_), channel_id=1, source_target_pairs={{0,8},{8,16},{16,24},{24,32},{32,40},{40,48},{48,56},{56,0},{1,9},... | collective-permute-start | bytes 786440 | tf_op jit(solution)/shard_map/ppermute | solution.py:317
  41.9 11.4 %copy-start.27 = (bf16[128,1024]{1,0:T(8,128)(2,1)}, bf16[128,1024]{1,0:T(8,128)(2,1)S(1)}, u32[]{:S(2)}) copy-start(bf16[128,1024]{1,0:T(8,128)(2,1)S(1)} %collective-permute-done.7.refs_9_) | copy-start | bytes 786436
  42.0 11.4 %collective-permute-start.11 = (bf16[128,1024]{1,0:T(8,128)(2,1)S(1)}, bf16[128,1024]{1,0:T(8,128)(2,1)S(1)}, u32[]{:S(2)}, u32[]{:S(2)}) collective-permute-start(bf16[128,1024]{1,0:T(8,128)(2,1)S(1)} %collective-permute-done.7.refs_9_), channel_id=1, source_target_pairs={{0,56},{8,0},{16,8},{24,16},{32,24},{40,32},{48,40},{56,48},{1,57}... | collective-permute-start | bytes 786440 | tf_op jit(solution)/shard_map/ppermute | solution.py:317
  60.1 7.5 %copy-start.15 = (bf16[136,1024]{1,0:T(8,128)(2,1)S(1)}, bf16[136,1024]{1,0:T(8,128)(2,1)}, u32[]{:S(2)}) copy-start(bf16[136,1024]{1,0:T(8,128)(2,1)} %copy-done.14) | copy-start | bytes 835588
  60.1 43.5 %all-to-all-start.1 = ((bf16[8,80,2048]{2,1,0:T(8,128)(2,1)}), bf16[8,80,2048]{2,1,0:T(8,128)(2,1)S(1)}, u32[]{:S(2)}, u32[]{:S(2)}) async-start(bf16[8,80,2048]{2,1,0:T(8,128)(2,1)} %shard_map.57.refs_6_), calls=%async_computation.1 | async-start | bytes 5242880 | tf_op jit(solution)/shard_map/all_to_all | solution.py:321
  64.7 12.9 %collective-permute-start.13 = (bf16[128,1024]{1,0:T(8,128)(2,1)S(1)}, bf16[128,1024]{1,0:T(8,128)(2,1)}, u32[]{:S(2)}, u32[]{:S(2)}) collective-permute-start(bf16[128,1024]{1,0:T(8,128)(2,1)S(1)} %copy-done.19), channel_id=1, source_target_pairs={{0,56},{8,0},{16,8},{24,16},{32,24},{40,32},{48,40},{56,48},{1,57}... | collective-permute-start | bytes 786440 | tf_op jit(solution)/shard_map/ppermute | solution.py:317
  67.6 13.9 %collective-permute-start.12 = (bf16[136,1024]{1,0:T(8,128)(2,1)S(1)}, bf16[136,1024]{1,0:T(8,128)(2,1)}, u32[]{:S(2)}, u32[]{:S(2)}) collective-permute-start(bf16[136,1024]{1,0:T(8,128)(2,1)S(1)} %copy-done.15), channel_id=1, source_target_pairs={{0,8},{8,16},{16,24},{24,32},{32,40},{40,48},{48,56},{56,0},{1,9},... | collective-permute-start | bytes 835592 | tf_op jit(solution)/shard_map/ppermute | solution.py:317
  70.2 17.7 %collective-permute-start.14 = (bf16[128,768]{1,0:T(8,128)(2,1)}, bf16[128,768]{1,0:T(8,128)(2,1)S(1)}, u32[]{:S(2)}, u32[]{:S(2)}) collective-permute-start(bf16[128,768]{1,0:T(8,128)(2,1)} %get-tuple-element.27), channel_id=1, source_target_pairs={{0,24},{8,32},{16,40},{24,48},{32,56},{40,0},{48,8},{56,16},{1,25}... | collective-permute-start | bytes 589832 | tf_op jit(solution)/shard_map/ppermute | solution.py:317
  75.1 15.3 %collective-permute-start.15 = (bf16[128,768]{1,0:T(8,128)(2,1)}, bf16[128,768]{1,0:T(8,128)(2,1)S(1)}, u32[]{:S(2)}, u32[]{:S(2)}) collective-permute-start(bf16[128,768]{1,0:T(8,128)(2,1)} %get-tuple-element.28), channel_id=1, source_target_pairs={{0,40},{8,48},{16,56},{24,0},{32,8},{40,16},{48,24},{56,32},{1,41}... | collective-permute-start | bytes 589832 | tf_op jit(solution)/shard_map/ppermute | solution.py:317
  75.3 21.0 %collective-permute-start.16 = (bf16[128,768]{1,0:T(8,128)(2,1)}, bf16[128,768]{1,0:T(8,128)(2,1)S(1)}, u32[]{:S(2)}, u32[]{:S(2)}) collective-permute-start(bf16[128,768]{1,0:T(8,128)(2,1)} %get-tuple-element.29), channel_id=1, source_target_pairs={{0,16},{8,24},{16,32},{24,40},{32,48},{40,56},{48,0},{56,8},{1,17}... | collective-permute-start | bytes 589832 | tf_op jit(solution)/shard_map/ppermute | solution.py:317
  77.6 21.9 %collective-permute-start.17 = (bf16[128,768]{1,0:T(8,128)(2,1)}, bf16[128,768]{1,0:T(8,128)(2,1)S(1)}, u32[]{:S(2)}, u32[]{:S(2)}) collective-permute-start(bf16[128,768]{1,0:T(8,128)(2,1)} %get-tuple-element.30), channel_id=1, source_target_pairs={{0,48},{8,56},{16,0},{24,8},{32,16},{40,24},{48,32},{56,40},{1,49}... | collective-permute-start | bytes 589832 | tf_op jit(solution)/shard_map/ppermute | solution.py:317
  87.9 11.5 %copy-start.2 = (bf16[128,768]{1,0:T(8,128)(2,1)}, bf16[128,768]{1,0:T(8,128)(2,1)S(1)}, u32[]{:S(2)}) copy-start(bf16[128,768]{1,0:T(8,128)(2,1)S(1)} %collective-permute-done.14.refs_7_.refs_5_) | copy-start | bytes 589828
  90.4 9.0 %copy-start.4 = (bf16[128,768]{1,0:T(8,128)(2,1)}, bf16[128,768]{1,0:T(8,128)(2,1)S(1)}, u32[]{:S(2)}) copy-start(bf16[128,768]{1,0:T(8,128)(2,1)S(1)} %collective-permute-done.15.refs_8_.refs_6_) | copy-start | bytes 589828
  105.1 26.0 %all-to-all-start.2 = ((bf16[8,48,2048]{2,1,0:T(8,128)(2,1)}), bf16[8,48,2048]{2,1,0:T(8,128)(2,1)S(1)}, u32[]{:S(2)}, u32[]{:S(2)}) async-start(bf16[8,48,2048]{2,1,0:T(8,128)(2,1)} %shard_map.60), calls=%async_computation.2 | async-start | bytes 3145728 | tf_op jit(solution)/shard_map/all_to_all | solution.py:321
  109.6 28.3 %collective-permute-start.18 = (bf16[128,768]{1,0:T(8,128)(2,1)}, bf16[128,768]{1,0:T(8,128)(2,1)}, u32[]{:S(2)}, u32[]{:S(2)}) collective-permute-start(bf16[128,768]{1,0:T(8,128)(2,1)} %get-tuple-element.32), channel_id=1, source_target_pairs={{0,8},{8,16},{16,24},{24,32},{32,40},{40,48},{48,56},{56,0},{1,9},... | collective-permute-start | bytes 589832 | tf_op jit(solution)/shard_map/ppermute | solution.py:317
  110.9 26.9 %collective-permute-start.19 = (bf16[128,768]{1,0:T(8,128)(2,1)}, bf16[128,768]{1,0:T(8,128)(2,1)}, u32[]{:S(2)}, u32[]{:S(2)}) collective-permute-start(bf16[128,768]{1,0:T(8,128)(2,1)} %get-tuple-element.33), channel_id=1, source_target_pairs={{0,56},{8,0},{16,8},{24,16},{32,24},{40,32},{48,40},{56,48},{1,57}... | collective-permute-start | bytes 589832 | tf_op jit(solution)/shard_map/ppermute | solution.py:317
  112.8 25.0 %collective-permute-start.20 = (bf16[128,768]{1,0:T(8,128)(2,1)}, bf16[128,768]{1,0:T(8,128)(2,1)}, u32[]{:S(2)}, u32[]{:S(2)}) collective-permute-start(bf16[128,768]{1,0:T(8,128)(2,1)} %get-tuple-element.34), channel_id=1, source_target_pairs={{0,32},{8,40},{16,48},{24,56},{32,0},{40,8},{48,16},{56,24},{1,33}... | collective-permute-start | bytes 589832 | tf_op jit(solution)/shard_map/ppermute | solution.py:317
  125.8 12.1 %copy-start.3 = (bf16[128,768]{1,0:T(8,128)(2,1)S(1)}, bf16[128,768]{1,0:T(8,128)(2,1)}, u32[]{:S(2)}) copy-start(bf16[128,768]{1,0:T(8,128)(2,1)} %copy-done.2) | copy-start | bytes 589828
  125.8 12.1 %copy-start.5 = (bf16[128,768]{1,0:T(8,128)(2,1)S(1)}, bf16[128,768]{1,0:T(8,128)(2,1)}, u32[]{:S(2)}) copy-start(bf16[128,768]{1,0:T(8,128)(2,1)} %copy-done.4) | copy-start | bytes 589828
  125.8 12.1 %copy-start.7 = (bf16[128,768]{1,0:T(8,128)(2,1)S(1)}, bf16[128,768]{1,0:T(8,128)(2,1)}, u32[]{:S(2)}) copy-start(bf16[128,768]{1,0:T(8,128)(2,1)} %copy-done.6) | copy-start | bytes 589828
  125.8 12.1 %copy-start.9 = (bf16[128,768]{1,0:T(8,128)(2,1)S(1)}, bf16[128,768]{1,0:T(8,128)(2,1)}, u32[]{:S(2)}) copy-start(bf16[128,768]{1,0:T(8,128)(2,1)} %copy-done.8) | copy-start | bytes 589828
  125.8 12.1 %copy-start.10 = (bf16[1,768,768]{2,1,0:T(8,128)(2,1)S(1)}, bf16[1,768,768]{2,1,0:T(8,128)(2,1)}, u32[]{:S(2)}) copy-start(bf16[1,768,768]{2,1,0:T(8,128)(2,1)} %refs_8_.1) | copy-start | bytes 3538948
  131.1 6.9 %copy-start.1 = (bf16[2048,640]{1,0:T(8,128)(2,1)S(1)}, bf16[2048,640]{1,0:T(8,128)(2,1)}, u32[]{:S(2)}) copy-start(bf16[2048,640]{1,0:T(8,128)(2,1)} %copy-done) | copy-start | bytes 7864324
  131.1 6.9 %copy-start.11 = (bf16[128,768]{1,0:T(8,128)(2,1)S(1)}, bf16[128,768]{1,0:T(8,128)(2,1)}, u32[]{:S(2)}) copy-start(bf16[128,768]{1,0:T(8,128)(2,1)} %get-tuple-element.31.refs_0_) | copy-start | bytes 589828
  141.8 12.6 %collective-permute-start.21 = (s16[272,768]{1,0:T(8,128)(2,1)S(1)}, s16[272,768]{1,0:T(8,128)(2,1)S(1)}, u32[]{:S(2)}, u32[]{:S(2)}) collective-permute-start(s16[272,768]{1,0:T(8,128)(2,1)S(1)} %get-tuple-element.39), channel_id=1, source_target_pairs={{0,64},{64,128},{128,192},{192,0},{1,65},{65,129},{129,193},{193,1... | collective-permute-start | bytes 1253384 | tf_op jit(solution)/shard_map/ppermute | solution.py:317
  142.3 13.8 %collective-permute-start.22 = (s16[272,768]{1,0:T(8,128)(2,1)S(1)}, s16[272,768]{1,0:T(8,128)(2,1)S(1)}, u32[]{:S(2)}, u32[]{:S(2)}) collective-permute-start(s16[272,768]{1,0:T(8,128)(2,1)S(1)} %get-tuple-element.40), channel_id=1, source_target_pairs={{0,192},{64,0},{128,64},{192,128},{1,193},{65,1},{129,65},{193,129... | collective-permute-start | bytes 1253384 | tf_op jit(solution)/shard_map/ppermute | solution.py:317
  145.9 19.2 %collective-permute-start.24 = (s16[272,768]{1,0:T(8,128)(2,1)S(1)}, s16[272,768]{1,0:T(8,128)(2,1)S(1)}, u32[]{:S(2)}, u32[]{:S(2)}) collective-permute-start(s16[272,768]{1,0:T(8,128)(2,1)S(1)} %get-tuple-element.42), channel_id=1, source_target_pairs={{0,192},{64,0},{128,64},{192,128},{1,193},{65,1},{129,65},{193,129... | collective-permute-start | bytes 1253384 | tf_op jit(solution)/shard_map/ppermute | solution.py:317
  146.8 18.3 %collective-permute-start.25 = (s16[272,768]{1,0:T(8,128)(2,1)S(1)}, s16[272,768]{1,0:T(8,128)(2,1)S(1)}, u32[]{:S(2)}, u32[]{:S(2)}) collective-permute-start(s16[272,768]{1,0:T(8,128)(2,1)S(1)} %get-tuple-element.43), channel_id=1, source_target_pairs={{0,64},{64,128},{128,192},{192,0},{1,65},{65,129},{129,193},{193,1... | collective-permute-start | bytes 1253384 | tf_op jit(solution)/shard_map/ppermute | solution.py:317
  157.0 13.9 %collective-permute-start.23 = (s16[272,768]{1,0:T(8,128)(2,1)S(1)}, s16[272,768]{1,0:T(8,128)(2,1)S(1)}, u32[]{:S(2)}, u32[]{:S(2)}) collective-permute-start(s16[272,768]{1,0:T(8,128)(2,1)S(1)} %get-tuple-element.41), channel_id=1, source_target_pairs={{0,64},{64,128},{128,192},{192,0},{1,65},{65,129},{129,193},{193,1... | collective-permute-start | bytes 1253384 | tf_op jit(solution)/shard_map/ppermute | solution.py:317
  157.4 15.0 %collective-permute-start.26 = (s16[272,768]{1,0:T(8,128)(2,1)S(1)}, s16[272,768]{1,0:T(8,128)(2,1)S(1)}, u32[]{:S(2)}, u32[]{:S(2)}) collective-permute-start(s16[272,768]{1,0:T(8,128)(2,1)S(1)} %get-tuple-element.44), channel_id=1, source_target_pairs={{0,192},{64,0},{128,64},{192,128},{1,193},{65,1},{129,65},{193,129... | collective-permute-start | bytes 1253384 | tf_op jit(solution)/shard_map/ppermute | solution.py:317
  (10 other events, 15.8 us)

commit v2 on v1

--- a/solution.py
+++ b/solution.py
@@ -203,75 +203,103 @@
 
 
 N_FIRST = len(FIRST) * TOK
-
-
-def block_sum(a_refs, g_ref, quarter, half):
+N_EARLY = ROWS - TOK
+
+
+def block_sum(a_refs, g_refs, quarter, half):
     start = pl.multiple_of(quarter * QUARTER + half * HALF, HALF)
     first, second = a_refs
-    return jnp.dot(
-        first[pl.ds(start, HALF), :], g_ref[0:N_FIRST, :], preferred_element_type=F32
-    ) + jnp.dot(second[pl.ds(start, HALF), :], g_ref[N_FIRST:, :], preferred_element_type=F32)
-
-
-def far_kernel(place_ref, *refs):
-    rows_refs, (basis_ref, first, second, g_ref, up_ref, down_ref) = refs[:N_Z], refs[N_Z:]
+    early, last = g_refs
+    middle = N_EARLY - N_FIRST
+    total = jnp.dot(
+        first[pl.ds(start, HALF), :], early[0:N_FIRST, :], preferred_element_type=F32
+    )
+    total += jnp.dot(
+        second[pl.ds(start, HALF), 0:middle], early[N_FIRST:, :], preferred_element_type=F32
+    )
+    return total + jnp.dot(
+        second[pl.ds(start, HALF), middle:], last[...], preferred_element_type=F32
+    )
+
+
+def early_kernel(*refs):
+    rows_refs, (basis_ref, g_ref) = refs[:-2], refs[-2:]
     for k, rows_ref in enumerate(rows_refs):
         rotated = jnp.dot(rows_ref[...], basis_ref[0], preferred_element_type=F32)
         g_ref[k * TOK : (k + 1) * TOK, :] = (rotated * rotated).astype(BF)
-    encode(block_sum((first, second), g_ref, place_ref[0], 0), up_ref)
-    encode(block_sum((first, second), g_ref, place_ref[0], 1), down_ref)
-
-
-def far_blocks(place, rows, basis_out, a_sq):
+
+
+def early_blocks(rows, basis_out):
+    n = len(rows) * TOK
+    return pl.pallas_call(
+        early_kernel,
+        out_shape=jax.ShapeDtypeStruct((n, FF), BF),
+        in_specs=[IN_VMEM] * (len(rows) + 1),
+        out_specs=IN_VMEM,
+        compiler_params=params(8),
+        cost_estimate=pl.CostEstimate(
+            flops=2 * n * FF * FF, bytes_accessed=4 << 20, transcendentals=0
+        ),
+    )(*rows, basis_out)
+
+
+def far_kernel(place_ref, rows_ref, basis_ref, first, second, early, last, up_ref, down_ref):
+    rotated = jnp.dot(rows_ref[...], basis_ref[0], preferred_element_type=F32)
+    last[...] = (rotated * rotated).astype(BF)
+    encode(block_sum((first, second), (early, last), place_ref[0], 0), up_ref)
+    encode(block_sum((first, second), (early, last), place_ref[0], 1), down_ref)
+
+
+def far_blocks(place, rows, basis_out, a_sq, early):
     return pl.pallas_call(
         far_kernel,
-        out_shape=(jax.ShapeDtypeStruct((ROWS, FF), BF), CODE, CODE),
-        in_specs=[IN_SMEM] + [IN_VMEM] * (N_Z + 3),
+        out_shape=(jax.ShapeDtypeStruct((TOK, FF), BF), CODE, CODE),
+        in_specs=[IN_SMEM] + [IN_VMEM] * 5,
         out_specs=[IN_VMEM] * 3,
         compiler_params=params(8),
         cost_estimate=pl.CostEstimate(
-            flops=2 * ROWS * FF * (FF + QUARTER), bytes_accessed=12 << 20, transcendentals=0
-        ),
-    )(place, *rows, basis_out, *a_sq)
-
-
-def near_kernel(place_ref, first, second, g_ref, up_ref, down_ref):
-    encode(block_sum((first, second), g_ref, place_ref[1], 1), up_ref)
-    encode(block_sum((first, second), g_ref, place_ref[2], 0), down_ref)
+            flops=2 * ROWS * FF * QUARTER, bytes_accessed=8 << 20, transcendentals=0
+        ),
+    )(place, rows, basis_out, *a_sq, early)
+
+
+def near_kernel(place_ref, first, second, early, last, up_ref, down_ref):
+    encode(block_sum((first, second), (early, last), place_ref[1], 1), up_ref)
+    encode(block_sum((first, second), (early, last), place_ref[2], 0), down_ref)
 
 
 def near_blocks(place, a_sq, g_sq):
     return pl.pallas_call(
         near_kernel,
         out_shape=(CODE, CODE),
-        in_specs=[IN_SMEM] + [IN_VMEM] * 3,
+        in_specs=[IN_SMEM] + [IN_VMEM] * 4,
         out_specs=[IN_VMEM] * 2,
         compiler_params=params(4),
         cost_estimate=pl.CostEstimate(
             flops=2 * ROWS * FF * QUARTER, bytes_accessed=4 << 20, transcendentals=0
         ),
-    )(place, *a_sq, g_sq)
-
-
-def rest_kernel(place_ref, first, second, g_ref, up_ref, down_ref, own_ref):
-    a_refs = (first, second)
-    up_ref[...] = block_sum(a_refs, g_ref, place_ref[1], 0)
-    down_ref[...] = block_sum(a_refs, g_ref, place_ref[2], 1)
-    own_ref[0:HALF, :] = block_sum(a_refs, g_ref, place_ref[3], 0)
-    own_ref[HALF:QUARTER, :] = block_sum(a_refs, g_ref, place_ref[3], 1)
+    )(place, *a_sq, *g_sq)
+
+
+def rest_kernel(place_ref, first, second, early, last, up_ref, down_ref, own_ref):
+    a_refs, g_refs = (first, second), (early, last)
+    up_ref[...] = block_sum(a_refs, g_refs, place_ref[1], 0)
+    down_ref[...] = block_sum(a_refs, g_refs, place_ref[2], 1)
+    own_ref[0:HALF, :] = block_sum(a_refs, g_refs, place_ref[3], 0)
+    own_ref[HALF:QUARTER, :] = block_sum(a_refs, g_refs, place_ref[3], 1)
 
 
 def rest_blocks(place, a_sq, g_sq):
     return pl.pallas_call(
         rest_kernel,
         out_shape=(BLOCK, BLOCK, jax.ShapeDtypeStruct((QUARTER, FF), F32)),
-        in_specs=[IN_SMEM] + [IN_VMEM] * 3,
+        in_specs=[IN_SMEM] + [IN_VMEM] * 4,
         out_specs=[IN_VMEM] * 3,
         compiler_params=params(4),
         cost_estimate=pl.CostEstimate(
             flops=4 * ROWS * FF * QUARTER, bytes_accessed=8 << 20, transcendentals=0
         ),
-    )(place, *a_sq, g_sq)
+    )(place, *a_sq, *g_sq)
 
 
 def pass_on_kernel(up_ref, down_ref, got_up_ref, got_down_ref, out_up_ref, out_down_ref):
@@ -342,15 +370,19 @@
     by_z = regroup(grads_in, [*ring[3], *ring[5]])
     rows_out = [by_z[k] if k == 0 else shift(by_z[k], "z", k) for k in ORDER]
 
-    a_sq, gates = [], [grads_in, *ring[3], *ring[5]]
+    in_order, gates = [], [grads_in, *ring[3], *ring[5]]
     for senders in (FIRST, SECOND):
         packed = pack_tokens(
             here, [ring[k][0] for k in senders], [ring[k][1] for k in senders], gates
         )
-        gates = [packed] + [rows_out[ORDER.index(k)] for k in (3, 5, 2, 6)]
-        a_sq.append(rotate_inputs(to_owners(packed), basis_in, a_sq))
-
-    g_sq, far_up, far_down = far_blocks(place, rows_out, basis_out, a_sq)
+        gates = [packed] + [rows_out[ORDER.index(k)] for k in (1, 7, 2, 6, 3, 5)]
+        in_order.append(to_owners(packed))
+    early = early_blocks(rows_out[:-1], basis_out)
+    a_sq = [rotate_inputs(in_order[0], basis_in, [])]
+    a_sq.append(rotate_inputs(in_order[1], basis_in, [*a_sq, early]))
+
+    last, far_up, far_down = far_blocks(place, rows_out[-1], basis_out, a_sq, early)
+    g_sq = (early, last)
     got_far_up, got_far_down = shift(far_up, "x", 1), shift(far_down, "x", -1)
     near_up, near_down = near_blocks(place, a_sq, g_sq)
     got_near_up, got_near_down = shift(near_up, "x", 1), shift(near_down, "x", -1)

time: 175 us -> 176 us (level)
  waiting for transfers between devices: 62.5 us -> 60.1 us
    ppermute x27, waiting for transfers between devices: 57.2 us -> 55.2 us  [shift(): return lax.ppermute(value, axis, [(i, (i + by) % n) for i in range(n)])]
    unnamed x56 -> x66, local copies, waits for them, and re-layouts: 5.69 us -> 6.73 us
    pallas_call x1 -> x2, Pallas kernels: 3.85 us -> 3.99 us  [the longest x1 2.75 us: far_blocks(): pl.pallas_call(far_kernel, out_shape=(jax.ShapeDtypeStruct((TOK, FF), BF)...]
  transfers between devices with their start and end apart: 30 -> 30, of which waited for: 16 -> 13; matrix products, arithmetic and copies ran while one was open for 0% -> 0% of each run, Pallas kernels for 17% -> 18%
where the time goes in v2:
time: 176 us; the launch traced here: 175 us
  starting transfers between devices  62.4 us (35%)
  waiting for transfers between devices  60.1 us (34%)
  Pallas kernels  45.1 us (26%)
  local copies, waits for them, and re-layouts  6.73 us (4%)
    ppermute x27, waiting for transfers between devices, shift(): return lax.ppermute(value, axis, [(i, (i + by) % n) for i in range(n)])  55.2 us
    ppermute x27, starting transfers between devices, shift(): return lax.ppermute(value, axis, [(i, (i + by) % n) for i in range(n)])  48.8 us
    pallas_call x2, Pallas kernels, rotate_inputs(): pl.pallas_call(rotate_kernel, out_shape=jax.ShapeDtypeStruct((D, rows), B...  16.2 us
    all_to_all x3, starting transfers between devices, to_owners(): lax.all_to_all(value, ('y', 'c'), split_axis=0, concat_axis=0, tiled=True)  13.6 us
    pallas_call x2, Pallas kernels, pack_tokens(): pl.pallas_call(functools.partial(pack_tokens_kernel, n), out_shape=jax.Sh...  8.15 us
    unnamed x66, local copies, waits for them, and re-layouts  6.73 us
    all_to_all x3, waiting for transfers between devices, to_owners(): lax.all_to_all(value, ('y', 'c'), split_axis=0, concat_axis=0, tiled=True)  4.88 us
    pallas_call x1, Pallas kernels, pack_grads(): pl.pallas_call(pack_grads_kernel, out_shape=jax.ShapeDtypeStruct((N_YC, N...  4.8 us
  transfers between devices with their start and end apart: 30, of which 13 were waited for; matrix products, arithmetic and copies ran while one was open for 0% of the time, Pallas kernels for 18%

profile of v2, /device:TPU:6, one launch (start us, length us, event | category | flops | bytes accessed | tf_op | source)
XLA Modules:
  0.0 174.8 jit_solution(8211336045710666177)
XLA Ops:
  0.0 4.8 %shard_map.56 = bf16[8,128,768]{2,1,0:T(8,128)(2,1)} custom-call(s32[1]{0:T(128)} %bitcast.4.here_ref, s32[8,128]{1,0:T(8,128)} %bitcast.8, bf16[1024,768]{1,0:T(8,128)(2,1)} %bitcast.10), custom_call_target="tpu_custom_call" | custom-call | flops 1610612736 | bytes 3145728 | tf_op jit(solution)/shard_map/pallas_call | solution.py:88
  4.8 4.5 %all-to-all-start = ((bf16[8,128,768]{2,1,0:T(8,128)(2,1)}), bf16[8,128,768]{2,1,0:T(8,128)(2,1)S(1)}, u32[]{:S(2)}, u32[]{:S(2)}) async-start(bf16[8,128,768]{2,1,0:T(8,128)(2,1)} %shard_map.56), calls=%async_computation | async-start | bytes 3145728 | tf_op jit(solution)/shard_map/all_to_all | solution.py:349
  9.3 1.9 %shard_map.55 = (bf16[136,1024]{1,0:T(8,128)(2,1)}, bf16[128,1024]{1,0:T(8,128)(2,1)}) custom-call(bf16[128,2048]{1,0:T(8,128)(2,1)} %tokens_ref.1, s32[8,128]{1,0:T(8,128)} %bitcast.9), custom_call_target="tpu_custom_call" | custom-call | tf_op jit(solution)/shard_map/pallas_call | solution.py:59
  11.1 1.9 %collective-permute-start = (bf16[136,1024]{1,0:T(8,128)(2,1)}, bf16[136,1024]{1,0:T(8,128)(2,1)S(1)}, u32[]{:S(2)}, u32[]{:S(2)}) collective-permute-start(bf16[136,1024]{1,0:T(8,128)(2,1)} %get-tuple-element.25.refs_0_), channel_id=1, source_target_pairs={{0,8},{8,16},{16,24},{24,32},{32,40},{40,48},{48,56},{56,0},{1,9},... | collective-permute-start | bytes 835592 | tf_op jit(solution)/shard_map/ppermute | solution.py:345
  13.1 3.9 %collective-permute-start.1 = (bf16[136,1024]{1,0:T(8,128)(2,1)}, bf16[136,1024]{1,0:T(8,128)(2,1)S(1)}, u32[]{:S(2)}, u32[]{:S(2)}) collective-permute-start(bf16[136,1024]{1,0:T(8,128)(2,1)} %get-tuple-element.25.refs_0_), channel_id=1, source_target_pairs={{0,56},{8,0},{16,8},{24,16},{32,24},{40,32},{48,40},{56,48},{1,57}... | collective-permute-start | bytes 835592 | tf_op jit(solution)/shard_map/ppermute | solution.py:345
  17.0 3.2 %collective-permute-start.5 = (bf16[128,1024]{1,0:T(8,128)(2,1)}, bf16[128,1024]{1,0:T(8,128)(2,1)S(1)}, u32[]{:S(2)}, u32[]{:S(2)}) collective-permute-start(bf16[128,1024]{1,0:T(8,128)(2,1)} %get-tuple-element.26.refs_5_), channel_id=1, source_target_pairs={{0,56},{8,0},{16,8},{24,16},{32,24},{40,32},{48,40},{56,48},{1,57}... | collective-permute-start | bytes 786440 | tf_op jit(solution)/shard_map/ppermute | solution.py:345
  20.2 4.5 %collective-permute-done.refs_1_ = bf16[136,1024]{1,0:T(8,128)(2,1)S(1)} collective-permute-done((bf16[136,1024]{1,0:T(8,128)(2,1)}, bf16[136,1024]{1,0:T(8,128)(2,1)S(1)}, u32[]{:S(2)}, u32[]{:S(2)}) %collective-permute-start) | collective-permute-done | bytes 278560 | tf_op jit(solution)/shard_map/ppermute | solution.py:345
  24.7 3.2 %collective-permute-start.3 = (bf16[136,1024]{1,0:T(8,128)(2,1)S(1)}, bf16[136,1024]{1,0:T(8,128)(2,1)S(1)}, u32[]{:S(2)}, u32[]{:S(2)}) collective-permute-start(bf16[136,1024]{1,0:T(8,128)(2,1)S(1)} %collective-permute-done.1.refs_2_), channel_id=1, source_target_pairs={{0,56},{8,0},{16,8},{24,16},{32,24},{40,32},{48,40},{56,48},{1,57}... | collective-permute-start | bytes 835592 | tf_op jit(solution)/shard_map/ppermute | solution.py:345
  28.0 2.4 %collective-permute-done.4.refs_6_ = bf16[128,1024]{1,0:T(8,128)(2,1)S(1)} collective-permute-done((bf16[128,1024]{1,0:T(8,128)(2,1)}, bf16[128,1024]{1,0:T(8,128)(2,1)S(1)}, u32[]{:S(2)}, u32[]{:S(2)}) %collective-permute-start.4) | collective-permute-done | bytes 262176 | tf_op jit(solution)/shard_map/ppermute | solution.py:345
  30.4 3.2 %collective-permute-start.7 = (bf16[128,1024]{1,0:T(8,128)(2,1)S(1)}, bf16[128,1024]{1,0:T(8,128)(2,1)S(1)}, u32[]{:S(2)}, u32[]{:S(2)}) collective-permute-start(bf16[128,1024]{1,0:T(8,128)(2,1)S(1)} %collective-permute-done.5.refs_7_), channel_id=1, source_target_pairs={{0,56},{8,0},{16,8},{24,16},{32,24},{40,32},{48,40},{56,48},{1,57}... | collective-permute-start | bytes 786440 | tf_op jit(solution)/shard_map/ppermute | solution.py:345
  33.6 2.7 %collective-permute-done.2.refs_3_ = bf16[136,1024]{1,0:T(8,128)(2,1)S(1)} collective-permute-done((bf16[136,1024]{1,0:T(8,128)(2,1)S(1)}, bf16[136,1024]{1,0:T(8,128)(2,1)S(1)}, u32[]{:S(2)}, u32[]{:S(2)}) %collective-permute-start.2) | collective-permute-done | bytes 278560 | tf_op jit(solution)/shard_map/ppermute | solution.py:345
  36.3 3.2 %collective-permute-start.10 = (bf16[136,1024]{1,0:T(8,128)(2,1)S(1)}, bf16[136,1024]{1,0:T(8,128)(2,1)S(1)}, u32[]{:S(2)}, u32[]{:S(2)}) collective-permute-start(bf16[136,1024]{1,0:T(8,128)(2,1)S(1)} %collective-permute-done.3.refs_4_), channel_id=1, source_target_pairs={{0,56},{8,0},{16,8},{24,16},{32,24},{40,32},{48,40},{56,48},{1,57}... | collective-permute-start | bytes 835592 | tf_op jit(solution)/shard_map/ppermute | solution.py:345
  39.6 2.4 %collective-permute-done.6.refs_8_ = bf16[128,1024]{1,0:T(8,128)(2,1)S(1)} collective-permute-done((bf16[128,1024]{1,0:T(8,128)(2,1)S(1)}, bf16[128,1024]{1,0:T(8,128)(2,1)S(1)}, u32[]{:S(2)}, u32[]{:S(2)}) %collective-permute-start.6) | collective-permute-done | bytes 262176 | tf_op jit(solution)/shard_map/ppermute | solution.py:345
  42.0 3.5 %collective-permute-start.11 = (bf16[128,1024]{1,0:T(8,128)(2,1)S(1)}, bf16[128,1024]{1,0:T(8,128)(2,1)S(1)}, u32[]{:S(2)}, u32[]{:S(2)}) collective-permute-start(bf16[128,1024]{1,0:T(8,128)(2,1)S(1)} %collective-permute-done.7.refs_9_), channel_id=1, source_target_pairs={{0,56},{8,0},{16,8},{24,16},{32,24},{40,32},{48,40},{56,48},{1,57}... | collective-permute-start | bytes 786440 | tf_op jit(solution)/shard_map/ppermute | solution.py:345
  45.4 7.9 %collective-permute-done.9.refs_12_.refs_2_.refs_3_ = bf16[128,1024]{1,0:T(8,128)(2,1)S(1)} collective-permute-done((bf16[128,1024]{1,0:T(8,128)(2,1)S(1)}, bf16[128,1024]{1,0:T(8,128)(2,1)S(1)}, u32[]{:S(2)}, u32[]{:S(2)}) %collective-permute-start.9) | collective-permute-done | bytes 262176 | tf_op jit(solution)/shard_map/ppermute | solution.py:345
  54.3 1.1 copy-done.16
  55.5 4.7 %shard_map.57.refs_6_ = bf16[8,80,2048]{2,1,0:T(8,128)(2,1)} custom-call(s32[1]{0:T(128)} %bitcast.4.here_ref, bf16[136,1024]{1,0:T(8,128)(2,1)} %get-tuple-element.25.refs_0_, bf16[136,1024]{1,0:T(8,128)(2,1)} %copy-done.23, bf16[136,1024]{1,0:T(8,128)(2,1)} %copy-done.24, bf16[136,1024]{1,0:T(8,128)(2,1)} %copy-done.26, bf16[136,1024]{1,0:T(8,128)(2,1)} %copy-done.27, ...), custom_call_target="tpu_custom_call" | custom-call | flops 335544320 | bytes 5242880 | tf_op jit(solution)/shard_map/pallas_call | solution.py:137
  60.1 4.6 %all-to-all-start.1 = ((bf16[8,80,2048]{2,1,0:T(8,128)(2,1)}), bf16[8,80,2048]{2,1,0:T(8,128)(2,1)}, u32[]{:S(2)}, u32[]{:S(2)}) async-start(bf16[8,80,2048]{2,1,0:T(8,128)(2,1)} %shard_map.57.refs_6_), calls=%async_computation.1 | async-start | bytes 5242880 | tf_op jit(solution)/shard_map/all_to_all | solution.py:349
  64.8 3.2 %collective-permute-start.13 = (bf16[128,1024]{1,0:T(8,128)(2,1)S(1)}, bf16[128,1024]{1,0:T(8,128)(2,1)S(1)}, u32[]{:S(2)}, u32[]{:S(2)}) collective-permute-start(bf16[128,1024]{1,0:T(8,128)(2,1)S(1)} %copy-done.22), channel_id=1, source_target_pairs={{0,56},{8,0},{16,8},{24,16},{32,24},{40,32},{48,40},{56,48},{1,57}... | collective-permute-start | bytes 786440 | tf_op jit(solution)/shard_map/ppermute | solution.py:345
  68.0 2.7 %shard_map.59 = (bf16[128,768]{1,0:T(8,128)(2,1)}, bf16[128,768]{1,0:T(8,128)(2,1)}, bf16[128,768]{1,0:T(8,128)(2,1)}, bf16[128,768]{1,0:T(8,128)(2,1)}, bf16[12...) custom-call(bf16[8,128,768]{2,1,0:T(8,128)(2,1)} %copy-done.16, ...), custom_call_target="tpu_custom_call" | custom-call | tf_op jit(solution)/shard_map/pallas_call | solution.py:108
  70.7 3.2 %collective-permute-start.15 = (bf16[128,768]{1,0:T(8,128)(2,1)}, bf16[128,768]{1,0:T(8,128)(2,1)S(1)}, u32[]{:S(2)}, u32[]{:S(2)}) collective-permute-start(bf16[128,768]{1,0:T(8,128)(2,1)} %get-tuple-element.28), channel_id=1, source_target_pairs={{0,56},{8,0},{16,8},{24,16},{32,24},{40,32},{48,40},{56,48},{1,57}... | collective-permute-start | bytes 589832 | tf_op jit(solution)/shard_map/ppermute | solution.py:345
  74.6 3.7 %collective-permute-start.17 = (bf16[128,768]{1,0:T(8,128)(2,1)}, bf16[128,768]{1,0:T(8,128)(2,1)S(1)}, u32[]{:S(2)}, u32[]{:S(2)}) collective-permute-start(bf16[128,768]{1,0:T(8,128)(2,1)} %get-tuple-element.30), channel_id=1, source_target_pairs={{0,48},{8,56},{16,0},{24,8},{32,16},{40,24},{48,32},{56,40},{1,49}... | collective-permute-start | bytes 589832 | tf_op jit(solution)/shard_map/ppermute | solution.py:345
  78.3 1.6 collective-permute-start.18
  79.9 3.4 %collective-permute-start.19 = (bf16[128,768]{1,0:T(8,128)(2,1)}, bf16[128,768]{1,0:T(8,128)(2,1)S(1)}, u32[]{:S(2)}, u32[]{:S(2)}) collective-permute-start(bf16[128,768]{1,0:T(8,128)(2,1)} %get-tuple-element.32), channel_id=1, source_target_pairs={{0,40},{8,48},{16,56},{24,0},{32,8},{40,16},{48,24},{56,32},{1,41}... | collective-permute-start | bytes 589832 | tf_op jit(solution)/shard_map/ppermute | solution.py:345
  83.4 6.9 %collective-permute-done.16.refs_9_.refs_3_ = bf16[128,768]{1,0:T(8,128)(2,1)S(1)} collective-permute-done((bf16[128,768]{1,0:T(8,128)(2,1)}, bf16[128,768]{1,0:T(8,128)(2,1)S(1)}, u32[]{:S(2)}, u32[]{:S(2)}) %collective-permute-start.16) | collective-permute-done | bytes 196640 | tf_op jit(solution)/shard_map/ppermute | solution.py:345
  90.2 11.1 %collective-permute-done.18.refs_11_.refs_5_ = bf16[128,768]{1,0:T(8,128)(2,1)S(1)} collective-permute-done((bf16[128,768]{1,0:T(8,128)(2,1)}, bf16[128,768]{1,0:T(8,128)(2,1)S(1)}, u32[]{:S(2)}, u32[]{:S(2)}) %collective-permute-start.18) | collective-permute-done | bytes 196640 | tf_op jit(solution)/shard_map/ppermute | solution.py:345
  102.8 3.5 %shard_map.60 = bf16[8,48,2048]{2,1,0:T(8,128)(2,1)} custom-call(s32[1]{0:T(128)} %bitcast.4.here_ref, bf16[136,1024]{1,0:T(8,128)(2,1)} %copy-done.17, bf16[136,1024]{1,0:T(8,128)(2,1)} %copy-done.19, bf16[136,1024]{1,0:T(8,128)(2,1)} %copy-done.25, bf16[128,1024]{1,0:T(8,128)(2,1)} %copy-done.20, bf16[128,1024]{1,0:T(8,128)(2,1)} %copy-done.21, ...), custom_call_target="tpu_custom_call" | custom-call | flops 201326592 | bytes 3145728 | tf_op jit(solution)/shard_map/pallas_call | solution.py:137
  106.3 4.6 %all-to-all-start.2 = ((bf16[8,48,2048]{2,1,0:T(8,128)(2,1)}), bf16[8,48,2048]{2,1,0:T(8,128)(2,1)}, u32[]{:S(2)}, u32[]{:S(2)}) async-start(bf16[8,48,2048]{2,1,0:T(8,128)(2,1)} %shard_map.60), calls=%async_computation.2 | async-start | bytes 3145728 | tf_op jit(solution)/shard_map/all_to_all | solution.py:349
  110.9 3.1 %collective-permute-start.20 = (bf16[128,768]{1,0:T(8,128)(2,1)}, bf16[128,768]{1,0:T(8,128)(2,1)}, u32[]{:S(2)}, u32[]{:S(2)}) collective-permute-start(bf16[128,768]{1,0:T(8,128)(2,1)} %get-tuple-element.34), channel_id=1, source_target_pairs={{0,32},{8,40},{16,48},{24,56},{32,0},{40,8},{48,16},{56,24},{1,33}... | collective-permute-start | bytes 589832 | tf_op jit(solution)/shard_map/ppermute | solution.py:345
  114.1 0.9 copy-done.14
  115.0 0.9 copy-done.15
  115.9 1.2 shard_map.61.refs_1_.early
  117.2 9.0 %shard_map.58.refs_0_.first = bf16[2048,640]{1,0:T(8,128)(2,1)S(1)} custom-call(bf16[8,80,2048]{2,1,0:T(8,128)(2,1)} %all-to-all-done.1.parts_ref, bf16[1,2048,2048]{2,1,0:T(8,128)(2,1)} %basis_ref.4), custom_call_target="tpu_custom_call" | custom-call | flops 5368709120 | bytes 13631488 | tf_op jit(solution)/shard_map/pallas_call | solution.py:168
  126.2 1.5 copy-done
  127.7 4.9 %all-to-all-done.2.parts_ref = bf16[8,48,2048]{2,1,0:T(8,128)(2,1)} async-done(((bf16[8,48,2048]{2,1,0:T(8,128)(2,1)}), bf16[8,48,2048]{2,1,0:T(8,128)(2,1)}, u32[]{:S(2)}, u32[]{:S(2)}) %all-to-all-start.2) | async-done | bytes 1572896 | tf_op jit(solution)/shard_map/all_to_all | solution.py:349
  132.5 7.2 %shard_map.62.second = bf16[2048,384]{1,0:T(8,128)(2,1)S(1)} custom-call(bf16[8,48,2048]{2,1,0:T(8,128)(2,1)} %all-to-all-done.2.parts_ref, bf16[1,2048,2048]{2,1,0:T(8,128)(2,1)} %basis_ref.4, bf16[2048,640]{1,0:T(8,128)(2,1)} %copy-done, bf16[896,768]{1,0:T(8,128)(2,1)S(1)} %shard_map.61.refs_1_.early), custom_call_target="tpu_custom_call" | custom-call | flops 3221225472 | bytes 11534336 | tf_op jit(solution)/shard_map/pallas_call | solution.py:168
  139.8 2.7 %shard_map.63 = (bf16[128,768]{1,0:T(8,128)(2,1)S(1)}, s16[272,768]{1,0:T(8,128)(2,1)S(1)}, s16[272,768]{1,0:T(8,128)(2,1)S(1)}) custom-call(s32[4]{0:T(128)S(1)} %pad_add_fusion.place_ref, bf16[128,768]{1,0:T(8,128)(2,1)} %collective-permute-done.20.rows_ref, bf16[1,768,768]{2,1,0:T(8,128)(2,1)S(1)} %copy-done.2, bf16[2048,640]{1,0:T(8,128)(2,1)S(1)} %copy-done.1, ...), custom_call_target="tpu_custom_call" | custom-call | flops 805306368 | bytes 8388608 | tf_op jit(solution)/shard_map/pallas_call | solution.py:254
  143.1 1.5 collective-permute-start.22
  144.7 2.1 %shard_map.66 = (s16[272,768]{1,0:T(8,128)(2,1)S(1)}, s16[272,768]{1,0:T(8,128)(2,1)S(1)}) custom-call(s32[4]{0:T(128)S(1)} %pad_add_fusion.place_ref, bf16[2048,640]{1,0:T(8,128)(2,1)S(1)} %copy-done.1, bf16[2048,384]{1,0:T(8,128)(2,1)S(1)} %shard_map.62.second, bf16[896,768]{1,0:T(8,128)(2,1)S(1)} %shard_map.61.refs_1_.early, ...), custom_call_target="tpu_custom_call" | custom-call | flops 805306368 | bytes 4194304 | tf_op jit(solution)/shard_map/pallas_call | solution.py:272
  147.7 2.4 %collective-permute-start.25 = (s16[272,768]{1,0:T(8,128)(2,1)S(1)}, s16[272,768]{1,0:T(8,128)(2,1)S(1)}, u32[]{:S(2)}, u32[]{:S(2)}) collective-permute-start(s16[272,768]{1,0:T(8,128)(2,1)S(1)} %get-tuple-element.43), channel_id=1, source_target_pairs={{0,64},{64,128},{128,192},{192,0},{1,65},{65,129},{129,193},{193,1... | collective-permute-start | bytes 1253384 | tf_op jit(solution)/shard_map/ppermute | solution.py:345
  150.1 2.7 %shard_map.64 = (f32[256,768]{1,0:T(8,128)S(1)}, f32[256,768]{1,0:T(8,128)S(1)}, f32[512,768]{1,0:T(8,128)S(1)}) custom-call(s32[4]{0:T(128)S(1)} %pad_add_fusion.place_ref, bf16[2048,640]{1,0:T(8,128)(2,1)S(1)} %copy-done.1, bf16[2048,384]{1,0:T(8,128)(2,1)S(1)} %shard_map.62.second, bf16[896,768]{1,0:T(8,128)(2,1)S(1)} %shard_map.61.refs_1_.early, ...), custom_call_target="tpu_custom_call" | custom-call | flops 1610612736 | bytes 8388608 | tf_op jit(solution)/shard_map/pallas_call | solution.py:293
  152.8 2.3 %collective-permute-done.21.got_up_ref = s16[272,768]{1,0:T(8,128)(2,1)S(1)} collective-permute-done((s16[272,768]{1,0:T(8,128)(2,1)S(1)}, s16[272,768]{1,0:T(8,128)(2,1)S(1)}, u32[]{:S(2)}, u32[]{:S(2)}) %collective-permute-start.21) | collective-permute-done | bytes 417824 | tf_op jit(solution)/shard_map/ppermute | solution.py:345
  155.2 1.7 collective-permute-done.22.got_down_ref
  158.2 1.7 collective-permute-start.26
  159.9 6.0 %collective-permute-done.24.top_b_ref = s16[272,768]{1,0:T(8,128)(2,1)S(1)} collective-permute-done((s16[272,768]{1,0:T(8,128)(2,1)S(1)}, s16[272,768]{1,0:T(8,128)(2,1)S(1)}, u32[]{:S(2)}, u32[]{:S(2)}) %collective-permute-start.24) | collective-permute-done | bytes 417824 | tf_op jit(solution)/shard_map/ppermute | solution.py:345
  165.9 5.9 %collective-permute-done.23.top_a_ref = s16[272,768]{1,0:T(8,128)(2,1)S(1)} collective-permute-done((s16[272,768]{1,0:T(8,128)(2,1)S(1)}, s16[272,768]{1,0:T(8,128)(2,1)S(1)}, u32[]{:S(2)}, u32[]{:S(2)}) %collective-permute-start.23) | collective-permute-done | bytes 417824 | tf_op jit(solution)/shard_map/ppermute | solution.py:345
  171.7 1.4 collective-permute-done.26.bottom_b_ref
  173.1 1.7 shard_map.67
  (92 shorter events, 5.9 us)
Async XLA Ops:
  4.8 48.6 %all-to-all-start = ((bf16[8,128,768]{2,1,0:T(8,128)(2,1)}), bf16[8,128,768]{2,1,0:T(8,128)(2,1)S(1)}, u32[]{:S(2)}, u32[]{:S(2)}) async-start(bf16[8,128,768]{2,1,0:T(8,128)(2,1)} %shard_map.56), calls=%async_computation | async-start | bytes 3145728 | tf_op jit(solution)/shard_map/all_to_all | solution.py:349
  11.1 13.6 %collective-permute-start = (bf16[136,1024]{1,0:T(8,128)(2,1)}, bf16[136,1024]{1,0:T(8,128)(2,1)S(1)}, u32[]{:S(2)}, u32[]{:S(2)}) collective-permute-start(bf16[136,1024]{1,0:T(8,128)(2,1)} %get-tuple-element.25.refs_0_), channel_id=1, source_target_pairs={{0,8},{8,16},{16,24},{24,32},{32,40},{40,48},{48,56},{56,0},{1,9},... | collective-permute-start | bytes 835592 | tf_op jit(solution)/shard_map/ppermute | solution.py:345
  13.1 11.7 %collective-permute-start.1 = (bf16[136,1024]{1,0:T(8,128)(2,1)}, bf16[136,1024]{1,0:T(8,128)(2,1)S(1)}, u32[]{:S(2)}, u32[]{:S(2)}) collective-permute-start(bf16[136,1024]{1,0:T(8,128)(2,1)} %get-tuple-element.25.refs_0_), channel_id=1, source_target_pairs={{0,56},{8,0},{16,8},{24,16},{32,24},{40,32},{48,40},{56,48},{1,57}... | collective-permute-start | bytes 835592 | tf_op jit(solution)/shard_map/ppermute | solution.py:345
  17.0 13.3 %collective-permute-start.4 = (bf16[128,1024]{1,0:T(8,128)(2,1)}, bf16[128,1024]{1,0:T(8,128)(2,1)S(1)}, u32[]{:S(2)}, u32[]{:S(2)}) collective-permute-start(bf16[128,1024]{1,0:T(8,128)(2,1)} %get-tuple-element.26.refs_5_), channel_id=1, source_target_pairs={{0,8},{8,16},{16,24},{24,32},{32,40},{40,48},{48,56},{56,0},{1,9},... | collective-permute-start | bytes 786440 | tf_op jit(solution)/shard_map/ppermute | solution.py:345
  17.0 13.3 %collective-permute-start.5 = (bf16[128,1024]{1,0:T(8,128)(2,1)}, bf16[128,1024]{1,0:T(8,128)(2,1)S(1)}, u32[]{:S(2)}, u32[]{:S(2)}) collective-permute-start(bf16[128,1024]{1,0:T(8,128)(2,1)} %get-tuple-element.26.refs_5_), channel_id=1, source_target_pairs={{0,56},{8,0},{16,8},{24,16},{32,24},{40,32},{48,40},{56,48},{1,57}... | collective-permute-start | bytes 786440 | tf_op jit(solution)/shard_map/ppermute | solution.py:345
  24.7 28.7 %copy-start.23 = (bf16[136,1024]{1,0:T(8,128)(2,1)}, bf16[136,1024]{1,0:T(8,128)(2,1)S(1)}, u32[]{:S(2)}) copy-start(bf16[136,1024]{1,0:T(8,128)(2,1)S(1)} %collective-permute-done.refs_1_) | copy-start | bytes 835588
  24.7 11.6 %collective-permute-start.2 = (bf16[136,1024]{1,0:T(8,128)(2,1)S(1)}, bf16[136,1024]{1,0:T(8,128)(2,1)S(1)}, u32[]{:S(2)}, u32[]{:S(2)}) collective-permute-start(bf16[136,1024]{1,0:T(8,128)(2,1)S(1)} %collective-permute-done.refs_1_), channel_id=1, source_target_pairs={{0,8},{8,16},{16,24},{24,32},{32,40},{40,48},{48,56},{56,0},{1,9},... | collective-permute-start | bytes 835592 | tf_op jit(solution)/shard_map/ppermute | solution.py:345
  24.7 28.7 %copy-start.24 = (bf16[136,1024]{1,0:T(8,128)(2,1)}, bf16[136,1024]{1,0:T(8,128)(2,1)S(1)}, u32[]{:S(2)}) copy-start(bf16[136,1024]{1,0:T(8,128)(2,1)S(1)} %collective-permute-done.1.refs_2_) | copy-start | bytes 835588
  24.7 11.6 %collective-permute-start.3 = (bf16[136,1024]{1,0:T(8,128)(2,1)S(1)}, bf16[136,1024]{1,0:T(8,128)(2,1)S(1)}, u32[]{:S(2)}, u32[]{:S(2)}) collective-permute-start(bf16[136,1024]{1,0:T(8,128)(2,1)S(1)} %collective-permute-done.1.refs_2_), channel_id=1, source_target_pairs={{0,56},{8,0},{16,8},{24,16},{32,24},{40,32},{48,40},{56,48},{1,57}... | collective-permute-start | bytes 835592 | tf_op jit(solution)/shard_map/ppermute | solution.py:345
  30.3 9.2 %copy-start.28 = (bf16[128,1024]{1,0:T(8,128)(2,1)}, bf16[128,1024]{1,0:T(8,128)(2,1)S(1)}, u32[]{:S(2)}) copy-start(bf16[128,1024]{1,0:T(8,128)(2,1)S(1)} %collective-permute-done.4.refs_6_) | copy-start | bytes 786436
  30.3 11.6 %collective-permute-start.6 = (bf16[128,1024]{1,0:T(8,128)(2,1)S(1)}, bf16[128,1024]{1,0:T(8,128)(2,1)S(1)}, u32[]{:S(2)}, u32[]{:S(2)}) collective-permute-start(bf16[128,1024]{1,0:T(8,128)(2,1)S(1)} %collective-permute-done.4.refs_6_), channel_id=1, source_target_pairs={{0,8},{8,16},{16,24},{24,32},{32,40},{40,48},{48,56},{56,0},{1,9},... | collective-permute-start | bytes 786440 | tf_op jit(solution)/shard_map/ppermute | solution.py:345
  30.3 11.6 %copy-start.29 = (bf16[128,1024]{1,0:T(8,128)(2,1)}, bf16[128,1024]{1,0:T(8,128)(2,1)S(1)}, u32[]{:S(2)}) copy-start(bf16[128,1024]{1,0:T(8,128)(2,1)S(1)} %collective-permute-done.5.refs_7_) | copy-start | bytes 786436
  30.4 11.6 %collective-permute-start.7 = (bf16[128,1024]{1,0:T(8,128)(2,1)S(1)}, bf16[128,1024]{1,0:T(8,128)(2,1)S(1)}, u32[]{:S(2)}, u32[]{:S(2)}) collective-permute-start(bf16[128,1024]{1,0:T(8,128)(2,1)S(1)} %collective-permute-done.5.refs_7_), channel_id=1, source_target_pairs={{0,56},{8,0},{16,8},{24,16},{32,24},{40,32},{48,40},{56,48},{1,57}... | collective-permute-start | bytes 786440 | tf_op jit(solution)/shard_map/ppermute | solution.py:345
  36.3 17.1 %copy-start.26 = (bf16[136,1024]{1,0:T(8,128)(2,1)}, bf16[136,1024]{1,0:T(8,128)(2,1)S(1)}, u32[]{:S(2)}) copy-start(bf16[136,1024]{1,0:T(8,128)(2,1)S(1)} %collective-permute-done.2.refs_3_) | copy-start | bytes 835588
  36.3 17.0 %collective-permute-start.8 = (bf16[136,1024]{1,0:T(8,128)(2,1)S(1)}, bf16[136,1024]{1,0:T(8,128)(2,1)S(1)}, u32[]{:S(2)}, u32[]{:S(2)}) collective-permute-start(bf16[136,1024]{1,0:T(8,128)(2,1)S(1)} %collective-permute-done.2.refs_3_), channel_id=1, source_target_pairs={{0,8},{8,16},{16,24},{24,32},{32,40},{40,48},{48,56},{56,0},{1,9},... | collective-permute-start | bytes 835592 | tf_op jit(solution)/shard_map/ppermute | solution.py:345
  36.3 17.0 %copy-start.27 = (bf16[136,1024]{1,0:T(8,128)(2,1)}, bf16[136,1024]{1,0:T(8,128)(2,1)S(1)}, u32[]{:S(2)}) copy-start(bf16[136,1024]{1,0:T(8,128)(2,1)S(1)} %collective-permute-done.3.refs_4_) | copy-start | bytes 835588
  36.3 17.1 %collective-permute-start.10 = (bf16[136,1024]{1,0:T(8,128)(2,1)S(1)}, bf16[136,1024]{1,0:T(8,128)(2,1)S(1)}, u32[]{:S(2)}, u32[]{:S(2)}) collective-permute-start(bf16[136,1024]{1,0:T(8,128)(2,1)S(1)} %collective-permute-done.3.refs_4_), channel_id=1, source_target_pairs={{0,56},{8,0},{16,8},{24,16},{32,24},{40,32},{48,40},{56,48},{1,57}... | collective-permute-start | bytes 835592 | tf_op jit(solution)/shard_map/ppermute | solution.py:345
  41.9 11.4 %copy-start.31 = (bf16[128,1024]{1,0:T(8,128)(2,1)}, bf16[128,1024]{1,0:T(8,128)(2,1)S(1)}, u32[]{:S(2)}) copy-start(bf16[128,1024]{1,0:T(8,128)(2,1)S(1)} %collective-permute-done.6.refs_8_) | copy-start | bytes 786436
  41.9 11.4 %collective-permute-start.9 = (bf16[128,1024]{1,0:T(8,128)(2,1)S(1)}, bf16[128,1024]{1,0:T(8,128)(2,1)S(1)}, u32[]{:S(2)}, u32[]{:S(2)}) collective-permute-start(bf16[128,1024]{1,0:T(8,128)(2,1)S(1)} %collective-permute-done.6.refs_8_), channel_id=1, source_target_pairs={{0,8},{8,16},{16,24},{24,32},{32,40},{40,48},{48,56},{56,0},{1,9},... | collective-permute-start | bytes 786440 | tf_op jit(solution)/shard_map/ppermute | solution.py:345
  41.9 11.4 %copy-start.32 = (bf16[128,1024]{1,0:T(8,128)(2,1)}, bf16[128,1024]{1,0:T(8,128)(2,1)S(1)}, u32[]{:S(2)}) copy-start(bf16[128,1024]{1,0:T(8,128)(2,1)S(1)} %collective-permute-done.7.refs_9_) | copy-start | bytes 786436
  42.0 11.4 %collective-permute-start.11 = (bf16[128,1024]{1,0:T(8,128)(2,1)S(1)}, bf16[128,1024]{1,0:T(8,128)(2,1)S(1)}, u32[]{:S(2)}, u32[]{:S(2)}) collective-permute-start(bf16[128,1024]{1,0:T(8,128)(2,1)S(1)} %collective-permute-done.7.refs_9_), channel_id=1, source_target_pairs={{0,56},{8,0},{16,8},{24,16},{32,24},{40,32},{48,40},{56,48},{1,57}... | collective-permute-start | bytes 786440 | tf_op jit(solution)/shard_map/ppermute | solution.py:345
  60.1 46.1 %all-to-all-start.1 = ((bf16[8,80,2048]{2,1,0:T(8,128)(2,1)}), bf16[8,80,2048]{2,1,0:T(8,128)(2,1)}, u32[]{:S(2)}, u32[]{:S(2)}) async-start(bf16[8,80,2048]{2,1,0:T(8,128)(2,1)} %shard_map.57.refs_6_), calls=%async_computation.1 | async-start | bytes 5242880 | tf_op jit(solution)/shard_map/all_to_all | solution.py:349
  64.7 13.6 %collective-permute-start.12 = (bf16[136,1024]{1,0:T(8,128)(2,1)S(1)}, bf16[136,1024]{1,0:T(8,128)(2,1)S(1)}, u32[]{:S(2)}, u32[]{:S(2)}) collective-permute-start(bf16[136,1024]{1,0:T(8,128)(2,1)S(1)} %copy-done.18), channel_id=1, source_target_pairs={{0,8},{8,16},{16,24},{24,32},{32,40},{40,48},{48,56},{56,0},{1,9},... | collective-permute-start | bytes 835592 | tf_op jit(solution)/shard_map/ppermute | solution.py:345
  64.8 9.7 %collective-permute-start.13 = (bf16[128,1024]{1,0:T(8,128)(2,1)S(1)}, bf16[128,1024]{1,0:T(8,128)(2,1)S(1)}, u32[]{:S(2)}, u32[]{:S(2)}) collective-permute-start(bf16[128,1024]{1,0:T(8,128)(2,1)S(1)} %copy-done.22), channel_id=1, source_target_pairs={{0,56},{8,0},{16,8},{24,16},{32,24},{40,32},{48,40},{56,48},{1,57}... | collective-permute-start | bytes 786440 | tf_op jit(solution)/shard_map/ppermute | solution.py:345
  70.7 9.2 %collective-permute-start.14 = (bf16[128,768]{1,0:T(8,128)(2,1)}, bf16[128,768]{1,0:T(8,128)(2,1)S(1)}, u32[]{:S(2)}, u32[]{:S(2)}) collective-permute-start(bf16[128,768]{1,0:T(8,128)(2,1)} %get-tuple-element.27), channel_id=1, source_target_pairs={{0,8},{8,16},{16,24},{24,32},{32,40},{40,48},{48,56},{56,0},{1,9},... | collective-permute-start | bytes 589832 | tf_op jit(solution)/shard_map/ppermute | solution.py:345
  70.7 12.6 %collective-permute-start.15 = (bf16[128,768]{1,0:T(8,128)(2,1)}, bf16[128,768]{1,0:T(8,128)(2,1)S(1)}, u32[]{:S(2)}, u32[]{:S(2)}) collective-permute-start(bf16[128,768]{1,0:T(8,128)(2,1)} %get-tuple-element.28), channel_id=1, source_target_pairs={{0,56},{8,0},{16,8},{24,16},{32,24},{40,32},{48,40},{56,48},{1,57}... | collective-permute-start | bytes 589832 | tf_op jit(solution)/shard_map/ppermute | solution.py:345
  73.9 16.3 %collective-permute-start.16 = (bf16[128,768]{1,0:T(8,128)(2,1)}, bf16[128,768]{1,0:T(8,128)(2,1)S(1)}, u32[]{:S(2)}, u32[]{:S(2)}) collective-permute-start(bf16[128,768]{1,0:T(8,128)(2,1)} %get-tuple-element.29), channel_id=1, source_target_pairs={{0,16},{8,24},{16,32},{24,40},{32,48},{40,56},{48,0},{56,8},{1,17}... | collective-permute-start | bytes 589832 | tf_op jit(solution)/shard_map/ppermute | solution.py:345
  74.6 26.8 %copy-start.30 = (bf16[128,1024]{1,0:T(8,128)(2,1)}, bf16[128,1024]{1,0:T(8,128)(2,1)S(1)}, u32[]{:S(2)}) copy-start(bf16[128,1024]{1,0:T(8,128)(2,1)S(1)} %collective-permute-done.13.refs_5_) | copy-start | bytes 786436
  74.6 15.7 %collective-permute-start.17 = (bf16[128,768]{1,0:T(8,128)(2,1)}, bf16[128,768]{1,0:T(8,128)(2,1)S(1)}, u32[]{:S(2)}, u32[]{:S(2)}) collective-permute-start(bf16[128,768]{1,0:T(8,128)(2,1)} %get-tuple-element.30), channel_id=1, source_target_pairs={{0,48},{8,56},{16,0},{24,8},{32,16},{40,24},{48,32},{56,40},{1,49}... | collective-permute-start | bytes 589832 | tf_op jit(solution)/shard_map/ppermute | solution.py:345
  78.3 23.1 %copy-start.25 = (bf16[136,1024]{1,0:T(8,128)(2,1)}, bf16[136,1024]{1,0:T(8,128)(2,1)S(1)}, u32[]{:S(2)}) copy-start(bf16[136,1024]{1,0:T(8,128)(2,1)S(1)} %collective-permute-done.12.refs_2_) | copy-start | bytes 835588
  78.3 23.1 %collective-permute-start.18 = (bf16[128,768]{1,0:T(8,128)(2,1)}, bf16[128,768]{1,0:T(8,128)(2,1)S(1)}, u32[]{:S(2)}, u32[]{:S(2)}) collective-permute-start(bf16[128,768]{1,0:T(8,128)(2,1)} %get-tuple-element.31), channel_id=1, source_target_pairs={{0,24},{8,32},{16,40},{24,48},{32,56},{40,0},{48,8},{56,16},{1,25}... | collective-permute-start | bytes 589832 | tf_op jit(solution)/shard_map/ppermute | solution.py:345
  79.9 21.5 %copy-start.3 = (bf16[128,768]{1,0:T(8,128)(2,1)}, bf16[128,768]{1,0:T(8,128)(2,1)S(1)}, u32[]{:S(2)}) copy-start(bf16[128,768]{1,0:T(8,128)(2,1)S(1)} %collective-permute-done.14.refs_7_.refs_1_) | copy-start | bytes 589828
  79.9 21.5 %collective-permute-start.19 = (bf16[128,768]{1,0:T(8,128)(2,1)}, bf16[128,768]{1,0:T(8,128)(2,1)S(1)}, u32[]{:S(2)}, u32[]{:S(2)}) collective-permute-start(bf16[128,768]{1,0:T(8,128)(2,1)} %get-tuple-element.32), channel_id=1, source_target_pairs={{0,40},{8,48},{16,56},{24,0},{32,8},{40,16},{48,24},{56,32},{1,41}... | collective-permute-start | bytes 589832 | tf_op jit(solution)/shard_map/ppermute | solution.py:345
  83.4 18.1 %copy-start.5 = (bf16[128,768]{1,0:T(8,128)(2,1)}, bf16[128,768]{1,0:T(8,128)(2,1)S(1)}, u32[]{:S(2)}) copy-start(bf16[128,768]{1,0:T(8,128)(2,1)S(1)} %collective-permute-done.15.refs_8_.refs_2_) | copy-start | bytes 589828
  90.2 11.2 %copy-start.7 = (bf16[128,768]{1,0:T(8,128)(2,1)}, bf16[128,768]{1,0:T(8,128)(2,1)S(1)}, u32[]{:S(2)}) copy-start(bf16[128,768]{1,0:T(8,128)(2,1)S(1)} %collective-permute-done.16.refs_9_.refs_3_) | copy-start | bytes 589828
  90.2 11.2 %copy-start.9 = (bf16[128,768]{1,0:T(8,128)(2,1)}, bf16[128,768]{1,0:T(8,128)(2,1)S(1)}, u32[]{:S(2)}) copy-start(bf16[128,768]{1,0:T(8,128)(2,1)S(1)} %collective-permute-done.17.refs_10_.refs_4_) | copy-start | bytes 589828
  106.2 7.8 %copy-start.2 = (bf16[1,768,768]{2,1,0:T(8,128)(2,1)S(1)}, bf16[1,768,768]{2,1,0:T(8,128)(2,1)}, u32[]{:S(2)}) copy-start(bf16[1,768,768]{2,1,0:T(8,128)(2,1)} %basis_ref.5) | copy-start | bytes 3538948
  106.2 7.8 %copy-start.4 = (bf16[128,768]{1,0:T(8,128)(2,1)S(1)}, bf16[128,768]{1,0:T(8,128)(2,1)}, u32[]{:S(2)}) copy-start(bf16[128,768]{1,0:T(8,128)(2,1)} %copy-done.3) | copy-start | bytes 589828
  106.2 7.8 %copy-start.6 = (bf16[128,768]{1,0:T(8,128)(2,1)S(1)}, bf16[128,768]{1,0:T(8,128)(2,1)}, u32[]{:S(2)}) copy-start(bf16[128,768]{1,0:T(8,128)(2,1)} %copy-done.5) | copy-start | bytes 589828
  106.2 7.8 %copy-start.8 = (bf16[128,768]{1,0:T(8,128)(2,1)S(1)}, bf16[128,768]{1,0:T(8,128)(2,1)}, u32[]{:S(2)}) copy-start(bf16[128,768]{1,0:T(8,128)(2,1)} %copy-done.7) | copy-start | bytes 589828
  106.3 26.3 %all-to-all-start.2 = ((bf16[8,48,2048]{2,1,0:T(8,128)(2,1)}), bf16[8,48,2048]{2,1,0:T(8,128)(2,1)}, u32[]{:S(2)}, u32[]{:S(2)}) async-start(bf16[8,48,2048]{2,1,0:T(8,128)(2,1)} %shard_map.60), calls=%async_computation.2 | async-start | bytes 3145728 | tf_op jit(solution)/shard_map/all_to_all | solution.py:349
  110.9 28.9 %collective-permute-start.20 = (bf16[128,768]{1,0:T(8,128)(2,1)}, bf16[128,768]{1,0:T(8,128)(2,1)}, u32[]{:S(2)}, u32[]{:S(2)}) collective-permute-start(bf16[128,768]{1,0:T(8,128)(2,1)} %get-tuple-element.34), channel_id=1, source_target_pairs={{0,32},{8,40},{16,48},{24,56},{32,0},{40,8},{48,16},{56,24},{1,33}... | collective-permute-start | bytes 589832 | tf_op jit(solution)/shard_map/ppermute | solution.py:345
  142.6 12.6 %collective-permute-start.21 = (s16[272,768]{1,0:T(8,128)(2,1)S(1)}, s16[272,768]{1,0:T(8,128)(2,1)S(1)}, u32[]{:S(2)}, u32[]{:S(2)}) collective-permute-start(s16[272,768]{1,0:T(8,128)(2,1)S(1)} %get-tuple-element.39), channel_id=1, source_target_pairs={{0,64},{64,128},{128,192},{192,0},{1,65},{65,129},{129,193},{193,1... | collective-permute-start | bytes 1253384 | tf_op jit(solution)/shard_map/ppermute | solution.py:345
  143.1 13.8 %collective-permute-start.22 = (s16[272,768]{1,0:T(8,128)(2,1)S(1)}, s16[272,768]{1,0:T(8,128)(2,1)S(1)}, u32[]{:S(2)}, u32[]{:S(2)}) collective-permute-start(s16[272,768]{1,0:T(8,128)(2,1)S(1)} %get-tuple-element.40), channel_id=1, source_target_pairs={{0,192},{64,0},{128,64},{192,128},{1,193},{65,1},{129,65},{193,129... | collective-permute-start | bytes 1253384 | tf_op jit(solution)/shard_map/ppermute | solution.py:345
  146.8 19.1 %collective-permute-start.24 = (s16[272,768]{1,0:T(8,128)(2,1)S(1)}, s16[272,768]{1,0:T(8,128)(2,1)S(1)}, u32[]{:S(2)}, u32[]{:S(2)}) collective-permute-start(s16[272,768]{1,0:T(8,128)(2,1)S(1)} %get-tuple-element.42), channel_id=1, source_target_pairs={{0,192},{64,0},{128,64},{192,128},{1,193},{65,1},{129,65},{193,129... | collective-permute-start | bytes 1253384 | tf_op jit(solution)/shard_map/ppermute | solution.py:345
  147.7 18.2 %collective-permute-start.25 = (s16[272,768]{1,0:T(8,128)(2,1)S(1)}, s16[272,768]{1,0:T(8,128)(2,1)S(1)}, u32[]{:S(2)}, u32[]{:S(2)}) collective-permute-start(s16[272,768]{1,0:T(8,128)(2,1)S(1)} %get-tuple-element.43), channel_id=1, source_target_pairs={{0,64},{64,128},{128,192},{192,0},{1,65},{65,129},{129,193},{193,1... | collective-permute-start | bytes 1253384 | tf_op jit(solution)/shard_map/ppermute | solution.py:345
  157.8 13.9 %collective-permute-start.23 = (s16[272,768]{1,0:T(8,128)(2,1)S(1)}, s16[272,768]{1,0:T(8,128)(2,1)S(1)}, u32[]{:S(2)}, u32[]{:S(2)}) collective-permute-start(s16[272,768]{1,0:T(8,128)(2,1)S(1)} %get-tuple-element.41), channel_id=1, source_target_pairs={{0,64},{64,128},{128,192},{192,0},{1,65},{65,129},{129,193},{193,1... | collective-permute-start | bytes 1253384 | tf_op jit(solution)/shard_map/ppermute | solution.py:345
  158.2 15.0 %collective-permute-start.26 = (s16[272,768]{1,0:T(8,128)(2,1)S(1)}, s16[272,768]{1,0:T(8,128)(2,1)S(1)}, u32[]{:S(2)}, u32[]{:S(2)}) collective-permute-start(s16[272,768]{1,0:T(8,128)(2,1)S(1)} %get-tuple-element.44), channel_id=1, source_target_pairs={{0,192},{64,0},{128,64},{192,128},{1,193},{65,1},{129,65},{193,129... | collective-permute-start | bytes 1253384 | tf_op jit(solution)/shard_map/ppermute | solution.py:345
  (15 other events, 41.2 us)

commit v3 on v1

--- a/solution.py
+++ b/solution.py
@@ -11,9 +11,7 @@
 CAP = 16
 N_X, N_Z, N_Y, N_C = 4, 8, 4, 2
 N_YC = N_Y * N_C
-FIRST = (0, 1, 7, 2, 6)
-SECOND = (3, 5, 4)
-ORDER = FIRST + SECOND
+ORDER = (0, 1, 7, 2, 6, 3, 5, 4)
 TOK = 128
 TOP = 8
 D = 2048
@@ -149,38 +147,25 @@
 STRIP = 512
 
 
-def rotate_kernel(parts_ref, basis_ref, *refs):
-    out_ref, rows_ref = refs[-2:]
-
-    @pl.when(pl.program_id(0) == 0)
-    def _():
-        for k in range(N_YC):
-            for b in range(rows_ref.shape[0] // TOK):
-                start = b * TOK + k * CAP
-                rows_ref[start : start + CAP, :] = parts_ref[k, b * CAP : (b + 1) * CAP, :]
-
-    rotated = jnp.dot(rows_ref[...], basis_ref[0], preferred_element_type=F32)
-    out_ref[...] = jnp.transpose((rotated * rotated).astype(BF))
-
-
-def rotate_inputs(parts, basis_in, gates):
-    rows = parts.shape[1] * N_YC
+def rotate_kernel(rows_ref, basis_ref, *refs):
+    rows = rows_ref[...].reshape(ROWS, D)
+    rotated = jnp.dot(rows, basis_ref[0], preferred_element_type=F32)
+    refs[-1][...] = jnp.transpose((rotated * rotated).astype(BF))
+
+
+def rotate_inputs(rows, basis_in, gates):
     return pl.pallas_call(
         rotate_kernel,
-        out_shape=jax.ShapeDtypeStruct((D, rows), BF),
+        out_shape=jax.ShapeDtypeStruct((D, ROWS), BF),
         grid=(D // STRIP,),
-        in_specs=[
-            pl.BlockSpec(parts.shape, lambda i: (0, 0, 0)),
-            pl.BlockSpec((1, D, STRIP), lambda i: (0, 0, i)),
-        ]
+        in_specs=[IN_VMEM, pl.BlockSpec((1, D, STRIP), lambda i: (0, 0, i))]
         + [pl.BlockSpec(memory_space=pl.ANY)] * len(gates),
-        out_specs=pl.BlockSpec((STRIP, rows), lambda i: (i, 0)),
-        scratch_shapes=[pltpu.VMEM((rows, D), BF)],
-        compiler_params=params(50),
-        cost_estimate=pl.CostEstimate(
-            flops=2 * rows * D * D, bytes_accessed=2 * D * D + 4 * rows * D, transcendentals=0
-        ),
-    )(parts, basis_in, *gates)
+        out_specs=pl.BlockSpec((STRIP, ROWS), lambda i: (i, 0)),
+        compiler_params=params(54),
+        cost_estimate=pl.CostEstimate(
+            flops=2 * ROWS * D * D, bytes_accessed=2 * D * D + 4 * ROWS * D, transcendentals=0
+        ),
+    )(rows, basis_in, *gates)
 
 
 def encode(values, out_ref):
@@ -202,76 +187,88 @@
 BLOCK = jax.ShapeDtypeStruct((HALF, FF), F32)
 
 
-N_FIRST = len(FIRST) * TOK
-
-
-def block_sum(a_refs, g_ref, quarter, half):
+def block_sum(a_ref, g_ref, quarter, half):
     start = pl.multiple_of(quarter * QUARTER + half * HALF, HALF)
-    first, second = a_refs
-    return jnp.dot(
-        first[pl.ds(start, HALF), :], g_ref[0:N_FIRST, :], preferred_element_type=F32
-    ) + jnp.dot(second[pl.ds(start, HALF), :], g_ref[N_FIRST:, :], preferred_element_type=F32)
-
-
-def far_kernel(place_ref, *refs):
-    rows_refs, (basis_ref, first, second, g_ref, up_ref, down_ref) = refs[:N_Z], refs[N_Z:]
+    return jnp.dot(a_ref[pl.ds(start, HALF), :], g_ref[...], preferred_element_type=F32)
+
+
+def rotate_grads_kernel(*refs):
+    rows_refs, (basis_ref, g_ref) = refs[:-2], refs[-2:]
     for k, rows_ref in enumerate(rows_refs):
         rotated = jnp.dot(rows_ref[...], basis_ref[0], preferred_element_type=F32)
-        g_ref[k * TOK : (k + 1) * TOK, :] = (rotated * rotated).astype(BF)
-    encode(block_sum((first, second), g_ref, place_ref[0], 0), up_ref)
-    encode(block_sum((first, second), g_ref, place_ref[0], 1), down_ref)
-
-
-def far_blocks(place, rows, basis_out, a_sq):
+        squared = (rotated * rotated).astype(BF)
+        for i in range(N_YC):
+            start = i * TOK + k * CAP
+            g_ref[start : start + CAP, :] = squared[i * CAP : (i + 1) * CAP, :]
+
+
+def rotate_grads(rows, basis_out):
+    return pl.pallas_call(
+        rotate_grads_kernel,
+        out_shape=jax.ShapeDtypeStruct((ROWS, FF), BF),
+        in_specs=[IN_VMEM] * (N_Z + 1),
+        out_specs=IN_VMEM,
+        compiler_params=params(8),
+        cost_estimate=pl.CostEstimate(
+            flops=2 * ROWS * FF * FF, bytes_accessed=4 << 20, transcendentals=0
+        ),
+    )(*rows, basis_out)
+
+
+def far_kernel(place_ref, a_ref, g_ref, up_ref, down_ref):
+    encode(block_sum(a_ref, g_ref, place_ref[0], 0), up_ref)
+    encode(block_sum(a_ref, g_ref, place_ref[0], 1), down_ref)
+
+
+def far_blocks(place, a_sq, g_sq):
     return pl.pallas_call(
         far_kernel,
-        out_shape=(jax.ShapeDtypeStruct((ROWS, FF), BF), CODE, CODE),
-        in_specs=[IN_SMEM] + [IN_VMEM] * (N_Z + 3),
-        out_specs=[IN_VMEM] * 3,
-        compiler_params=params(8),
-        cost_estimate=pl.CostEstimate(
-            flops=2 * ROWS * FF * (FF + QUARTER), bytes_accessed=12 << 20, transcendentals=0
-        ),
-    )(place, *rows, basis_out, *a_sq)
-
-
-def near_kernel(place_ref, first, second, g_ref, up_ref, down_ref):
-    encode(block_sum((first, second), g_ref, place_ref[1], 1), up_ref)
-    encode(block_sum((first, second), g_ref, place_ref[2], 0), down_ref)
+        out_shape=(CODE, CODE),
+        in_specs=[IN_SMEM] + [IN_VMEM] * 2,
+        out_specs=[IN_VMEM] * 2,
+        compiler_params=params(4),
+        cost_estimate=pl.CostEstimate(
+            flops=2 * ROWS * FF * QUARTER, bytes_accessed=4 << 20, transcendentals=0
+        ),
+    )(place, a_sq, g_sq)
+
+
+def near_kernel(place_ref, a_ref, g_ref, up_ref, down_ref):
+    encode(block_sum(a_ref, g_ref, place_ref[1], 1), up_ref)
+    encode(block_sum(a_ref, g_ref, place_ref[2], 0), down_ref)
 
 
 def near_blocks(place, a_sq, g_sq):
     return pl.pallas_call(
         near_kernel,
         out_shape=(CODE, CODE),
-        in_specs=[IN_SMEM] + [IN_VMEM] * 3,
+        in_specs=[IN_SMEM] + [IN_VMEM] * 2,
         out_specs=[IN_VMEM] * 2,
         compiler_params=params(4),
         cost_estimate=pl.CostEstimate(
             flops=2 * ROWS * FF * QUARTER, bytes_accessed=4 << 20, transcendentals=0
         ),
-    )(place, *a_sq, g_sq)
-
-
-def rest_kernel(place_ref, first, second, g_ref, up_ref, down_ref, own_ref):
-    a_refs = (first, second)
-    up_ref[...] = block_sum(a_refs, g_ref, place_ref[1], 0)
-    down_ref[...] = block_sum(a_refs, g_ref, place_ref[2], 1)
-    own_ref[0:HALF, :] = block_sum(a_refs, g_ref, place_ref[3], 0)
-    own_ref[HALF:QUARTER, :] = block_sum(a_refs, g_ref, place_ref[3], 1)
+    )(place, a_sq, g_sq)
+
+
+def rest_kernel(place_ref, a_ref, g_ref, up_ref, down_ref, own_ref):
+    up_ref[...] = block_sum(a_ref, g_ref, place_ref[1], 0)
+    down_ref[...] = block_sum(a_ref, g_ref, place_ref[2], 1)
+    own_ref[0:HALF, :] = block_sum(a_ref, g_ref, place_ref[3], 0)
+    own_ref[HALF:QUARTER, :] = block_sum(a_ref, g_ref, place_ref[3], 1)
 
 
 def rest_blocks(place, a_sq, g_sq):
     return pl.pallas_call(
         rest_kernel,
         out_shape=(BLOCK, BLOCK, jax.ShapeDtypeStruct((QUARTER, FF), F32)),
-        in_specs=[IN_SMEM] + [IN_VMEM] * 3,
+        in_specs=[IN_SMEM] + [IN_VMEM] * 2,
         out_specs=[IN_VMEM] * 3,
         compiler_params=params(4),
         cost_estimate=pl.CostEstimate(
             flops=4 * ROWS * FF * QUARTER, bytes_accessed=8 << 20, transcendentals=0
         ),
-    )(place, *a_sq, g_sq)
+    )(place, a_sq, g_sq)
 
 
 def pass_on_kernel(up_ref, down_ref, got_up_ref, got_down_ref, out_up_ref, out_down_ref):
@@ -342,15 +339,13 @@
     by_z = regroup(grads_in, [*ring[3], *ring[5]])
     rows_out = [by_z[k] if k == 0 else shift(by_z[k], "z", k) for k in ORDER]
 
-    a_sq, gates = [], [grads_in, *ring[3], *ring[5]]
-    for senders in (FIRST, SECOND):
-        packed = pack_tokens(
-            here, [ring[k][0] for k in senders], [ring[k][1] for k in senders], gates
-        )
-        gates = [packed] + [rows_out[ORDER.index(k)] for k in (3, 5, 2, 6)]
-        a_sq.append(rotate_inputs(to_owners(packed), basis_in, a_sq))
-
-    g_sq, far_up, far_down = far_blocks(place, rows_out, basis_out, a_sq)
+    rows_in = to_owners(
+        pack_tokens(here, [ring[k][0] for k in ORDER], [ring[k][1] for k in ORDER], [grads_in])
+    )
+    g_sq = rotate_grads(rows_out, basis_out)
+    a_sq = rotate_inputs(rows_in, basis_in, [g_sq])
+
+    far_up, far_down = far_blocks(place, a_sq, g_sq)
     got_far_up, got_far_down = shift(far_up, "x", 1), shift(far_down, "x", -1)
     near_up, near_down = near_blocks(place, a_sq, g_sq)
     got_near_up, got_near_down = shift(near_up, "x", 1), shift(near_down, "x", -1)

time: 175 us -> 176 us (level)
  waiting for transfers between devices: 62.5 us -> 77.9 us
  starting transfers between devices: 61.1 us -> 52 us
  Pallas kernels: 44.4 us -> 39.6 us
    ppermute x27, waiting for transfers between devices: 57.2 us -> 71.8 us  [shift(): return lax.ppermute(value, axis, [(i, (i + by) % n) for i in range(n)])]
    ppermute x27, starting transfers between devices: 47.6 us -> 43 us  [shift(): return lax.ppermute(value, axis, [(i, (i + by) % n) for i in range(n)])]
    all_to_all x3 -> x2, starting transfers between devices: 13.5 us -> 9.01 us  [to_owners(): lax.all_to_all(value, ('y', 'c'), split_axis=0, concat_axis=0, tiled=True)]
    pallas_call x3, Pallas kernels: 19.6 us -> 17 us  [the longest x1 13.6 us: rotate_inputs(): pl.pallas_call(rotate_kernel, out_shape=jax.ShapeDtypeStruct((D, ROWS), B...]
    pallas_call x2 -> x1, Pallas kernels: 8.14 us -> 6.48 us  [pack_tokens(): pl.pallas_call(functools.partial(pack_tokens_kernel, n), out_shape=jax.Sh...]
    all_to_all x3 -> x2, waiting for transfers between devices: 5.29 us -> 6.04 us  [to_owners(): lax.all_to_all(value, ('y', 'c'), split_axis=0, concat_axis=0, tiled=True)]
    unnamed x56 -> x38, local copies, waits for them, and re-layouts: 5.69 us -> 6.23 us
  transfers between devices with their start and end apart: 30 -> 29, of which waited for: 16 -> 19; matrix products, arithmetic and copies ran while one was open for 0% -> 0% of each run, Pallas kernels for 17% -> 6%
where the time goes in v3:
time: 176 us
  waiting for transfers between devices  77.9 us (44%)
  starting transfers between devices  52 us (30%)
  Pallas kernels  39.6 us (22%)
  local copies, waits for them, and re-layouts  6.23 us (4%)
    ppermute x27, waiting for transfers between devices, shift(): return lax.ppermute(value, axis, [(i, (i + by) % n) for i in range(n)])  71.8 us
    ppermute x27, starting transfers between devices, shift(): return lax.ppermute(value, axis, [(i, (i + by) % n) for i in range(n)])  43 us
    pallas_call x1, Pallas kernels, rotate_inputs(): pl.pallas_call(rotate_kernel, out_shape=jax.ShapeDtypeStruct((D, ROWS), B...  13.6 us
    all_to_all x2, starting transfers between devices, to_owners(): lax.all_to_all(value, ('y', 'c'), split_axis=0, concat_axis=0, tiled=True)  9.01 us
    pallas_call x1, Pallas kernels, pack_tokens(): pl.pallas_call(functools.partial(pack_tokens_kernel, n), out_shape=jax.Sh...  6.48 us
    unnamed x38, local copies, waits for them, and re-layouts  6.23 us
    all_to_all x2, waiting for transfers between devices, to_owners(): lax.all_to_all(value, ('y', 'c'), split_axis=0, concat_axis=0, tiled=True)  6.04 us
    pallas_call x1, Pallas kernels, pack_grads(): pl.pallas_call(pack_grads_kernel, out_shape=jax.ShapeDtypeStruct((N_YC, N...  4.8 us
  transfers between devices with their start and end apart: 29, of which 19 were waited for; matrix products, arithmetic and copies ran while one was open for 0% of the time, Pallas kernels for 6%

profile of v3, /device:TPU:6, one launch (start us, length us, event | category | flops | bytes accessed | tf_op | source)
XLA Modules:
  0.0 176.0 jit_solution(14985022084603929973)
XLA Ops:
  0.0 4.8 %shard_map.56 = bf16[8,128,768]{2,1,0:T(8,128)(2,1)} custom-call(s32[1]{0:T(128)} %bitcast.4.here_ref, s32[8,128]{1,0:T(8,128)} %bitcast.8, bf16[1024,768]{1,0:T(8,128)(2,1)} %bitcast.10), custom_call_target="tpu_custom_call" | custom-call | flops 1610612736 | bytes 3145728 | tf_op jit(solution)/shard_map/pallas_call | solution.py:86
  4.8 4.5 %all-to-all-start = ((bf16[8,128,768]{2,1,0:T(8,128)(2,1)}), bf16[8,128,768]{2,1,0:T(8,128)(2,1)S(1)}, u32[]{:S(2)}, u32[]{:S(2)}) async-start(bf16[8,128,768]{2,1,0:T(8,128)(2,1)} %shard_map.56), calls=%async_computation | async-start | bytes 3145728 | tf_op jit(solution)/shard_map/all_to_all | solution.py:318
  9.3 1.9 %shard_map.55 = (bf16[136,1024]{1,0:T(8,128)(2,1)}, bf16[128,1024]{1,0:T(8,128)(2,1)}) custom-call(bf16[128,2048]{1,0:T(8,128)(2,1)} %tokens_ref.1, s32[8,128]{1,0:T(8,128)} %bitcast.9), custom_call_target="tpu_custom_call" | custom-call | tf_op jit(solution)/shard_map/pallas_call | solution.py:57
  11.1 1.9 %collective-permute-start = (bf16[136,1024]{1,0:T(8,128)(2,1)}, bf16[136,1024]{1,0:T(8,128)(2,1)S(1)}, u32[]{:S(2)}, u32[]{:S(2)}) collective-permute-start(bf16[136,1024]{1,0:T(8,128)(2,1)} %get-tuple-element.24.refs_0_), channel_id=1, source_target_pairs={{0,8},{8,16},{16,24},{24,32},{32,40},{40,48},{48,56},{56,0},{1,9},... | collective-permute-start | bytes 835592 | tf_op jit(solution)/shard_map/ppermute | solution.py:314
  13.1 3.9 %collective-permute-start.8 = (bf16[128,1024]{1,0:T(8,128)(2,1)}, bf16[128,1024]{1,0:T(8,128)(2,1)S(1)}, u32[]{:S(2)}, u32[]{:S(2)}) collective-permute-start(bf16[128,1024]{1,0:T(8,128)(2,1)} %get-tuple-element.25.refs_8_), channel_id=1, source_target_pairs={{0,56},{8,0},{16,8},{24,16},{32,24},{40,32},{48,40},{56,48},{1,57}... | collective-permute-start | bytes 786440 | tf_op jit(solution)/shard_map/ppermute | solution.py:314
  17.0 2.0 %collective-permute-start.1 = (bf16[136,1024]{1,0:T(8,128)(2,1)}, bf16[136,1024]{1,0:T(8,128)(2,1)S(1)}, u32[]{:S(2)}, u32[]{:S(2)}) collective-permute-start(bf16[136,1024]{1,0:T(8,128)(2,1)} %get-tuple-element.24.refs_0_), channel_id=1, source_target_pairs={{0,56},{8,0},{16,8},{24,16},{32,24},{40,32},{48,40},{56,48},{1,57}... | collective-permute-start | bytes 835592 | tf_op jit(solution)/shard_map/ppermute | solution.py:314
  19.0 5.5 %collective-permute-done.refs_1_ = bf16[136,1024]{1,0:T(8,128)(2,1)S(1)} collective-permute-done((bf16[136,1024]{1,0:T(8,128)(2,1)}, bf16[136,1024]{1,0:T(8,128)(2,1)S(1)}, u32[]{:S(2)}, u32[]{:S(2)}) %collective-permute-start) | collective-permute-done | bytes 278560 | tf_op jit(solution)/shard_map/ppermute | solution.py:314
  24.6 3.3 %collective-permute-start.10 = (bf16[128,1024]{1,0:T(8,128)(2,1)S(1)}, bf16[128,1024]{1,0:T(8,128)(2,1)S(1)}, u32[]{:S(2)}, u32[]{:S(2)}) collective-permute-start(bf16[128,1024]{1,0:T(8,128)(2,1)S(1)} %collective-permute-done.8.refs_10_), channel_id=1, source_target_pairs={{0,56},{8,0},{16,8},{24,16},{32,24},{40,32},{48,40},{56,48},{1,57}... | collective-permute-start | bytes 786440 | tf_op jit(solution)/shard_map/ppermute | solution.py:314
  27.9 2.0 %collective-permute-done.1.refs_2_ = bf16[136,1024]{1,0:T(8,128)(2,1)S(1)} collective-permute-done((bf16[136,1024]{1,0:T(8,128)(2,1)}, bf16[136,1024]{1,0:T(8,128)(2,1)S(1)}, u32[]{:S(2)}, u32[]{:S(2)}) %collective-permute-start.1) | collective-permute-done | bytes 278560 | tf_op jit(solution)/shard_map/ppermute | solution.py:314
  29.9 3.6 %collective-permute-start.3 = (bf16[136,1024]{1,0:T(8,128)(2,1)S(1)}, bf16[136,1024]{1,0:T(8,128)(2,1)S(1)}, u32[]{:S(2)}, u32[]{:S(2)}) collective-permute-start(bf16[136,1024]{1,0:T(8,128)(2,1)S(1)} %collective-permute-done.1.refs_2_), channel_id=1, source_target_pairs={{0,56},{8,0},{16,8},{24,16},{32,24},{40,32},{48,40},{56,48},{1,57}... | collective-permute-start | bytes 835592 | tf_op jit(solution)/shard_map/ppermute | solution.py:314
  33.5 1.8 %collective-permute-done.2.refs_3_ = bf16[136,1024]{1,0:T(8,128)(2,1)S(1)} collective-permute-done((bf16[136,1024]{1,0:T(8,128)(2,1)S(1)}, bf16[136,1024]{1,0:T(8,128)(2,1)S(1)}, u32[]{:S(2)}, u32[]{:S(2)}) %collective-permute-start.2) | collective-permute-done | bytes 278560 | tf_op jit(solution)/shard_map/ppermute | solution.py:314
  35.3 5.6 %collective-permute-done.7.refs_9_ = bf16[128,1024]{1,0:T(8,128)(2,1)S(1)} collective-permute-done((bf16[128,1024]{1,0:T(8,128)(2,1)}, bf16[128,1024]{1,0:T(8,128)(2,1)S(1)}, u32[]{:S(2)}, u32[]{:S(2)}) %collective-permute-start.7) | collective-permute-done | bytes 262176 | tf_op jit(solution)/shard_map/ppermute | solution.py:314
  40.9 3.2 %collective-permute-start.12 = (bf16[128,1024]{1,0:T(8,128)(2,1)S(1)}, bf16[128,1024]{1,0:T(8,128)(2,1)S(1)}, u32[]{:S(2)}, u32[]{:S(2)}) collective-permute-start(bf16[128,1024]{1,0:T(8,128)(2,1)S(1)} %collective-permute-done.10.refs_12_), channel_id=1, source_target_pairs={{0,56},{8,0},{16,8},{24,16},{32,24},{40,32},{48,40},{56,48},{1,57}... | collective-permute-start | bytes 786440 | tf_op jit(solution)/shard_map/ppermute | solution.py:314
  44.7 2.2 %collective-permute-done.4.refs_5_.refs_1_ = bf16[136,1024]{1,0:T(8,128)(2,1)S(1)} collective-permute-done((bf16[136,1024]{1,0:T(8,128)(2,1)S(1)}, bf16[136,1024]{1,0:T(8,128)(2,1)S(1)}, u32[]{:S(2)}, u32[]{:S(2)}) %collective-permute-start.4) | collective-permute-done | bytes 278560 | tf_op jit(solution)/shard_map/ppermute | solution.py:314
  46.9 5.6 %collective-permute-done.9.refs_11_ = bf16[128,1024]{1,0:T(8,128)(2,1)S(1)} collective-permute-done((bf16[128,1024]{1,0:T(8,128)(2,1)S(1)}, bf16[128,1024]{1,0:T(8,128)(2,1)S(1)}, u32[]{:S(2)}, u32[]{:S(2)}) %collective-permute-start.9) | collective-permute-done | bytes 262176 | tf_op jit(solution)/shard_map/ppermute | solution.py:314
  52.5 3.2 %collective-permute-start.13 = (bf16[128,1024]{1,0:T(8,128)(2,1)S(1)}, bf16[128,1024]{1,0:T(8,128)(2,1)S(1)}, u32[]{:S(2)}, u32[]{:S(2)}) collective-permute-start(bf16[128,1024]{1,0:T(8,128)(2,1)S(1)} %collective-permute-done.12.refs_14_.refs_4_), channel_id=1, source_target_pairs={{0,56},{8,0},{16,8},{24,16},{32,24},{40,32},{48,40},{56,48},{1,57}... | collective-permute-start | bytes 786440 | tf_op jit(solution)/shard_map/ppermute | solution.py:314
  55.7 7.3 %collective-permute-done.11.refs_13_.refs_2_ = bf16[128,1024]{1,0:T(8,128)(2,1)S(1)} collective-permute-done((bf16[128,1024]{1,0:T(8,128)(2,1)S(1)}, bf16[128,1024]{1,0:T(8,128)(2,1)S(1)}, u32[]{:S(2)}, u32[]{:S(2)}) %collective-permute-start.11) | collective-permute-done | bytes 262176 | tf_op jit(solution)/shard_map/ppermute | solution.py:314
  63.9 1.1 copy-done.5
  65.1 6.5 %shard_map.57 = bf16[8,128,2048]{2,1,0:T(8,128)(2,1)} custom-call(s32[1]{0:T(128)} %bitcast.4.here_ref, bf16[136,1024]{1,0:T(8,128)(2,1)} %get-tuple-element.24.refs_0_, bf16[136,1024]{1,0:T(8,128)(2,1)} %copy-done.10, bf16[136,1024]{1,0:T(8,128)(2,1)} %copy-done.11, bf16[136,1024]{1,0:T(8,128)(2,1)} %copy-done.12, bf16[136,1024]{1,0:T(8,128)(2,1)} %copy-done.13, ...), custom_call_target="tpu_custom_call" | custom-call | flops 536870912 | bytes 8388608 | tf_op jit(solution)/shard_map/pallas_call | solution.py:135
  71.5 4.5 %all-to-all-start.1 = ((bf16[8,128,2048]{2,1,0:T(8,128)(2,1)}), bf16[8,128,2048]{2,1,0:T(8,128)(2,1)}, u32[]{:S(2)}, u32[]{:S(2)}) async-start(bf16[8,128,2048]{2,1,0:T(8,128)(2,1)} %shard_map.57), calls=%async_computation.1 | async-start | bytes 8388608 | tf_op jit(solution)/shard_map/all_to_all | solution.py:318
  76.1 2.7 %shard_map.58 = (bf16[128,768]{1,0:T(8,128)(2,1)}, bf16[128,768]{1,0:T(8,128)(2,1)}, bf16[128,768]{1,0:T(8,128)(2,1)}, bf16[128,768]{1,0:T(8,128)(2,1)}, bf16[12...) custom-call(bf16[8,128,768]{2,1,0:T(8,128)(2,1)} %copy-done.5, ...), custom_call_target="tpu_custom_call" | custom-call | tf_op jit(solution)/shard_map/pallas_call | solution.py:106
  78.8 3.2 %collective-permute-start.15 = (bf16[128,768]{1,0:T(8,128)(2,1)}, bf16[128,768]{1,0:T(8,128)(2,1)S(1)}, u32[]{:S(2)}, u32[]{:S(2)}) collective-permute-start(bf16[128,768]{1,0:T(8,128)(2,1)} %get-tuple-element.28), channel_id=1, source_target_pairs={{0,56},{8,0},{16,8},{24,16},{32,24},{40,32},{48,40},{56,48},{1,57}... | collective-permute-start | bytes 589832 | tf_op jit(solution)/shard_map/ppermute | solution.py:314
  82.0 4.1 %collective-permute-start.17 = (bf16[128,768]{1,0:T(8,128)(2,1)}, bf16[128,768]{1,0:T(8,128)(2,1)S(1)}, u32[]{:S(2)}, u32[]{:S(2)}) collective-permute-start(bf16[128,768]{1,0:T(8,128)(2,1)} %get-tuple-element.30), channel_id=1, source_target_pairs={{0,48},{8,56},{16,0},{24,8},{32,16},{40,24},{48,32},{56,40},{1,49}... | collective-permute-start | bytes 589832 | tf_op jit(solution)/shard_map/ppermute | solution.py:314
  86.4 1.8 %collective-permute-done.14.refs_1_ = bf16[128,768]{1,0:T(8,128)(2,1)S(1)} collective-permute-done((bf16[128,768]{1,0:T(8,128)(2,1)}, bf16[128,768]{1,0:T(8,128)(2,1)S(1)}, u32[]{:S(2)}, u32[]{:S(2)}) %collective-permute-start.14) | collective-permute-done | bytes 196640 | tf_op jit(solution)/shard_map/ppermute | solution.py:314
  88.1 3.1 %collective-permute-start.19 = (bf16[128,768]{1,0:T(8,128)(2,1)}, bf16[128,768]{1,0:T(8,128)(2,1)S(1)}, u32[]{:S(2)}, u32[]{:S(2)}) collective-permute-start(bf16[128,768]{1,0:T(8,128)(2,1)} %get-tuple-element.32), channel_id=1, source_target_pairs={{0,40},{8,48},{16,56},{24,0},{32,8},{40,16},{48,24},{56,32},{1,41}... | collective-permute-start | bytes 589832 | tf_op jit(solution)/shard_map/ppermute | solution.py:314
  91.2 1.3 collective-permute-done.15.refs_2_
  92.5 2.8 %collective-permute-start.20 = (bf16[128,768]{1,0:T(8,128)(2,1)}, bf16[128,768]{1,0:T(8,128)(2,1)S(1)}, u32[]{:S(2)}, u32[]{:S(2)}) collective-permute-start(bf16[128,768]{1,0:T(8,128)(2,1)} %get-tuple-element.33), channel_id=1, source_target_pairs={{0,32},{8,40},{16,48},{24,56},{32,0},{40,8},{48,16},{56,24},{1,33}... | collective-permute-start | bytes 589832 | tf_op jit(solution)/shard_map/ppermute | solution.py:314
  95.4 2.9 %collective-permute-done.16.refs_3_ = bf16[128,768]{1,0:T(8,128)(2,1)S(1)} collective-permute-done((bf16[128,768]{1,0:T(8,128)(2,1)}, bf16[128,768]{1,0:T(8,128)(2,1)S(1)}, u32[]{:S(2)}, u32[]{:S(2)}) %collective-permute-start.16) | collective-permute-done | bytes 196640 | tf_op jit(solution)/shard_map/ppermute | solution.py:314
  98.3 1.1 collective-permute-done.17.refs_4_
  99.3 9.8 %collective-permute-done.18.refs_5_ = bf16[128,768]{1,0:T(8,128)(2,1)S(1)} collective-permute-done((bf16[128,768]{1,0:T(8,128)(2,1)}, bf16[128,768]{1,0:T(8,128)(2,1)S(1)}, u32[]{:S(2)}, u32[]{:S(2)}) %collective-permute-start.18) | collective-permute-done | bytes 196640 | tf_op jit(solution)/shard_map/ppermute | solution.py:314
  109.1 7.1 %collective-permute-done.19.refs_6_ = bf16[128,768]{1,0:T(8,128)(2,1)S(1)} collective-permute-done((bf16[128,768]{1,0:T(8,128)(2,1)}, bf16[128,768]{1,0:T(8,128)(2,1)S(1)}, u32[]{:S(2)}, u32[]{:S(2)}) %collective-permute-start.19) | collective-permute-done | bytes 196640 | tf_op jit(solution)/shard_map/ppermute | solution.py:314
  117.2 1.4 shard_map.59.refs_0_.g_ref
  118.6 1.1 copy-done.1
  119.7 6.0 %all-to-all-done.1.rows_ref = bf16[8,128,2048]{2,1,0:T(8,128)(2,1)} async-done(((bf16[8,128,2048]{2,1,0:T(8,128)(2,1)}), bf16[8,128,2048]{2,1,0:T(8,128)(2,1)}, u32[]{:S(2)}, u32[]{:S(2)}) %all-to-all-start.1) | async-done | bytes 4194336 | tf_op jit(solution)/shard_map/all_to_all | solution.py:318
  125.8 13.6 %shard_map.60.a_ref = bf16[2048,1024]{1,0:T(8,128)(2,1)} custom-call(bf16[8,128,2048]{2,1,0:T(8,128)(2,1)} %all-to-all-done.1.rows_ref, bf16[1,2048,2048]{2,1,0:T(8,128)(2,1)} %basis_ref.1, bf16[1024,768]{1,0:T(8,128)(2,1)} %copy-done.1), custom_call_target="tpu_custom_call" | custom-call | flops 8589934592 | bytes 16777216 | tf_op jit(solution)/shard_map/pallas_call | solution.py:157
  139.4 2.2 %copy-done = bf16[2048,1024]{1,0:T(8,128)(2,1)S(1)} copy-done((bf16[2048,1024]{1,0:T(8,128)(2,1)S(1)}, bf16[2048,1024]{1,0:T(8,128)(2,1)}, u32[]{:S(2)}) %copy-start) | copy-done | bytes 4194328
  141.6 1.9 %shard_map.62 = (s16[272,768]{1,0:T(8,128)(2,1)S(1)}, s16[272,768]{1,0:T(8,128)(2,1)S(1)}) custom-call(s32[4]{0:T(128)S(1)} %pad_add_fusion.place_ref, bf16[2048,1024]{1,0:T(8,128)(2,1)S(1)} %copy-done, bf16[1024,768]{1,0:T(8,128)(2,1)S(1)} %copy-done.2), custom_call_target="tpu_custom_call" | custom-call | flops 805306368 | bytes 4194304 | tf_op jit(solution)/shard_map/pallas_call | solution.py:224
  144.3 1.5 collective-permute-start.22
  145.9 1.9 %shard_map.64 = (s16[272,768]{1,0:T(8,128)(2,1)S(1)}, s16[272,768]{1,0:T(8,128)(2,1)S(1)}) custom-call(s32[4]{0:T(128)S(1)} %pad_add_fusion.place_ref, bf16[2048,1024]{1,0:T(8,128)(2,1)S(1)} %copy-done, bf16[1024,768]{1,0:T(8,128)(2,1)S(1)} %copy-done.2), custom_call_target="tpu_custom_call" | custom-call | flops 805306368 | bytes 4194304 | tf_op jit(solution)/shard_map/pallas_call | solution.py:242
  148.7 2.4 %collective-permute-start.25 = (s16[272,768]{1,0:T(8,128)(2,1)S(1)}, s16[272,768]{1,0:T(8,128)(2,1)S(1)}, u32[]{:S(2)}, u32[]{:S(2)}) collective-permute-start(s16[272,768]{1,0:T(8,128)(2,1)S(1)} %get-tuple-element.41), channel_id=1, source_target_pairs={{0,64},{64,128},{128,192},{192,0},{1,65},{65,129},{129,193},{193,1... | collective-permute-start | bytes 1253384 | tf_op jit(solution)/shard_map/ppermute | solution.py:314
  151.1 2.3 %shard_map.61 = (f32[256,768]{1,0:T(8,128)S(1)}, f32[256,768]{1,0:T(8,128)S(1)}, f32[512,768]{1,0:T(8,128)S(1)}) custom-call(s32[4]{0:T(128)S(1)} %pad_add_fusion.place_ref, bf16[2048,1024]{1,0:T(8,128)(2,1)S(1)} %copy-done, bf16[1024,768]{1,0:T(8,128)(2,1)S(1)} %copy-done.2), custom_call_target="tpu_custom_call" | custom-call | flops 1610612736 | bytes 8388608 | tf_op jit(solution)/shard_map/pallas_call | solution.py:262
  153.5 2.9 %collective-permute-done.21.got_up_ref = s16[272,768]{1,0:T(8,128)(2,1)S(1)} collective-permute-done((s16[272,768]{1,0:T(8,128)(2,1)S(1)}, s16[272,768]{1,0:T(8,128)(2,1)S(1)}, u32[]{:S(2)}, u32[]{:S(2)}) %collective-permute-start.21) | collective-permute-done | bytes 417824 | tf_op jit(solution)/shard_map/ppermute | solution.py:314
  156.4 1.7 collective-permute-done.22.got_down_ref
  159.3 1.7 collective-permute-start.26
  161.1 6.0 %collective-permute-done.24.top_b_ref = s16[272,768]{1,0:T(8,128)(2,1)S(1)} collective-permute-done((s16[272,768]{1,0:T(8,128)(2,1)S(1)}, s16[272,768]{1,0:T(8,128)(2,1)S(1)}, u32[]{:S(2)}, u32[]{:S(2)}) %collective-permute-start.24) | collective-permute-done | bytes 417824 | tf_op jit(solution)/shard_map/ppermute | solution.py:314
  167.1 5.9 %collective-permute-done.23.top_a_ref = s16[272,768]{1,0:T(8,128)(2,1)S(1)} collective-permute-done((s16[272,768]{1,0:T(8,128)(2,1)S(1)}, s16[272,768]{1,0:T(8,128)(2,1)S(1)}, u32[]{:S(2)}, u32[]{:S(2)}) %collective-permute-start.23) | collective-permute-done | bytes 417824 | tf_op jit(solution)/shard_map/ppermute | solution.py:314
  172.9 1.4 collective-permute-done.26.bottom_b_ref
  174.3 1.7 shard_map.65
  (60 shorter events, 5.6 us)
Async XLA Ops:
  4.8 59.1 %all-to-all-start = ((bf16[8,128,768]{2,1,0:T(8,128)(2,1)}), bf16[8,128,768]{2,1,0:T(8,128)(2,1)S(1)}, u32[]{:S(2)}, u32[]{:S(2)}) async-start(bf16[8,128,768]{2,1,0:T(8,128)(2,1)} %shard_map.56), calls=%async_computation | async-start | bytes 3145728 | tf_op jit(solution)/shard_map/all_to_all | solution.py:318
  11.1 13.4 %collective-permute-start = (bf16[136,1024]{1,0:T(8,128)(2,1)}, bf16[136,1024]{1,0:T(8,128)(2,1)S(1)}, u32[]{:S(2)}, u32[]{:S(2)}) collective-permute-start(bf16[136,1024]{1,0:T(8,128)(2,1)} %get-tuple-element.24.refs_0_), channel_id=1, source_target_pairs={{0,8},{8,16},{16,24},{24,32},{32,40},{40,48},{48,56},{56,0},{1,9},... | collective-permute-start | bytes 835592 | tf_op jit(solution)/shard_map/ppermute | solution.py:314
  13.1 11.5 %collective-permute-start.8 = (bf16[128,1024]{1,0:T(8,128)(2,1)}, bf16[128,1024]{1,0:T(8,128)(2,1)S(1)}, u32[]{:S(2)}, u32[]{:S(2)}) collective-permute-start(bf16[128,1024]{1,0:T(8,128)(2,1)} %get-tuple-element.25.refs_8_), channel_id=1, source_target_pairs={{0,56},{8,0},{16,8},{24,16},{32,24},{40,32},{48,40},{56,48},{1,57}... | collective-permute-start | bytes 786440 | tf_op jit(solution)/shard_map/ppermute | solution.py:314
  17.0 12.9 %collective-permute-start.1 = (bf16[136,1024]{1,0:T(8,128)(2,1)}, bf16[136,1024]{1,0:T(8,128)(2,1)S(1)}, u32[]{:S(2)}, u32[]{:S(2)}) collective-permute-start(bf16[136,1024]{1,0:T(8,128)(2,1)} %get-tuple-element.24.refs_0_), channel_id=1, source_target_pairs={{0,56},{8,0},{16,8},{24,16},{32,24},{40,32},{48,40},{56,48},{1,57}... | collective-permute-start | bytes 835592 | tf_op jit(solution)/shard_map/ppermute | solution.py:314
  24.5 39.3 %copy-start.10 = (bf16[136,1024]{1,0:T(8,128)(2,1)}, bf16[136,1024]{1,0:T(8,128)(2,1)S(1)}, u32[]{:S(2)}) copy-start(bf16[136,1024]{1,0:T(8,128)(2,1)S(1)} %collective-permute-done.refs_1_) | copy-start | bytes 835588
  24.5 10.7 %collective-permute-start.2 = (bf16[136,1024]{1,0:T(8,128)(2,1)S(1)}, bf16[136,1024]{1,0:T(8,128)(2,1)S(1)}, u32[]{:S(2)}, u32[]{:S(2)}) collective-permute-start(bf16[136,1024]{1,0:T(8,128)(2,1)S(1)} %collective-permute-done.refs_1_), channel_id=1, source_target_pairs={{0,8},{8,16},{16,24},{24,32},{32,40},{40,48},{48,56},{56,0},{1,9},... | collective-permute-start | bytes 835592 | tf_op jit(solution)/shard_map/ppermute | solution.py:314
  24.5 16.4 %collective-permute-start.7 = (bf16[128,1024]{1,0:T(8,128)(2,1)}, bf16[128,1024]{1,0:T(8,128)(2,1)S(1)}, u32[]{:S(2)}, u32[]{:S(2)}) collective-permute-start(bf16[128,1024]{1,0:T(8,128)(2,1)} %get-tuple-element.25.refs_8_), channel_id=1, source_target_pairs={{0,8},{8,16},{16,24},{24,32},{32,40},{40,48},{48,56},{56,0},{1,9},... | collective-permute-start | bytes 786440 | tf_op jit(solution)/shard_map/ppermute | solution.py:314
  24.5 19.6 %copy-start.14 = (bf16[128,1024]{1,0:T(8,128)(2,1)}, bf16[128,1024]{1,0:T(8,128)(2,1)S(1)}, u32[]{:S(2)}) copy-start(bf16[128,1024]{1,0:T(8,128)(2,1)S(1)} %collective-permute-done.8.refs_10_) | copy-start | bytes 786436
  24.6 16.3 %collective-permute-start.10 = (bf16[128,1024]{1,0:T(8,128)(2,1)S(1)}, bf16[128,1024]{1,0:T(8,128)(2,1)S(1)}, u32[]{:S(2)}, u32[]{:S(2)}) collective-permute-start(bf16[128,1024]{1,0:T(8,128)(2,1)S(1)} %collective-permute-done.8.refs_10_), channel_id=1, source_target_pairs={{0,56},{8,0},{16,8},{24,16},{32,24},{40,32},{48,40},{56,48},{1,57}... | collective-permute-start | bytes 786440 | tf_op jit(solution)/shard_map/ppermute | solution.py:314
  29.9 34.0 %copy-start.11 = (bf16[136,1024]{1,0:T(8,128)(2,1)}, bf16[136,1024]{1,0:T(8,128)(2,1)S(1)}, u32[]{:S(2)}) copy-start(bf16[136,1024]{1,0:T(8,128)(2,1)S(1)} %collective-permute-done.1.refs_2_) | copy-start | bytes 835588
  29.9 14.2 %collective-permute-start.3 = (bf16[136,1024]{1,0:T(8,128)(2,1)S(1)}, bf16[136,1024]{1,0:T(8,128)(2,1)S(1)}, u32[]{:S(2)}, u32[]{:S(2)}) collective-permute-start(bf16[136,1024]{1,0:T(8,128)(2,1)S(1)} %collective-permute-done.1.refs_2_), channel_id=1, source_target_pairs={{0,56},{8,0},{16,8},{24,16},{32,24},{40,32},{48,40},{56,48},{1,57}... | collective-permute-start | bytes 835592 | tf_op jit(solution)/shard_map/ppermute | solution.py:314
  35.3 28.6 %copy-start.12 = (bf16[136,1024]{1,0:T(8,128)(2,1)}, bf16[136,1024]{1,0:T(8,128)(2,1)S(1)}, u32[]{:S(2)}) copy-start(bf16[136,1024]{1,0:T(8,128)(2,1)S(1)} %collective-permute-done.2.refs_3_) | copy-start | bytes 835588
  35.3 11.6 %collective-permute-start.4 = (bf16[136,1024]{1,0:T(8,128)(2,1)S(1)}, bf16[136,1024]{1,0:T(8,128)(2,1)S(1)}, u32[]{:S(2)}, u32[]{:S(2)}) collective-permute-start(bf16[136,1024]{1,0:T(8,128)(2,1)S(1)} %collective-permute-done.2.refs_3_), channel_id=1, source_target_pairs={{0,8},{8,16},{16,24},{24,32},{32,40},{40,48},{48,56},{56,0},{1,9},... | collective-permute-start | bytes 835592 | tf_op jit(solution)/shard_map/ppermute | solution.py:314
  40.9 6.0 %copy-start.15 = (bf16[128,1024]{1,0:T(8,128)(2,1)}, bf16[128,1024]{1,0:T(8,128)(2,1)S(1)}, u32[]{:S(2)}) copy-start(bf16[128,1024]{1,0:T(8,128)(2,1)S(1)} %collective-permute-done.7.refs_9_) | copy-start | bytes 786436
  40.9 11.6 %collective-permute-start.9 = (bf16[128,1024]{1,0:T(8,128)(2,1)S(1)}, bf16[128,1024]{1,0:T(8,128)(2,1)S(1)}, u32[]{:S(2)}, u32[]{:S(2)}) collective-permute-start(bf16[128,1024]{1,0:T(8,128)(2,1)S(1)} %collective-permute-done.7.refs_9_), channel_id=1, source_target_pairs={{0,8},{8,16},{16,24},{24,32},{32,40},{40,48},{48,56},{56,0},{1,9},... | collective-permute-start | bytes 786440 | tf_op jit(solution)/shard_map/ppermute | solution.py:314
  40.9 22.1 %copy-start.16 = (bf16[128,1024]{1,0:T(8,128)(2,1)}, bf16[128,1024]{1,0:T(8,128)(2,1)S(1)}, u32[]{:S(2)}) copy-start(bf16[128,1024]{1,0:T(8,128)(2,1)S(1)} %collective-permute-done.10.refs_12_) | copy-start | bytes 786436
  40.9 11.6 %collective-permute-start.12 = (bf16[128,1024]{1,0:T(8,128)(2,1)S(1)}, bf16[128,1024]{1,0:T(8,128)(2,1)S(1)}, u32[]{:S(2)}, u32[]{:S(2)}) collective-permute-start(bf16[128,1024]{1,0:T(8,128)(2,1)S(1)} %collective-permute-done.10.refs_12_), channel_id=1, source_target_pairs={{0,56},{8,0},{16,8},{24,16},{32,24},{40,32},{48,40},{56,48},{1,57}... | collective-permute-start | bytes 786440 | tf_op jit(solution)/shard_map/ppermute | solution.py:314
  44.1 18.9 %copy-start.13 = (bf16[136,1024]{1,0:T(8,128)(2,1)}, bf16[136,1024]{1,0:T(8,128)(2,1)S(1)}, u32[]{:S(2)}) copy-start(bf16[136,1024]{1,0:T(8,128)(2,1)S(1)} %collective-permute-done.3.refs_4_) | copy-start | bytes 835588
  44.1 18.9 %collective-permute-start.5 = (bf16[136,1024]{1,0:T(8,128)(2,1)S(1)}, bf16[136,1024]{1,0:T(8,128)(2,1)S(1)}, u32[]{:S(2)}, u32[]{:S(2)}) collective-permute-start(bf16[136,1024]{1,0:T(8,128)(2,1)S(1)} %collective-permute-done.3.refs_4_), channel_id=1, source_target_pairs={{0,56},{8,0},{16,8},{24,16},{32,24},{40,32},{48,40},{56,48},{1,57}... | collective-permute-start | bytes 835592 | tf_op jit(solution)/shard_map/ppermute | solution.py:314
  46.9 17.0 %copy-start.6 = (bf16[136,1024]{1,0:T(8,128)(2,1)}, bf16[136,1024]{1,0:T(8,128)(2,1)S(1)}, u32[]{:S(2)}) copy-start(bf16[136,1024]{1,0:T(8,128)(2,1)S(1)} %collective-permute-done.4.refs_5_.refs_1_) | copy-start | bytes 835588
  46.9 17.0 %collective-permute-start.6 = (bf16[136,1024]{1,0:T(8,128)(2,1)S(1)}, bf16[136,1024]{1,0:T(8,128)(2,1)}, u32[]{:S(2)}, u32[]{:S(2)}) collective-permute-start(bf16[136,1024]{1,0:T(8,128)(2,1)S(1)} %collective-permute-done.4.refs_5_.refs_1_), channel_id=1, source_target_pairs={{0,8},{8,16},{16,24},{24,32},{32,40},{40,48},{48,56},{56,0},{1,9},... | collective-permute-start | bytes 835592 | tf_op jit(solution)/shard_map/ppermute | solution.py:314
  52.5 10.6 %copy-start.17 = (bf16[128,1024]{1,0:T(8,128)(2,1)}, bf16[128,1024]{1,0:T(8,128)(2,1)S(1)}, u32[]{:S(2)}) copy-start(bf16[128,1024]{1,0:T(8,128)(2,1)S(1)} %collective-permute-done.9.refs_11_) | copy-start | bytes 786436
  52.5 10.5 %collective-permute-start.11 = (bf16[128,1024]{1,0:T(8,128)(2,1)S(1)}, bf16[128,1024]{1,0:T(8,128)(2,1)S(1)}, u32[]{:S(2)}, u32[]{:S(2)}) collective-permute-start(bf16[128,1024]{1,0:T(8,128)(2,1)S(1)} %collective-permute-done.9.refs_11_), channel_id=1, source_target_pairs={{0,8},{8,16},{16,24},{24,32},{32,40},{40,48},{48,56},{56,0},{1,9},... | collective-permute-start | bytes 786440 | tf_op jit(solution)/shard_map/ppermute | solution.py:314
  52.5 11.4 %copy-start.8 = (bf16[128,1024]{1,0:T(8,128)(2,1)}, bf16[128,1024]{1,0:T(8,128)(2,1)S(1)}, u32[]{:S(2)}) copy-start(bf16[128,1024]{1,0:T(8,128)(2,1)S(1)} %collective-permute-done.12.refs_14_.refs_4_) | copy-start | bytes 786436
  52.5 10.5 %collective-permute-start.13 = (bf16[128,1024]{1,0:T(8,128)(2,1)S(1)}, bf16[128,1024]{1,0:T(8,128)(2,1)S(1)}, u32[]{:S(2)}, u32[]{:S(2)}) collective-permute-start(bf16[128,1024]{1,0:T(8,128)(2,1)S(1)} %collective-permute-done.12.refs_14_.refs_4_), channel_id=1, source_target_pairs={{0,56},{8,0},{16,8},{24,16},{32,24},{40,32},{48,40},{56,48},{1,57}... | collective-permute-start | bytes 786440 | tf_op jit(solution)/shard_map/ppermute | solution.py:314
  63.0 0.9 copy-start.9
  63.0 0.9 copy-start.7
  63.1 0.8 copy-start.18
  63.9 1.1 copy-start.5
  71.5 54.2 %all-to-all-start.1 = ((bf16[8,128,2048]{2,1,0:T(8,128)(2,1)}), bf16[8,128,2048]{2,1,0:T(8,128)(2,1)}, u32[]{:S(2)}, u32[]{:S(2)}) async-start(bf16[8,128,2048]{2,1,0:T(8,128)(2,1)} %shard_map.57), calls=%async_computation.1 | async-start | bytes 8388608 | tf_op jit(solution)/shard_map/all_to_all | solution.py:318
  76.1 40.2 %copy-start.3 = (bf16[1,768,768]{2,1,0:T(8,128)(2,1)S(1)}, bf16[1,768,768]{2,1,0:T(8,128)(2,1)}, u32[]{:S(2)}) copy-start(bf16[1,768,768]{2,1,0:T(8,128)(2,1)} %refs_8_.1) | copy-start | bytes 3538948
  78.8 9.4 %collective-permute-start.14 = (bf16[128,768]{1,0:T(8,128)(2,1)}, bf16[128,768]{1,0:T(8,128)(2,1)S(1)}, u32[]{:S(2)}, u32[]{:S(2)}) collective-permute-start(bf16[128,768]{1,0:T(8,128)(2,1)} %get-tuple-element.27), channel_id=1, source_target_pairs={{0,8},{8,16},{16,24},{24,32},{32,40},{40,48},{48,56},{56,0},{1,9},... | collective-permute-start | bytes 589832 | tf_op jit(solution)/shard_map/ppermute | solution.py:314
  78.8 13.7 %collective-permute-start.15 = (bf16[128,768]{1,0:T(8,128)(2,1)}, bf16[128,768]{1,0:T(8,128)(2,1)S(1)}, u32[]{:S(2)}, u32[]{:S(2)}) collective-permute-start(bf16[128,768]{1,0:T(8,128)(2,1)} %get-tuple-element.28), channel_id=1, source_target_pairs={{0,56},{8,0},{16,8},{24,16},{32,24},{40,32},{48,40},{56,48},{1,57}... | collective-permute-start | bytes 589832 | tf_op jit(solution)/shard_map/ppermute | solution.py:314
  82.0 16.2 %collective-permute-start.16 = (bf16[128,768]{1,0:T(8,128)(2,1)}, bf16[128,768]{1,0:T(8,128)(2,1)S(1)}, u32[]{:S(2)}, u32[]{:S(2)}) collective-permute-start(bf16[128,768]{1,0:T(8,128)(2,1)} %get-tuple-element.29), channel_id=1, source_target_pairs={{0,16},{8,24},{16,32},{24,40},{32,48},{40,56},{48,0},{56,8},{1,17}... | collective-permute-start | bytes 589832 | tf_op jit(solution)/shard_map/ppermute | solution.py:314
  82.0 17.3 %collective-permute-start.17 = (bf16[128,768]{1,0:T(8,128)(2,1)}, bf16[128,768]{1,0:T(8,128)(2,1)S(1)}, u32[]{:S(2)}, u32[]{:S(2)}) collective-permute-start(bf16[128,768]{1,0:T(8,128)(2,1)} %get-tuple-element.30), channel_id=1, source_target_pairs={{0,48},{8,56},{16,0},{24,8},{32,16},{40,24},{48,32},{56,40},{1,49}... | collective-permute-start | bytes 589832 | tf_op jit(solution)/shard_map/ppermute | solution.py:314
  86.2 22.9 %collective-permute-start.18 = (bf16[128,768]{1,0:T(8,128)(2,1)}, bf16[128,768]{1,0:T(8,128)(2,1)S(1)}, u32[]{:S(2)}, u32[]{:S(2)}) collective-permute-start(bf16[128,768]{1,0:T(8,128)(2,1)} %get-tuple-element.31), channel_id=1, source_target_pairs={{0,24},{8,32},{16,40},{24,48},{32,56},{40,0},{48,8},{56,16},{1,25}... | collective-permute-start | bytes 589832 | tf_op jit(solution)/shard_map/ppermute | solution.py:314
  88.1 28.1 %collective-permute-start.19 = (bf16[128,768]{1,0:T(8,128)(2,1)}, bf16[128,768]{1,0:T(8,128)(2,1)S(1)}, u32[]{:S(2)}, u32[]{:S(2)}) collective-permute-start(bf16[128,768]{1,0:T(8,128)(2,1)} %get-tuple-element.32), channel_id=1, source_target_pairs={{0,40},{8,48},{16,56},{24,0},{32,8},{40,16},{48,24},{56,32},{1,41}... | collective-permute-start | bytes 589832 | tf_op jit(solution)/shard_map/ppermute | solution.py:314
  92.5 23.7 %collective-permute-start.20 = (bf16[128,768]{1,0:T(8,128)(2,1)}, bf16[128,768]{1,0:T(8,128)(2,1)S(1)}, u32[]{:S(2)}, u32[]{:S(2)}) collective-permute-start(bf16[128,768]{1,0:T(8,128)(2,1)} %get-tuple-element.33), channel_id=1, source_target_pairs={{0,32},{8,40},{16,48},{24,56},{32,0},{40,8},{48,16},{56,24},{1,33}... | collective-permute-start | bytes 589832 | tf_op jit(solution)/shard_map/ppermute | solution.py:314
  116.2 0.9 copy-start.4
  118.6 1.1 copy-start.1
  125.8 13.6 %copy-start.2 = (bf16[1024,768]{1,0:T(8,128)(2,1)S(1)}, bf16[1024,768]{1,0:T(8,128)(2,1)}, u32[]{:S(2)}) copy-start(bf16[1024,768]{1,0:T(8,128)(2,1)} %copy-done.1) | copy-start | bytes 4718596
  139.4 2.2 %copy-start = (bf16[2048,1024]{1,0:T(8,128)(2,1)S(1)}, bf16[2048,1024]{1,0:T(8,128)(2,1)}, u32[]{:S(2)}) copy-start(bf16[2048,1024]{1,0:T(8,128)(2,1)} %shard_map.60.a_ref) | copy-start | bytes 12582916
  143.5 12.9 %collective-permute-start.21 = (s16[272,768]{1,0:T(8,128)(2,1)S(1)}, s16[272,768]{1,0:T(8,128)(2,1)S(1)}, u32[]{:S(2)}, u32[]{:S(2)}) collective-permute-start(s16[272,768]{1,0:T(8,128)(2,1)S(1)} %get-tuple-element.37), channel_id=1, source_target_pairs={{0,64},{64,128},{128,192},{192,0},{1,65},{65,129},{129,193},{193,1... | collective-permute-start | bytes 1253384 | tf_op jit(solution)/shard_map/ppermute | solution.py:314
  144.3 13.8 %collective-permute-start.22 = (s16[272,768]{1,0:T(8,128)(2,1)S(1)}, s16[272,768]{1,0:T(8,128)(2,1)S(1)}, u32[]{:S(2)}, u32[]{:S(2)}) collective-permute-start(s16[272,768]{1,0:T(8,128)(2,1)S(1)} %get-tuple-element.38), channel_id=1, source_target_pairs={{0,192},{64,0},{128,64},{192,128},{1,193},{65,1},{129,65},{193,129... | collective-permute-start | bytes 1253384 | tf_op jit(solution)/shard_map/ppermute | solution.py:314
  147.8 19.2 %collective-permute-start.24 = (s16[272,768]{1,0:T(8,128)(2,1)S(1)}, s16[272,768]{1,0:T(8,128)(2,1)S(1)}, u32[]{:S(2)}, u32[]{:S(2)}) collective-permute-start(s16[272,768]{1,0:T(8,128)(2,1)S(1)} %get-tuple-element.40), channel_id=1, source_target_pairs={{0,192},{64,0},{128,64},{192,128},{1,193},{65,1},{129,65},{193,129... | collective-permute-start | bytes 1253384 | tf_op jit(solution)/shard_map/ppermute | solution.py:314
  148.7 18.3 %collective-permute-start.25 = (s16[272,768]{1,0:T(8,128)(2,1)S(1)}, s16[272,768]{1,0:T(8,128)(2,1)S(1)}, u32[]{:S(2)}, u32[]{:S(2)}) collective-permute-start(s16[272,768]{1,0:T(8,128)(2,1)S(1)} %get-tuple-element.41), channel_id=1, source_target_pairs={{0,64},{64,128},{128,192},{192,0},{1,65},{65,129},{129,193},{193,1... | collective-permute-start | bytes 1253384 | tf_op jit(solution)/shard_map/ppermute | solution.py:314
  159.0 14.0 %collective-permute-start.23 = (s16[272,768]{1,0:T(8,128)(2,1)S(1)}, s16[272,768]{1,0:T(8,128)(2,1)S(1)}, u32[]{:S(2)}, u32[]{:S(2)}) collective-permute-start(s16[272,768]{1,0:T(8,128)(2,1)S(1)} %get-tuple-element.39), channel_id=1, source_target_pairs={{0,64},{64,128},{128,192},{192,0},{1,65},{65,129},{129,193},{193,1... | collective-permute-start | bytes 1253384 | tf_op jit(solution)/shard_map/ppermute | solution.py:314
  159.3 15.0 %collective-permute-start.26 = (s16[272,768]{1,0:T(8,128)(2,1)S(1)}, s16[272,768]{1,0:T(8,128)(2,1)S(1)}, u32[]{:S(2)}, u32[]{:S(2)}) collective-permute-start(s16[272,768]{1,0:T(8,128)(2,1)S(1)} %get-tuple-element.42), channel_id=1, source_target_pairs={{0,192},{64,0},{128,64},{192,128},{1,193},{65,1},{129,65},{193,129... | collective-permute-start | bytes 1253384 | tf_op jit(solution)/shard_map/ppermute | solution.py:314

commit v4 on v3

--- a/solution.py
+++ b/solution.py
@@ -161,7 +161,7 @@
         in_specs=[IN_VMEM, pl.BlockSpec((1, D, STRIP), lambda i: (0, 0, i))]
         + [pl.BlockSpec(memory_space=pl.ANY)] * len(gates),
         out_specs=pl.BlockSpec((STRIP, ROWS), lambda i: (i, 0)),
-        compiler_params=params(54),
+        compiler_params=params(46),
         cost_estimate=pl.CostEstimate(
             flops=2 * ROWS * D * D, bytes_accessed=2 * D * D + 4 * ROWS * D, transcendentals=0
         ),
@@ -334,7 +334,7 @@
     here = z.astype(I32).reshape(1)
 
     ring = z_ring(*stage(tokens, routing.T))
-    packed = pack_grads(here, routing.T, grads.reshape(TOK * TOP, FF), [])
+    packed = pack_grads(here, routing.T, grads.reshape(TOK * TOP, FF), [ring[2][0], ring[2][1], ring[6][0], ring[6][1]])
     grads_in = to_owners(packed)
     by_z = regroup(grads_in, [*ring[3], *ring[5]])
     rows_out = [by_z[k] if k == 0 else shift(by_z[k], "z", k) for k in ORDER]

time: 176 us -> 180 us (1.023)
  waiting for transfers between devices: 77.9 us -> 81.2 us
    ppermute x27, waiting for transfers between devices: 71.8 us -> 78.2 us  [shift(): return lax.ppermute(value, axis, [(i, (i + by) % n) for i in range(n)])]
    all_to_all x2, waiting for transfers between devices: 6.04 us -> 2.98 us  [to_owners(): lax.all_to_all(value, ('y', 'c'), split_axis=0, concat_axis=0, tiled=True)]
  transfers between devices with their start and end apart: 29 -> 29, of which waited for: 19 -> 16; matrix products, arithmetic and copies ran while one was open for 0% -> 0% of each run, Pallas kernels for 6% -> 5%
where the time goes in v4:
time: 180 us; the launch traced here: 179 us
  waiting for transfers between devices  81.2 us (45%)
  starting transfers between devices  51.5 us (29%)
  Pallas kernels  38.6 us (21%)
  local copies, waits for them, and re-layouts  7.87 us (4%)
    ppermute x27, waiting for transfers between devices, shift(): return lax.ppermute(value, axis, [(i, (i + by) % n) for i in range(n)])  78.2 us
    ppermute x27, starting transfers between devices, shift(): return lax.ppermute(value, axis, [(i, (i + by) % n) for i in range(n)])  42.5 us
    pallas_call x1, Pallas kernels, rotate_inputs(): pl.pallas_call(rotate_kernel, out_shape=jax.ShapeDtypeStruct((D, ROWS), B...  12.5 us
    all_to_all x2, starting transfers between devices, to_owners(): lax.all_to_all(value, ('y', 'c'), split_axis=0, concat_axis=0, tiled=True)  9.02 us
    unnamed x38, local copies, waits for them, and re-layouts  7.87 us
    pallas_call x1, Pallas kernels, pack_tokens(): pl.pallas_call(functools.partial(pack_tokens_kernel, n), out_shape=jax.Sh...  6.47 us
    pallas_call x1, Pallas kernels, pack_grads(): pl.pallas_call(pack_grads_kernel, out_shape=jax.ShapeDtypeStruct((N_YC, N...  4.8 us
  transfers between devices with their start and end apart: 29, of which 16 were waited for; matrix products, arithmetic and copies ran while one was open for 0% of the time, Pallas kernels for 5%

profile of v4, /device:TPU:6, one launch (start us, length us, event | category | flops | bytes accessed | tf_op | source)
XLA Modules:
  0.0 179.4 jit_solution(5147708208098010952)
XLA Ops:
  0.0 1.9 %shard_map.55 = (bf16[136,1024]{1,0:T(8,128)(2,1)}, bf16[128,1024]{1,0:T(8,128)(2,1)}) custom-call(bf16[128,2048]{1,0:T(8,128)(2,1)} %tokens_ref.1, s32[8,128]{1,0:T(8,128)} %bitcast.8), custom_call_target="tpu_custom_call" | custom-call | tf_op jit(solution)/shard_map/pallas_call | solution.py:57
  1.9 5.9 %collective-permute-start.1 = (bf16[136,1024]{1,0:T(8,128)(2,1)}, bf16[136,1024]{1,0:T(8,128)(2,1)S(1)}, u32[]{:S(2)}, u32[]{:S(2)}) collective-permute-start(bf16[136,1024]{1,0:T(8,128)(2,1)} %get-tuple-element.24.refs_0_), channel_id=1, source_target_pairs={{0,56},{8,0},{16,8},{24,16},{32,24},{40,32},{48,40},{56,48},{1,57}... | collective-permute-start | bytes 835592 | tf_op jit(solution)/shard_map/ppermute | solution.py:314
  7.7 3.2 %collective-permute-start.8 = (bf16[128,1024]{1,0:T(8,128)(2,1)}, bf16[128,1024]{1,0:T(8,128)(2,1)S(1)}, u32[]{:S(2)}, u32[]{:S(2)}) collective-permute-start(bf16[128,1024]{1,0:T(8,128)(2,1)} %get-tuple-element.25.refs_8_), channel_id=1, source_target_pairs={{0,56},{8,0},{16,8},{24,16},{32,24},{40,32},{48,40},{56,48},{1,57}... | collective-permute-start | bytes 786440 | tf_op jit(solution)/shard_map/ppermute | solution.py:314
  11.0 4.1 %collective-permute-done.1.refs_2_ = bf16[136,1024]{1,0:T(8,128)(2,1)S(1)} collective-permute-done((bf16[136,1024]{1,0:T(8,128)(2,1)}, bf16[136,1024]{1,0:T(8,128)(2,1)S(1)}, u32[]{:S(2)}, u32[]{:S(2)}) %collective-permute-start.1) | collective-permute-done | bytes 278560 | tf_op jit(solution)/shard_map/ppermute | solution.py:314
  15.1 3.6 %collective-permute-start.3 = (bf16[136,1024]{1,0:T(8,128)(2,1)S(1)}, bf16[136,1024]{1,0:T(8,128)(2,1)}, u32[]{:S(2)}, u32[]{:S(2)}) collective-permute-start(bf16[136,1024]{1,0:T(8,128)(2,1)S(1)} %collective-permute-done.1.refs_2_), channel_id=1, source_target_pairs={{0,56},{8,0},{16,8},{24,16},{32,24},{40,32},{48,40},{56,48},{1,57}... | collective-permute-start | bytes 835592 | tf_op jit(solution)/shard_map/ppermute | solution.py:314
  18.7 2.0 %collective-permute-done.8.refs_10_ = bf16[128,1024]{1,0:T(8,128)(2,1)S(1)} collective-permute-done((bf16[128,1024]{1,0:T(8,128)(2,1)}, bf16[128,1024]{1,0:T(8,128)(2,1)S(1)}, u32[]{:S(2)}, u32[]{:S(2)}) %collective-permute-start.8) | collective-permute-done | bytes 262176 | tf_op jit(solution)/shard_map/ppermute | solution.py:314
  20.7 3.6 %collective-permute-start.10 = (bf16[128,1024]{1,0:T(8,128)(2,1)S(1)}, bf16[128,1024]{1,0:T(8,128)(2,1)}, u32[]{:S(2)}, u32[]{:S(2)}) collective-permute-start(bf16[128,1024]{1,0:T(8,128)(2,1)S(1)} %collective-permute-done.8.refs_10_), channel_id=1, source_target_pairs={{0,56},{8,0},{16,8},{24,16},{32,24},{40,32},{48,40},{56,48},{1,57}... | collective-permute-start | bytes 786440 | tf_op jit(solution)/shard_map/ppermute | solution.py:314
  24.3 6.7 %collective-permute-done.10.refs_3_.refs_12_ = bf16[128,1024]{1,0:T(8,128)(2,1)} collective-permute-done((bf16[128,1024]{1,0:T(8,128)(2,1)S(1)}, bf16[128,1024]{1,0:T(8,128)(2,1)}, u32[]{:S(2)}, u32[]{:S(2)}) %collective-permute-start.10) | collective-permute-done | bytes 262176 | tf_op jit(solution)/shard_map/ppermute | solution.py:314
  31.1 3.5 %collective-permute-done.9.refs_1_.refs_11_ = bf16[128,1024]{1,0:T(8,128)(2,1)} collective-permute-done((bf16[128,1024]{1,0:T(8,128)(2,1)S(1)}, bf16[128,1024]{1,0:T(8,128)(2,1)}, u32[]{:S(2)}, u32[]{:S(2)}) %collective-permute-start.9) | collective-permute-done | bytes 262176 | tf_op jit(solution)/shard_map/ppermute | solution.py:314
  34.6 4.8 %shard_map.56 = bf16[8,128,768]{2,1,0:T(8,128)(2,1)} custom-call(s32[1]{0:T(128)} %bitcast.4.here_ref, s32[8,128]{1,0:T(8,128)} %bitcast.9, bf16[1024,768]{1,0:T(8,128)(2,1)} %bitcast.10, bf16[136,1024]{1,0:T(8,128)(2,1)} %collective-permute-done.2.refs_0_.refs_3_, bf16[128,1024]{1,0:T(8,128)(2,1)} %collective-permute-done.9.refs_1_.refs_11_, ...), custom_call_target="tpu_custom_call" | custom-call | flops 1610612736 | bytes 3145728 | tf_op jit(solution)/shard_map/pallas_call | solution.py:86
  39.4 4.5 %all-to-all-start = ((bf16[8,128,768]{2,1,0:T(8,128)(2,1)}), bf16[8,128,768]{2,1,0:T(8,128)(2,1)S(1)}, u32[]{:S(2)}, u32[]{:S(2)}) async-start(bf16[8,128,768]{2,1,0:T(8,128)(2,1)} %shard_map.56), calls=%async_computation | async-start | bytes 3145728 | tf_op jit(solution)/shard_map/all_to_all | solution.py:318
  43.9 3.2 %collective-permute-start.12 = (bf16[128,1024]{1,0:T(8,128)(2,1)}, bf16[128,1024]{1,0:T(8,128)(2,1)S(1)}, u32[]{:S(2)}, u32[]{:S(2)}) collective-permute-start(bf16[128,1024]{1,0:T(8,128)(2,1)} %collective-permute-done.10.refs_3_.refs_12_), channel_id=1, source_target_pairs={{0,56},{8,0},{16,8},{24,16},{32,24},{40,32},{48,40},{56,48},{1,57}... | collective-permute-start | bytes 786440 | tf_op jit(solution)/shard_map/ppermute | solution.py:314
  47.2 7.2 %collective-permute-done.4.refs_5_.refs_1_ = bf16[136,1024]{1,0:T(8,128)(2,1)S(1)} collective-permute-done((bf16[136,1024]{1,0:T(8,128)(2,1)}, bf16[136,1024]{1,0:T(8,128)(2,1)S(1)}, u32[]{:S(2)}, u32[]{:S(2)}) %collective-permute-start.4) | collective-permute-done | bytes 278560 | tf_op jit(solution)/shard_map/ppermute | solution.py:314
  54.4 3.3 %collective-permute-start.13 = (bf16[128,1024]{1,0:T(8,128)(2,1)S(1)}, bf16[128,1024]{1,0:T(8,128)(2,1)S(1)}, u32[]{:S(2)}, u32[]{:S(2)}) collective-permute-start(bf16[128,1024]{1,0:T(8,128)(2,1)S(1)} %collective-permute-done.12.refs_14_.refs_4_), channel_id=1, source_target_pairs={{0,56},{8,0},{16,8},{24,16},{32,24},{40,32},{48,40},{56,48},{1,57}... | collective-permute-start | bytes 786440 | tf_op jit(solution)/shard_map/ppermute | solution.py:314
  57.7 11.8 %collective-permute-done.11.refs_13_.refs_2_ = bf16[128,1024]{1,0:T(8,128)(2,1)S(1)} collective-permute-done((bf16[128,1024]{1,0:T(8,128)(2,1)}, bf16[128,1024]{1,0:T(8,128)(2,1)S(1)}, u32[]{:S(2)}, u32[]{:S(2)}) %collective-permute-start.11) | collective-permute-done | bytes 262176 | tf_op jit(solution)/shard_map/ppermute | solution.py:314
  70.5 1.1 copy-done.8
  71.7 6.5 %shard_map.57 = bf16[8,128,2048]{2,1,0:T(8,128)(2,1)} custom-call(s32[1]{0:T(128)} %bitcast.4.here_ref, bf16[136,1024]{1,0:T(8,128)(2,1)} %get-tuple-element.24.refs_0_, bf16[136,1024]{1,0:T(8,128)(2,1)} %copy-done.14, bf16[136,1024]{1,0:T(8,128)(2,1)} %copy-done.13, bf16[136,1024]{1,0:T(8,128)(2,1)} %collective-permute-done.2.refs_0_.refs_3_, ...), custom_call_target="tpu_custom_call" | custom-call | flops 536870912 | bytes 8388608 | tf_op jit(solution)/shard_map/pallas_call | solution.py:135
  78.1 4.5 %all-to-all-start.1 = ((bf16[8,128,2048]{2,1,0:T(8,128)(2,1)}), bf16[8,128,2048]{2,1,0:T(8,128)(2,1)}, u32[]{:S(2)}, u32[]{:S(2)}) async-start(bf16[8,128,2048]{2,1,0:T(8,128)(2,1)} %shard_map.57), calls=%async_computation.1 | async-start | bytes 8388608 | tf_op jit(solution)/shard_map/all_to_all | solution.py:318
  82.7 2.7 %shard_map.58 = (bf16[128,768]{1,0:T(8,128)(2,1)}, bf16[128,768]{1,0:T(8,128)(2,1)}, bf16[128,768]{1,0:T(8,128)(2,1)}, bf16[128,768]{1,0:T(8,128)(2,1)}, bf16[12...) custom-call(bf16[8,128,768]{2,1,0:T(8,128)(2,1)} %copy-done.8, ...), custom_call_target="tpu_custom_call" | custom-call | tf_op jit(solution)/shard_map/pallas_call | solution.py:106
  85.4 3.2 %collective-permute-start.15 = (bf16[128,768]{1,0:T(8,128)(2,1)}, bf16[128,768]{1,0:T(8,128)(2,1)S(1)}, u32[]{:S(2)}, u32[]{:S(2)}) collective-permute-start(bf16[128,768]{1,0:T(8,128)(2,1)} %get-tuple-element.28), channel_id=1, source_target_pairs={{0,56},{8,0},{16,8},{24,16},{32,24},{40,32},{48,40},{56,48},{1,57}... | collective-permute-start | bytes 589832 | tf_op jit(solution)/shard_map/ppermute | solution.py:314
  88.6 4.1 %collective-permute-start.17 = (bf16[128,768]{1,0:T(8,128)(2,1)}, bf16[128,768]{1,0:T(8,128)(2,1)S(1)}, u32[]{:S(2)}, u32[]{:S(2)}) collective-permute-start(bf16[128,768]{1,0:T(8,128)(2,1)} %get-tuple-element.30), channel_id=1, source_target_pairs={{0,48},{8,56},{16,0},{24,8},{32,16},{40,24},{48,32},{56,40},{1,49}... | collective-permute-start | bytes 589832 | tf_op jit(solution)/shard_map/ppermute | solution.py:314
  92.8 3.7 %collective-permute-done.14.refs_1_ = bf16[128,768]{1,0:T(8,128)(2,1)S(1)} collective-permute-done((bf16[128,768]{1,0:T(8,128)(2,1)}, bf16[128,768]{1,0:T(8,128)(2,1)S(1)}, u32[]{:S(2)}, u32[]{:S(2)}) %collective-permute-start.14) | collective-permute-done | bytes 196640 | tf_op jit(solution)/shard_map/ppermute | solution.py:314
  96.5 1.3 collective-permute-start.19
  97.8 3.2 %collective-permute-start.20 = (bf16[128,768]{1,0:T(8,128)(2,1)}, bf16[128,768]{1,0:T(8,128)(2,1)S(1)}, u32[]{:S(2)}, u32[]{:S(2)}) collective-permute-start(bf16[128,768]{1,0:T(8,128)(2,1)} %get-tuple-element.33), channel_id=1, source_target_pairs={{0,32},{8,40},{16,48},{24,56},{32,0},{40,8},{48,16},{56,24},{1,33}... | collective-permute-start | bytes 589832 | tf_op jit(solution)/shard_map/ppermute | solution.py:314
  101.0 9.7 %collective-permute-done.16.refs_3_ = bf16[128,768]{1,0:T(8,128)(2,1)S(1)} collective-permute-done((bf16[128,768]{1,0:T(8,128)(2,1)}, bf16[128,768]{1,0:T(8,128)(2,1)S(1)}, u32[]{:S(2)}, u32[]{:S(2)}) %collective-permute-start.16) | collective-permute-done | bytes 196640 | tf_op jit(solution)/shard_map/ppermute | solution.py:314
  110.8 5.4 %collective-permute-done.18.refs_5_ = bf16[128,768]{1,0:T(8,128)(2,1)S(1)} collective-permute-done((bf16[128,768]{1,0:T(8,128)(2,1)}, bf16[128,768]{1,0:T(8,128)(2,1)S(1)}, u32[]{:S(2)}, u32[]{:S(2)}) %collective-permute-start.18) | collective-permute-done | bytes 196640 | tf_op jit(solution)/shard_map/ppermute | solution.py:314
  116.9 6.0 %collective-permute-done.19.refs_6_ = bf16[128,768]{1,0:T(8,128)(2,1)S(1)} collective-permute-done((bf16[128,768]{1,0:T(8,128)(2,1)}, bf16[128,768]{1,0:T(8,128)(2,1)S(1)}, u32[]{:S(2)}, u32[]{:S(2)}) %collective-permute-start.19) | collective-permute-done | bytes 196640 | tf_op jit(solution)/shard_map/ppermute | solution.py:314
  124.2 0.9 copy-done.1
  125.2 0.9 copy-done.3
  126.1 0.9 copy-done.5
  127.0 0.9 copy-done.7
  127.9 1.4 shard_map.59.refs_0_.g_ref
  129.4 3.0 %all-to-all-done.1.rows_ref = bf16[8,128,2048]{2,1,0:T(8,128)(2,1)} async-done(((bf16[8,128,2048]{2,1,0:T(8,128)(2,1)}), bf16[8,128,2048]{2,1,0:T(8,128)(2,1)}, u32[]{:S(2)}, u32[]{:S(2)}) %all-to-all-start.1) | async-done | bytes 4194336 | tf_op jit(solution)/shard_map/all_to_all | solution.py:318
  132.3 12.5 %shard_map.60.a_ref = bf16[2048,1024]{1,0:T(8,128)(2,1)S(1)} custom-call(bf16[8,128,2048]{2,1,0:T(8,128)(2,1)} %all-to-all-done.1.rows_ref, bf16[1,2048,2048]{2,1,0:T(8,128)(2,1)} %basis_ref.1, bf16[1024,768]{1,0:T(8,128)(2,1)S(1)} %shard_map.59.refs_0_.g_ref), custom_call_target="tpu_custom_call" | custom-call | flops 8589934592 | bytes 16777216 | tf_op jit(solution)/shard_map/pallas_call | solution.py:157
  144.9 1.9 %shard_map.62 = (s16[272,768]{1,0:T(8,128)(2,1)S(1)}, s16[272,768]{1,0:T(8,128)(2,1)S(1)}) custom-call(s32[4]{0:T(128)S(1)} %pad_add_fusion.place_ref, bf16[2048,1024]{1,0:T(8,128)(2,1)S(1)} %shard_map.60.a_ref, bf16[1024,768]{1,0:T(8,128)(2,1)S(1)} %shard_map.59.refs_0_.g_ref), custom_call_target="tpu_custom_call" | custom-call | flops 805306368 | bytes 4194304 | tf_op jit(solution)/shard_map/pallas_call | solution.py:224
  147.6 1.5 collective-permute-start.22
  149.2 1.9 %shard_map.64 = (s16[272,768]{1,0:T(8,128)(2,1)S(1)}, s16[272,768]{1,0:T(8,128)(2,1)S(1)}) custom-call(s32[4]{0:T(128)S(1)} %pad_add_fusion.place_ref, bf16[2048,1024]{1,0:T(8,128)(2,1)S(1)} %shard_map.60.a_ref, bf16[1024,768]{1,0:T(8,128)(2,1)S(1)} %shard_map.59.refs_0_.g_ref), custom_call_target="tpu_custom_call" | custom-call | flops 805306368 | bytes 4194304 | tf_op jit(solution)/shard_map/pallas_call | solution.py:242
  151.1 0.9 collective-permute-start.24
  152.1 2.4 %collective-permute-start.25 = (s16[272,768]{1,0:T(8,128)(2,1)S(1)}, s16[272,768]{1,0:T(8,128)(2,1)S(1)}, u32[]{:S(2)}, u32[]{:S(2)}) collective-permute-start(s16[272,768]{1,0:T(8,128)(2,1)S(1)} %get-tuple-element.41), channel_id=1, source_target_pairs={{0,64},{64,128},{128,192},{192,0},{1,65},{65,129},{129,193},{193,1... | collective-permute-start | bytes 1253384 | tf_op jit(solution)/shard_map/ppermute | solution.py:314
  154.4 2.3 %shard_map.61 = (f32[256,768]{1,0:T(8,128)S(1)}, f32[256,768]{1,0:T(8,128)S(1)}, f32[512,768]{1,0:T(8,128)S(1)}) custom-call(s32[4]{0:T(128)S(1)} %pad_add_fusion.place_ref, bf16[2048,1024]{1,0:T(8,128)(2,1)S(1)} %shard_map.60.a_ref, bf16[1024,768]{1,0:T(8,128)(2,1)S(1)} %shard_map.59.refs_0_.g_ref), custom_call_target="tpu_custom_call" | custom-call | flops 1610612736 | bytes 8388608 | tf_op jit(solution)/shard_map/pallas_call | solution.py:262
  156.8 2.9 %collective-permute-done.21.got_up_ref = s16[272,768]{1,0:T(8,128)(2,1)S(1)} collective-permute-done((s16[272,768]{1,0:T(8,128)(2,1)S(1)}, s16[272,768]{1,0:T(8,128)(2,1)S(1)}, u32[]{:S(2)}, u32[]{:S(2)}) %collective-permute-start.21) | collective-permute-done | bytes 417824 | tf_op jit(solution)/shard_map/ppermute | solution.py:314
  159.7 1.7 collective-permute-done.22.got_down_ref
  161.4 0.9 shard_map.63
  162.7 1.7 collective-permute-start.26
  164.4 6.0 %collective-permute-done.24.top_b_ref = s16[272,768]{1,0:T(8,128)(2,1)S(1)} collective-permute-done((s16[272,768]{1,0:T(8,128)(2,1)S(1)}, s16[272,768]{1,0:T(8,128)(2,1)S(1)}, u32[]{:S(2)}, u32[]{:S(2)}) %collective-permute-start.24) | collective-permute-done | bytes 417824 | tf_op jit(solution)/shard_map/ppermute | solution.py:314
  170.4 5.9 %collective-permute-done.23.top_a_ref = s16[272,768]{1,0:T(8,128)(2,1)S(1)} collective-permute-done((s16[272,768]{1,0:T(8,128)(2,1)S(1)}, s16[272,768]{1,0:T(8,128)(2,1)S(1)}, u32[]{:S(2)}, u32[]{:S(2)}) %collective-permute-start.23) | collective-permute-done | bytes 417824 | tf_op jit(solution)/shard_map/ppermute | solution.py:314
  176.2 1.4 collective-permute-done.26.bottom_b_ref
  177.7 1.7 shard_map.65
  (60 shorter events, 4.4 us)
Async XLA Ops:
  1.9 13.2 %collective-permute-start.1 = (bf16[136,1024]{1,0:T(8,128)(2,1)}, bf16[136,1024]{1,0:T(8,128)(2,1)S(1)}, u32[]{:S(2)}, u32[]{:S(2)}) collective-permute-start(bf16[136,1024]{1,0:T(8,128)(2,1)} %get-tuple-element.24.refs_0_), channel_id=1, source_target_pairs={{0,56},{8,0},{16,8},{24,16},{32,24},{40,32},{48,40},{56,48},{1,57}... | collective-permute-start | bytes 835592 | tf_op jit(solution)/shard_map/ppermute | solution.py:314
  7.7 11.0 %collective-permute-start = (bf16[136,1024]{1,0:T(8,128)(2,1)}, bf16[136,1024]{1,0:T(8,128)(2,1)S(1)}, u32[]{:S(2)}, u32[]{:S(2)}) collective-permute-start(bf16[136,1024]{1,0:T(8,128)(2,1)} %get-tuple-element.24.refs_0_), channel_id=1, source_target_pairs={{0,8},{8,16},{16,24},{24,32},{32,40},{40,48},{48,56},{56,0},{1,9},... | collective-permute-start | bytes 835592 | tf_op jit(solution)/shard_map/ppermute | solution.py:314
  7.7 13.0 %collective-permute-start.8 = (bf16[128,1024]{1,0:T(8,128)(2,1)}, bf16[128,1024]{1,0:T(8,128)(2,1)S(1)}, u32[]{:S(2)}, u32[]{:S(2)}) collective-permute-start(bf16[128,1024]{1,0:T(8,128)(2,1)} %get-tuple-element.25.refs_8_), channel_id=1, source_target_pairs={{0,56},{8,0},{16,8},{24,16},{32,24},{40,32},{48,40},{56,48},{1,57}... | collective-permute-start | bytes 786440 | tf_op jit(solution)/shard_map/ppermute | solution.py:314
  11.0 13.4 %collective-permute-start.7 = (bf16[128,1024]{1,0:T(8,128)(2,1)}, bf16[128,1024]{1,0:T(8,128)(2,1)S(1)}, u32[]{:S(2)}, u32[]{:S(2)}) collective-permute-start(bf16[128,1024]{1,0:T(8,128)(2,1)} %get-tuple-element.25.refs_8_), channel_id=1, source_target_pairs={{0,8},{8,16},{16,24},{24,32},{32,40},{40,48},{48,56},{56,0},{1,9},... | collective-permute-start | bytes 786440 | tf_op jit(solution)/shard_map/ppermute | solution.py:314
  15.1 24.3 %copy-start.13 = (bf16[136,1024]{1,0:T(8,128)(2,1)}, bf16[136,1024]{1,0:T(8,128)(2,1)S(1)}, u32[]{:S(2)}) copy-start(bf16[136,1024]{1,0:T(8,128)(2,1)S(1)} %collective-permute-done.1.refs_2_) | copy-start | bytes 835588
  15.1 19.5 %collective-permute-start.3 = (bf16[136,1024]{1,0:T(8,128)(2,1)S(1)}, bf16[136,1024]{1,0:T(8,128)(2,1)}, u32[]{:S(2)}, u32[]{:S(2)}) collective-permute-start(bf16[136,1024]{1,0:T(8,128)(2,1)S(1)} %collective-permute-done.1.refs_2_), channel_id=1, source_target_pairs={{0,56},{8,0},{16,8},{24,16},{32,24},{40,32},{48,40},{56,48},{1,57}... | collective-permute-start | bytes 835592 | tf_op jit(solution)/shard_map/ppermute | solution.py:314
  18.7 20.7 %copy-start.14 = (bf16[136,1024]{1,0:T(8,128)(2,1)}, bf16[136,1024]{1,0:T(8,128)(2,1)S(1)}, u32[]{:S(2)}) copy-start(bf16[136,1024]{1,0:T(8,128)(2,1)S(1)} %collective-permute-done.refs_1_) | copy-start | bytes 835588
  18.7 15.8 %collective-permute-start.2 = (bf16[136,1024]{1,0:T(8,128)(2,1)S(1)}, bf16[136,1024]{1,0:T(8,128)(2,1)}, u32[]{:S(2)}, u32[]{:S(2)}) collective-permute-start(bf16[136,1024]{1,0:T(8,128)(2,1)S(1)} %collective-permute-done.refs_1_), channel_id=1, source_target_pairs={{0,8},{8,16},{16,24},{24,32},{32,40},{40,48},{48,56},{56,0},{1,9},... | collective-permute-start | bytes 835592 | tf_op jit(solution)/shard_map/ppermute | solution.py:314
  20.7 18.7 %copy-start.16 = (bf16[128,1024]{1,0:T(8,128)(2,1)}, bf16[128,1024]{1,0:T(8,128)(2,1)S(1)}, u32[]{:S(2)}) copy-start(bf16[128,1024]{1,0:T(8,128)(2,1)S(1)} %collective-permute-done.8.refs_10_) | copy-start | bytes 786436
  20.7 10.3 %collective-permute-start.10 = (bf16[128,1024]{1,0:T(8,128)(2,1)S(1)}, bf16[128,1024]{1,0:T(8,128)(2,1)}, u32[]{:S(2)}, u32[]{:S(2)}) collective-permute-start(bf16[128,1024]{1,0:T(8,128)(2,1)S(1)} %collective-permute-done.8.refs_10_), channel_id=1, source_target_pairs={{0,56},{8,0},{16,8},{24,16},{32,24},{40,32},{48,40},{56,48},{1,57}... | collective-permute-start | bytes 786440 | tf_op jit(solution)/shard_map/ppermute | solution.py:314
  24.3 15.0 %copy-start.17 = (bf16[128,1024]{1,0:T(8,128)(2,1)}, bf16[128,1024]{1,0:T(8,128)(2,1)S(1)}, u32[]{:S(2)}) copy-start(bf16[128,1024]{1,0:T(8,128)(2,1)S(1)} %collective-permute-done.7.refs_9_) | copy-start | bytes 786436
  24.3 10.2 %collective-permute-start.9 = (bf16[128,1024]{1,0:T(8,128)(2,1)S(1)}, bf16[128,1024]{1,0:T(8,128)(2,1)}, u32[]{:S(2)}, u32[]{:S(2)}) collective-permute-start(bf16[128,1024]{1,0:T(8,128)(2,1)S(1)} %collective-permute-done.7.refs_9_), channel_id=1, source_target_pairs={{0,8},{8,16},{16,24},{24,32},{32,40},{40,48},{48,56},{56,0},{1,9},... | collective-permute-start | bytes 786440 | tf_op jit(solution)/shard_map/ppermute | solution.py:314
  39.4 30.1 %all-to-all-start = ((bf16[8,128,768]{2,1,0:T(8,128)(2,1)}), bf16[8,128,768]{2,1,0:T(8,128)(2,1)S(1)}, u32[]{:S(2)}, u32[]{:S(2)}) async-start(bf16[8,128,768]{2,1,0:T(8,128)(2,1)} %shard_map.56), calls=%async_computation | async-start | bytes 3145728 | tf_op jit(solution)/shard_map/all_to_all | solution.py:318
  43.9 10.5 %collective-permute-start.4 = (bf16[136,1024]{1,0:T(8,128)(2,1)}, bf16[136,1024]{1,0:T(8,128)(2,1)S(1)}, u32[]{:S(2)}, u32[]{:S(2)}) collective-permute-start(bf16[136,1024]{1,0:T(8,128)(2,1)} %collective-permute-done.2.refs_0_.refs_3_), channel_id=1, source_target_pairs={{0,8},{8,16},{16,24},{24,32},{32,40},{40,48},{48,56},{56,0},{1,9},... | collective-permute-start | bytes 835592 | tf_op jit(solution)/shard_map/ppermute | solution.py:314
  43.9 10.5 %collective-permute-start.12 = (bf16[128,1024]{1,0:T(8,128)(2,1)}, bf16[128,1024]{1,0:T(8,128)(2,1)S(1)}, u32[]{:S(2)}, u32[]{:S(2)}) collective-permute-start(bf16[128,1024]{1,0:T(8,128)(2,1)} %collective-permute-done.10.refs_3_.refs_12_), channel_id=1, source_target_pairs={{0,56},{8,0},{16,8},{24,16},{32,24},{40,32},{48,40},{56,48},{1,57}... | collective-permute-start | bytes 786440 | tf_op jit(solution)/shard_map/ppermute | solution.py:314
  47.1 22.4 %collective-permute-start.5 = (bf16[136,1024]{1,0:T(8,128)(2,1)}, bf16[136,1024]{1,0:T(8,128)(2,1)S(1)}, u32[]{:S(2)}, u32[]{:S(2)}) collective-permute-start(bf16[136,1024]{1,0:T(8,128)(2,1)} %collective-permute-done.3.refs_2_.refs_4_), channel_id=1, source_target_pairs={{0,56},{8,0},{16,8},{24,16},{32,24},{40,32},{48,40},{56,48},{1,57}... | collective-permute-start | bytes 835592 | tf_op jit(solution)/shard_map/ppermute | solution.py:314
  54.4 15.2 %copy-start.9 = (bf16[136,1024]{1,0:T(8,128)(2,1)}, bf16[136,1024]{1,0:T(8,128)(2,1)S(1)}, u32[]{:S(2)}) copy-start(bf16[136,1024]{1,0:T(8,128)(2,1)S(1)} %collective-permute-done.4.refs_5_.refs_1_) | copy-start | bytes 835588
  54.4 15.1 %collective-permute-start.6 = (bf16[136,1024]{1,0:T(8,128)(2,1)S(1)}, bf16[136,1024]{1,0:T(8,128)(2,1)S(1)}, u32[]{:S(2)}, u32[]{:S(2)}) collective-permute-start(bf16[136,1024]{1,0:T(8,128)(2,1)S(1)} %collective-permute-done.4.refs_5_.refs_1_), channel_id=1, source_target_pairs={{0,8},{8,16},{16,24},{24,32},{32,40},{40,48},{48,56},{56,0},{1,9},... | collective-permute-start | bytes 835592 | tf_op jit(solution)/shard_map/ppermute | solution.py:314
  54.4 15.1 %collective-permute-start.11 = (bf16[128,1024]{1,0:T(8,128)(2,1)}, bf16[128,1024]{1,0:T(8,128)(2,1)S(1)}, u32[]{:S(2)}, u32[]{:S(2)}) collective-permute-start(bf16[128,1024]{1,0:T(8,128)(2,1)} %collective-permute-done.9.refs_1_.refs_11_), channel_id=1, source_target_pairs={{0,8},{8,16},{16,24},{24,32},{32,40},{40,48},{48,56},{56,0},{1,9},... | collective-permute-start | bytes 786440 | tf_op jit(solution)/shard_map/ppermute | solution.py:314
  54.4 15.2 %copy-start.11 = (bf16[128,1024]{1,0:T(8,128)(2,1)}, bf16[128,1024]{1,0:T(8,128)(2,1)S(1)}, u32[]{:S(2)}) copy-start(bf16[128,1024]{1,0:T(8,128)(2,1)S(1)} %collective-permute-done.12.refs_14_.refs_4_) | copy-start | bytes 786436
  54.4 15.1 %collective-permute-start.13 = (bf16[128,1024]{1,0:T(8,128)(2,1)S(1)}, bf16[128,1024]{1,0:T(8,128)(2,1)S(1)}, u32[]{:S(2)}, u32[]{:S(2)}) collective-permute-start(bf16[128,1024]{1,0:T(8,128)(2,1)S(1)} %collective-permute-done.12.refs_14_.refs_4_), channel_id=1, source_target_pairs={{0,56},{8,0},{16,8},{24,16},{32,24},{40,32},{48,40},{56,48},{1,57}... | collective-permute-start | bytes 786440 | tf_op jit(solution)/shard_map/ppermute | solution.py:314
  69.5 0.7 copy-start.12
  69.5 0.8 copy-start.10
  69.5 0.9 copy-start.18
  69.5 1.0 copy-start.15
  70.5 1.1 copy-start.8
  78.1 54.2 %all-to-all-start.1 = ((bf16[8,128,2048]{2,1,0:T(8,128)(2,1)}), bf16[8,128,2048]{2,1,0:T(8,128)(2,1)}, u32[]{:S(2)}, u32[]{:S(2)}) async-start(bf16[8,128,2048]{2,1,0:T(8,128)(2,1)} %shard_map.57), calls=%async_computation.1 | async-start | bytes 8388608 | tf_op jit(solution)/shard_map/all_to_all | solution.py:318
  82.7 41.5 %copy-start = (bf16[1,768,768]{2,1,0:T(8,128)(2,1)S(1)}, bf16[1,768,768]{2,1,0:T(8,128)(2,1)}, u32[]{:S(2)}) copy-start(bf16[1,768,768]{2,1,0:T(8,128)(2,1)} %refs_8_.1) | copy-start | bytes 3538948
  85.4 11.1 %collective-permute-start.14 = (bf16[128,768]{1,0:T(8,128)(2,1)}, bf16[128,768]{1,0:T(8,128)(2,1)S(1)}, u32[]{:S(2)}, u32[]{:S(2)}) collective-permute-start(bf16[128,768]{1,0:T(8,128)(2,1)} %get-tuple-element.27), channel_id=1, source_target_pairs={{0,8},{8,16},{16,24},{24,32},{32,40},{40,48},{48,56},{56,0},{1,9},... | collective-permute-start | bytes 589832 | tf_op jit(solution)/shard_map/ppermute | solution.py:314
  85.4 12.4 %collective-permute-start.15 = (bf16[128,768]{1,0:T(8,128)(2,1)}, bf16[128,768]{1,0:T(8,128)(2,1)S(1)}, u32[]{:S(2)}, u32[]{:S(2)}) collective-permute-start(bf16[128,768]{1,0:T(8,128)(2,1)} %get-tuple-element.28), channel_id=1, source_target_pairs={{0,56},{8,0},{16,8},{24,16},{32,24},{40,32},{48,40},{56,48},{1,57}... | collective-permute-start | bytes 589832 | tf_op jit(solution)/shard_map/ppermute | solution.py:314
  88.6 22.2 %collective-permute-start.16 = (bf16[128,768]{1,0:T(8,128)(2,1)}, bf16[128,768]{1,0:T(8,128)(2,1)S(1)}, u32[]{:S(2)}, u32[]{:S(2)}) collective-permute-start(bf16[128,768]{1,0:T(8,128)(2,1)} %get-tuple-element.29), channel_id=1, source_target_pairs={{0,16},{8,24},{16,32},{24,40},{32,48},{40,56},{48,0},{56,8},{1,17}... | collective-permute-start | bytes 589832 | tf_op jit(solution)/shard_map/ppermute | solution.py:314
  88.6 22.2 %collective-permute-start.17 = (bf16[128,768]{1,0:T(8,128)(2,1)}, bf16[128,768]{1,0:T(8,128)(2,1)S(1)}, u32[]{:S(2)}, u32[]{:S(2)}) collective-permute-start(bf16[128,768]{1,0:T(8,128)(2,1)} %get-tuple-element.30), channel_id=1, source_target_pairs={{0,48},{8,56},{16,0},{24,8},{32,16},{40,24},{48,32},{56,40},{1,49}... | collective-permute-start | bytes 589832 | tf_op jit(solution)/shard_map/ppermute | solution.py:314
  92.7 23.5 %collective-permute-start.18 = (bf16[128,768]{1,0:T(8,128)(2,1)}, bf16[128,768]{1,0:T(8,128)(2,1)S(1)}, u32[]{:S(2)}, u32[]{:S(2)}) collective-permute-start(bf16[128,768]{1,0:T(8,128)(2,1)} %get-tuple-element.31), channel_id=1, source_target_pairs={{0,24},{8,32},{16,40},{24,48},{32,56},{40,0},{48,8},{56,16},{1,25}... | collective-permute-start | bytes 589832 | tf_op jit(solution)/shard_map/ppermute | solution.py:314
  96.5 26.4 %collective-permute-start.19 = (bf16[128,768]{1,0:T(8,128)(2,1)}, bf16[128,768]{1,0:T(8,128)(2,1)S(1)}, u32[]{:S(2)}, u32[]{:S(2)}) collective-permute-start(bf16[128,768]{1,0:T(8,128)(2,1)} %get-tuple-element.32), channel_id=1, source_target_pairs={{0,40},{8,48},{16,56},{24,0},{32,8},{40,16},{48,24},{56,32},{1,41}... | collective-permute-start | bytes 589832 | tf_op jit(solution)/shard_map/ppermute | solution.py:314
  97.8 25.8 %collective-permute-start.20 = (bf16[128,768]{1,0:T(8,128)(2,1)}, bf16[128,768]{1,0:T(8,128)(2,1)S(1)}, u32[]{:S(2)}, u32[]{:S(2)}) collective-permute-start(bf16[128,768]{1,0:T(8,128)(2,1)} %get-tuple-element.33), channel_id=1, source_target_pairs={{0,32},{8,40},{16,48},{24,56},{32,0},{40,8},{48,16},{56,24},{1,33}... | collective-permute-start | bytes 589832 | tf_op jit(solution)/shard_map/ppermute | solution.py:314
  116.2 0.7 copy-start.2
  122.9 0.7 copy-start.4
  123.5 0.7 copy-start.6
  124.2 0.9 copy-start.1
  125.2 0.9 copy-start.3
  126.1 0.9 copy-start.5
  127.0 0.9 copy-start.7
  146.9 12.9 %collective-permute-start.21 = (s16[272,768]{1,0:T(8,128)(2,1)S(1)}, s16[272,768]{1,0:T(8,128)(2,1)S(1)}, u32[]{:S(2)}, u32[]{:S(2)}) collective-permute-start(s16[272,768]{1,0:T(8,128)(2,1)S(1)} %get-tuple-element.37), channel_id=1, source_target_pairs={{0,64},{64,128},{128,192},{192,0},{1,65},{65,129},{129,193},{193,1... | collective-permute-start | bytes 1253384 | tf_op jit(solution)/shard_map/ppermute | solution.py:314
  147.6 13.8 %collective-permute-start.22 = (s16[272,768]{1,0:T(8,128)(2,1)S(1)}, s16[272,768]{1,0:T(8,128)(2,1)S(1)}, u32[]{:S(2)}, u32[]{:S(2)}) collective-permute-start(s16[272,768]{1,0:T(8,128)(2,1)S(1)} %get-tuple-element.38), channel_id=1, source_target_pairs={{0,192},{64,0},{128,64},{192,128},{1,193},{65,1},{129,65},{193,129... | collective-permute-start | bytes 1253384 | tf_op jit(solution)/shard_map/ppermute | solution.py:314
  151.1 19.2 %collective-permute-start.24 = (s16[272,768]{1,0:T(8,128)(2,1)S(1)}, s16[272,768]{1,0:T(8,128)(2,1)S(1)}, u32[]{:S(2)}, u32[]{:S(2)}) collective-permute-start(s16[272,768]{1,0:T(8,128)(2,1)S(1)} %get-tuple-element.40), channel_id=1, source_target_pairs={{0,192},{64,0},{128,64},{192,128},{1,193},{65,1},{129,65},{193,129... | collective-permute-start | bytes 1253384 | tf_op jit(solution)/shard_map/ppermute | solution.py:314
  152.1 18.3 %collective-permute-start.25 = (s16[272,768]{1,0:T(8,128)(2,1)S(1)}, s16[272,768]{1,0:T(8,128)(2,1)S(1)}, u32[]{:S(2)}, u32[]{:S(2)}) collective-permute-start(s16[272,768]{1,0:T(8,128)(2,1)S(1)} %get-tuple-element.41), channel_id=1, source_target_pairs={{0,64},{64,128},{128,192},{192,0},{1,65},{65,129},{129,193},{193,1... | collective-permute-start | bytes 1253384 | tf_op jit(solution)/shard_map/ppermute | solution.py:314
  162.3 14.0 %collective-permute-start.23 = (s16[272,768]{1,0:T(8,128)(2,1)S(1)}, s16[272,768]{1,0:T(8,128)(2,1)S(1)}, u32[]{:S(2)}, u32[]{:S(2)}) collective-permute-start(s16[272,768]{1,0:T(8,128)(2,1)S(1)} %get-tuple-element.39), channel_id=1, source_target_pairs={{0,64},{64,128},{128,192},{192,0},{1,65},{65,129},{129,193},{193,1... | collective-permute-start | bytes 1253384 | tf_op jit(solution)/shard_map/ppermute | solution.py:314
  162.7 15.0 %collective-permute-start.26 = (s16[272,768]{1,0:T(8,128)(2,1)S(1)}, s16[272,768]{1,0:T(8,128)(2,1)S(1)}, u32[]{:S(2)}, u32[]{:S(2)}) collective-permute-start(s16[272,768]{1,0:T(8,128)(2,1)S(1)} %get-tuple-element.42), channel_id=1, source_target_pairs={{0,192},{64,0},{128,64},{192,128},{1,193},{65,1},{129,65},{193,129... | collective-permute-start | bytes 1253384 | tf_op jit(solution)/shard_map/ppermute | solution.py:314

commit v5 on v4

--- a/solution.py
+++ b/solution.py
@@ -334,7 +334,7 @@
     here = z.astype(I32).reshape(1)
 
     ring = z_ring(*stage(tokens, routing.T))
-    packed = pack_grads(here, routing.T, grads.reshape(TOK * TOP, FF), [ring[2][0], ring[2][1], ring[6][0], ring[6][1]])
+    packed = pack_grads(here, routing.T, grads.reshape(TOK * TOP, FF), [])
     grads_in = to_owners(packed)
     by_z = regroup(grads_in, [*ring[3], *ring[5]])
     rows_out = [by_z[k] if k == 0 else shift(by_z[k], "z", k) for k in ORDER]

time: 180 us -> 173 us (0.961)
  waiting for transfers between devices: 81.2 us -> 74.2 us
    ppermute x27, waiting for transfers between devices: 78.2 us -> 71.2 us  [shift(): return lax.ppermute(value, axis, [(i, (i + by) % n) for i in range(n)])]
    unnamed x38 -> x44, local copies, waits for them, and re-layouts: 7.87 us -> 7.74 us
  transfers between devices with their start and end apart: 29 -> 29, of which waited for: 16 -> 19; matrix products, arithmetic and copies ran while one was open for 0% -> 0% of each run, Pallas kernels for 5% -> 6%
where the time goes in v5:
time: 173 us
  waiting for transfers between devices  74.2 us (43%)
  starting transfers between devices  52 us (30%)
  Pallas kernels  38.6 us (22%)
  local copies, waits for them, and re-layouts  7.74 us (4%)
    ppermute x27, waiting for transfers between devices, shift(): return lax.ppermute(value, axis, [(i, (i + by) % n) for i in range(n)])  71.2 us
    ppermute x27, starting transfers between devices, shift(): return lax.ppermute(value, axis, [(i, (i + by) % n) for i in range(n)])  43 us
    pallas_call x1, Pallas kernels, rotate_inputs(): pl.pallas_call(rotate_kernel, out_shape=jax.ShapeDtypeStruct((D, ROWS), B...  12.5 us
    all_to_all x2, starting transfers between devices, to_owners(): lax.all_to_all(value, ('y', 'c'), split_axis=0, concat_axis=0, tiled=True)  9.03 us
    unnamed x44, local copies, waits for them, and re-layouts  7.74 us
    pallas_call x1, Pallas kernels, pack_tokens(): pl.pallas_call(functools.partial(pack_tokens_kernel, n), out_shape=jax.Sh...  6.48 us
    pallas_call x1, Pallas kernels, pack_grads(): pl.pallas_call(pack_grads_kernel, out_shape=jax.ShapeDtypeStruct((N_YC, N...  4.8 us
  transfers between devices with their start and end apart: 29, of which 19 were waited for; matrix products, arithmetic and copies ran while one was open for 0% of the time, Pallas kernels for 6%

profile of v5, /device:TPU:6, one launch (start us, length us, event | category | flops | bytes accessed | tf_op | source)
XLA Modules:
  0.0 172.8 jit_solution(4008371492756229047)
XLA Ops:
  0.0 4.8 %shard_map.56 = bf16[8,128,768]{2,1,0:T(8,128)(2,1)} custom-call(s32[1]{0:T(128)} %bitcast.4.here_ref, s32[8,128]{1,0:T(8,128)} %bitcast.8, bf16[1024,768]{1,0:T(8,128)(2,1)} %bitcast.10), custom_call_target="tpu_custom_call" | custom-call | flops 1610612736 | bytes 3145728 | tf_op jit(solution)/shard_map/pallas_call | solution.py:86
  4.8 4.5 %all-to-all-start = ((bf16[8,128,768]{2,1,0:T(8,128)(2,1)}), bf16[8,128,768]{2,1,0:T(8,128)(2,1)S(1)}, u32[]{:S(2)}, u32[]{:S(2)}) async-start(bf16[8,128,768]{2,1,0:T(8,128)(2,1)} %shard_map.56), calls=%async_computation | async-start | bytes 3145728 | tf_op jit(solution)/shard_map/all_to_all | solution.py:318
  9.3 1.9 %shard_map.55 = (bf16[136,1024]{1,0:T(8,128)(2,1)}, bf16[128,1024]{1,0:T(8,128)(2,1)}) custom-call(bf16[128,2048]{1,0:T(8,128)(2,1)} %tokens_ref.1, s32[8,128]{1,0:T(8,128)} %bitcast.9), custom_call_target="tpu_custom_call" | custom-call | tf_op jit(solution)/shard_map/pallas_call | solution.py:57
  11.1 1.9 %collective-permute-start = (bf16[136,1024]{1,0:T(8,128)(2,1)}, bf16[136,1024]{1,0:T(8,128)(2,1)S(1)}, u32[]{:S(2)}, u32[]{:S(2)}) collective-permute-start(bf16[136,1024]{1,0:T(8,128)(2,1)} %get-tuple-element.24.refs_0_), channel_id=1, source_target_pairs={{0,8},{8,16},{16,24},{24,32},{32,40},{40,48},{48,56},{56,0},{1,9},... | collective-permute-start | bytes 835592 | tf_op jit(solution)/shard_map/ppermute | solution.py:314
  13.1 3.9 %collective-permute-start.8 = (bf16[128,1024]{1,0:T(8,128)(2,1)}, bf16[128,1024]{1,0:T(8,128)(2,1)S(1)}, u32[]{:S(2)}, u32[]{:S(2)}) collective-permute-start(bf16[128,1024]{1,0:T(8,128)(2,1)} %get-tuple-element.25.refs_8_), channel_id=1, source_target_pairs={{0,56},{8,0},{16,8},{24,16},{32,24},{40,32},{48,40},{56,48},{1,57}... | collective-permute-start | bytes 786440 | tf_op jit(solution)/shard_map/ppermute | solution.py:314
  17.0 2.0 %collective-permute-start.1 = (bf16[136,1024]{1,0:T(8,128)(2,1)}, bf16[136,1024]{1,0:T(8,128)(2,1)S(1)}, u32[]{:S(2)}, u32[]{:S(2)}) collective-permute-start(bf16[136,1024]{1,0:T(8,128)(2,1)} %get-tuple-element.24.refs_0_), channel_id=1, source_target_pairs={{0,56},{8,0},{16,8},{24,16},{32,24},{40,32},{48,40},{56,48},{1,57}... | collective-permute-start | bytes 835592 | tf_op jit(solution)/shard_map/ppermute | solution.py:314
  19.0 5.5 %collective-permute-done.refs_1_ = bf16[136,1024]{1,0:T(8,128)(2,1)S(1)} collective-permute-done((bf16[136,1024]{1,0:T(8,128)(2,1)}, bf16[136,1024]{1,0:T(8,128)(2,1)S(1)}, u32[]{:S(2)}, u32[]{:S(2)}) %collective-permute-start) | collective-permute-done | bytes 278560 | tf_op jit(solution)/shard_map/ppermute | solution.py:314
  24.6 3.3 %collective-permute-start.10 = (bf16[128,1024]{1,0:T(8,128)(2,1)S(1)}, bf16[128,1024]{1,0:T(8,128)(2,1)S(1)}, u32[]{:S(2)}, u32[]{:S(2)}) collective-permute-start(bf16[128,1024]{1,0:T(8,128)(2,1)S(1)} %collective-permute-done.8.refs_10_), channel_id=1, source_target_pairs={{0,56},{8,0},{16,8},{24,16},{32,24},{40,32},{48,40},{56,48},{1,57}... | collective-permute-start | bytes 786440 | tf_op jit(solution)/shard_map/ppermute | solution.py:314
  27.9 2.0 %collective-permute-done.1.refs_2_ = bf16[136,1024]{1,0:T(8,128)(2,1)S(1)} collective-permute-done((bf16[136,1024]{1,0:T(8,128)(2,1)}, bf16[136,1024]{1,0:T(8,128)(2,1)S(1)}, u32[]{:S(2)}, u32[]{:S(2)}) %collective-permute-start.1) | collective-permute-done | bytes 278560 | tf_op jit(solution)/shard_map/ppermute | solution.py:314
  29.9 3.6 %collective-permute-start.3 = (bf16[136,1024]{1,0:T(8,128)(2,1)S(1)}, bf16[136,1024]{1,0:T(8,128)(2,1)S(1)}, u32[]{:S(2)}, u32[]{:S(2)}) collective-permute-start(bf16[136,1024]{1,0:T(8,128)(2,1)S(1)} %collective-permute-done.1.refs_2_), channel_id=1, source_target_pairs={{0,56},{8,0},{16,8},{24,16},{32,24},{40,32},{48,40},{56,48},{1,57}... | collective-permute-start | bytes 835592 | tf_op jit(solution)/shard_map/ppermute | solution.py:314
  33.5 1.8 %collective-permute-done.2.refs_3_ = bf16[136,1024]{1,0:T(8,128)(2,1)S(1)} collective-permute-done((bf16[136,1024]{1,0:T(8,128)(2,1)S(1)}, bf16[136,1024]{1,0:T(8,128)(2,1)S(1)}, u32[]{:S(2)}, u32[]{:S(2)}) %collective-permute-start.2) | collective-permute-done | bytes 278560 | tf_op jit(solution)/shard_map/ppermute | solution.py:314
  35.3 5.6 %collective-permute-done.7.refs_9_ = bf16[128,1024]{1,0:T(8,128)(2,1)S(1)} collective-permute-done((bf16[128,1024]{1,0:T(8,128)(2,1)}, bf16[128,1024]{1,0:T(8,128)(2,1)S(1)}, u32[]{:S(2)}, u32[]{:S(2)}) %collective-permute-start.7) | collective-permute-done | bytes 262176 | tf_op jit(solution)/shard_map/ppermute | solution.py:314
  40.9 3.3 %collective-permute-start.12 = (bf16[128,1024]{1,0:T(8,128)(2,1)S(1)}, bf16[128,1024]{1,0:T(8,128)(2,1)S(1)}, u32[]{:S(2)}, u32[]{:S(2)}) collective-permute-start(bf16[128,1024]{1,0:T(8,128)(2,1)S(1)} %collective-permute-done.10.refs_12_), channel_id=1, source_target_pairs={{0,56},{8,0},{16,8},{24,16},{32,24},{40,32},{48,40},{56,48},{1,57}... | collective-permute-start | bytes 786440 | tf_op jit(solution)/shard_map/ppermute | solution.py:314
  44.7 2.2 %collective-permute-done.4.refs_5_.refs_1_ = bf16[136,1024]{1,0:T(8,128)(2,1)S(1)} collective-permute-done((bf16[136,1024]{1,0:T(8,128)(2,1)S(1)}, bf16[136,1024]{1,0:T(8,128)(2,1)S(1)}, u32[]{:S(2)}, u32[]{:S(2)}) %collective-permute-start.4) | collective-permute-done | bytes 278560 | tf_op jit(solution)/shard_map/ppermute | solution.py:314
  46.9 5.6 %collective-permute-done.9.refs_11_ = bf16[128,1024]{1,0:T(8,128)(2,1)S(1)} collective-permute-done((bf16[128,1024]{1,0:T(8,128)(2,1)S(1)}, bf16[128,1024]{1,0:T(8,128)(2,1)S(1)}, u32[]{:S(2)}, u32[]{:S(2)}) %collective-permute-start.9) | collective-permute-done | bytes 262176 | tf_op jit(solution)/shard_map/ppermute | solution.py:314
  52.5 3.2 %collective-permute-start.13 = (bf16[128,1024]{1,0:T(8,128)(2,1)S(1)}, bf16[128,1024]{1,0:T(8,128)(2,1)S(1)}, u32[]{:S(2)}, u32[]{:S(2)}) collective-permute-start(bf16[128,1024]{1,0:T(8,128)(2,1)S(1)} %collective-permute-done.12.refs_14_.refs_4_), channel_id=1, source_target_pairs={{0,56},{8,0},{16,8},{24,16},{32,24},{40,32},{48,40},{56,48},{1,57}... | collective-permute-start | bytes 786440 | tf_op jit(solution)/shard_map/ppermute | solution.py:314
  55.7 7.3 %collective-permute-done.11.refs_13_.refs_2_ = bf16[128,1024]{1,0:T(8,128)(2,1)S(1)} collective-permute-done((bf16[128,1024]{1,0:T(8,128)(2,1)S(1)}, bf16[128,1024]{1,0:T(8,128)(2,1)S(1)}, u32[]{:S(2)}, u32[]{:S(2)}) %collective-permute-start.11) | collective-permute-done | bytes 262176 | tf_op jit(solution)/shard_map/ppermute | solution.py:314
  64.0 1.1 copy-done.8
  65.1 6.5 %shard_map.57 = bf16[8,128,2048]{2,1,0:T(8,128)(2,1)} custom-call(s32[1]{0:T(128)} %bitcast.4.here_ref, bf16[136,1024]{1,0:T(8,128)(2,1)} %get-tuple-element.24.refs_0_, bf16[136,1024]{1,0:T(8,128)(2,1)} %copy-done.13, bf16[136,1024]{1,0:T(8,128)(2,1)} %copy-done.14, bf16[136,1024]{1,0:T(8,128)(2,1)} %copy-done.15, bf16[136,1024]{1,0:T(8,128)(2,1)} %copy-done.16, ...), custom_call_target="tpu_custom_call" | custom-call | flops 536870912 | bytes 8388608 | tf_op jit(solution)/shard_map/pallas_call | solution.py:135
  71.6 4.6 %all-to-all-start.1 = ((bf16[8,128,2048]{2,1,0:T(8,128)(2,1)}), bf16[8,128,2048]{2,1,0:T(8,128)(2,1)}, u32[]{:S(2)}, u32[]{:S(2)}) async-start(bf16[8,128,2048]{2,1,0:T(8,128)(2,1)} %shard_map.57), calls=%async_computation.1 | async-start | bytes 8388608 | tf_op jit(solution)/shard_map/all_to_all | solution.py:318
  76.2 2.7 %shard_map.58 = (bf16[128,768]{1,0:T(8,128)(2,1)}, bf16[128,768]{1,0:T(8,128)(2,1)}, bf16[128,768]{1,0:T(8,128)(2,1)}, bf16[128,768]{1,0:T(8,128)(2,1)}, bf16[12...) custom-call(bf16[8,128,768]{2,1,0:T(8,128)(2,1)} %copy-done.8, ...), custom_call_target="tpu_custom_call" | custom-call | tf_op jit(solution)/shard_map/pallas_call | solution.py:106
  78.9 3.2 %collective-permute-start.15 = (bf16[128,768]{1,0:T(8,128)(2,1)}, bf16[128,768]{1,0:T(8,128)(2,1)S(1)}, u32[]{:S(2)}, u32[]{:S(2)}) collective-permute-start(bf16[128,768]{1,0:T(8,128)(2,1)} %get-tuple-element.28), channel_id=1, source_target_pairs={{0,56},{8,0},{16,8},{24,16},{32,24},{40,32},{48,40},{56,48},{1,57}... | collective-permute-start | bytes 589832 | tf_op jit(solution)/shard_map/ppermute | solution.py:314
  82.1 4.1 %collective-permute-start.17 = (bf16[128,768]{1,0:T(8,128)(2,1)}, bf16[128,768]{1,0:T(8,128)(2,1)S(1)}, u32[]{:S(2)}, u32[]{:S(2)}) collective-permute-start(bf16[128,768]{1,0:T(8,128)(2,1)} %get-tuple-element.30), channel_id=1, source_target_pairs={{0,48},{8,56},{16,0},{24,8},{32,16},{40,24},{48,32},{56,40},{1,49}... | collective-permute-start | bytes 589832 | tf_op jit(solution)/shard_map/ppermute | solution.py:314
  86.5 1.8 %collective-permute-done.14.refs_1_ = bf16[128,768]{1,0:T(8,128)(2,1)S(1)} collective-permute-done((bf16[128,768]{1,0:T(8,128)(2,1)}, bf16[128,768]{1,0:T(8,128)(2,1)S(1)}, u32[]{:S(2)}, u32[]{:S(2)}) %collective-permute-start.14) | collective-permute-done | bytes 196640 | tf_op jit(solution)/shard_map/ppermute | solution.py:314
  88.2 3.1 %collective-permute-start.19 = (bf16[128,768]{1,0:T(8,128)(2,1)}, bf16[128,768]{1,0:T(8,128)(2,1)S(1)}, u32[]{:S(2)}, u32[]{:S(2)}) collective-permute-start(bf16[128,768]{1,0:T(8,128)(2,1)} %get-tuple-element.32), channel_id=1, source_target_pairs={{0,40},{8,48},{16,56},{24,0},{32,8},{40,16},{48,24},{56,32},{1,41}... | collective-permute-start | bytes 589832 | tf_op jit(solution)/shard_map/ppermute | solution.py:314
  91.3 1.3 collective-permute-done.15.refs_2_
  92.6 2.8 %collective-permute-start.20 = (bf16[128,768]{1,0:T(8,128)(2,1)}, bf16[128,768]{1,0:T(8,128)(2,1)S(1)}, u32[]{:S(2)}, u32[]{:S(2)}) collective-permute-start(bf16[128,768]{1,0:T(8,128)(2,1)} %get-tuple-element.33), channel_id=1, source_target_pairs={{0,32},{8,40},{16,48},{24,56},{32,0},{40,8},{48,16},{56,24},{1,33}... | collective-permute-start | bytes 589832 | tf_op jit(solution)/shard_map/ppermute | solution.py:314
  95.5 2.9 %collective-permute-done.16.refs_3_ = bf16[128,768]{1,0:T(8,128)(2,1)S(1)} collective-permute-done((bf16[128,768]{1,0:T(8,128)(2,1)}, bf16[128,768]{1,0:T(8,128)(2,1)S(1)}, u32[]{:S(2)}, u32[]{:S(2)}) %collective-permute-start.16) | collective-permute-done | bytes 196640 | tf_op jit(solution)/shard_map/ppermute | solution.py:314
  98.3 1.0 collective-permute-done.17.refs_4_
  99.3 9.8 %collective-permute-done.18.refs_5_ = bf16[128,768]{1,0:T(8,128)(2,1)S(1)} collective-permute-done((bf16[128,768]{1,0:T(8,128)(2,1)}, bf16[128,768]{1,0:T(8,128)(2,1)S(1)}, u32[]{:S(2)}, u32[]{:S(2)}) %collective-permute-start.18) | collective-permute-done | bytes 196640 | tf_op jit(solution)/shard_map/ppermute | solution.py:314
  109.8 6.5 %collective-permute-done.19.refs_6_ = bf16[128,768]{1,0:T(8,128)(2,1)S(1)} collective-permute-done((bf16[128,768]{1,0:T(8,128)(2,1)}, bf16[128,768]{1,0:T(8,128)(2,1)S(1)}, u32[]{:S(2)}, u32[]{:S(2)}) %collective-permute-start.19) | collective-permute-done | bytes 196640 | tf_op jit(solution)/shard_map/ppermute | solution.py:314
  117.7 0.9 copy-done.1
  118.6 0.9 copy-done.3
  121.4 1.4 shard_map.59.refs_0_.g_ref
  122.8 3.0 %all-to-all-done.1.rows_ref = bf16[8,128,2048]{2,1,0:T(8,128)(2,1)} async-done(((bf16[8,128,2048]{2,1,0:T(8,128)(2,1)}), bf16[8,128,2048]{2,1,0:T(8,128)(2,1)}, u32[]{:S(2)}, u32[]{:S(2)}) %all-to-all-start.1) | async-done | bytes 4194336 | tf_op jit(solution)/shard_map/all_to_all | solution.py:318
  125.8 12.5 %shard_map.60.a_ref = bf16[2048,1024]{1,0:T(8,128)(2,1)S(1)} custom-call(bf16[8,128,2048]{2,1,0:T(8,128)(2,1)} %all-to-all-done.1.rows_ref, bf16[1,2048,2048]{2,1,0:T(8,128)(2,1)} %basis_ref.1, bf16[1024,768]{1,0:T(8,128)(2,1)S(1)} %shard_map.59.refs_0_.g_ref), custom_call_target="tpu_custom_call" | custom-call | flops 8589934592 | bytes 16777216 | tf_op jit(solution)/shard_map/pallas_call | solution.py:157
  138.4 1.9 %shard_map.62 = (s16[272,768]{1,0:T(8,128)(2,1)S(1)}, s16[272,768]{1,0:T(8,128)(2,1)S(1)}) custom-call(s32[4]{0:T(128)S(1)} %pad_add_fusion.place_ref, bf16[2048,1024]{1,0:T(8,128)(2,1)S(1)} %shard_map.60.a_ref, bf16[1024,768]{1,0:T(8,128)(2,1)S(1)} %shard_map.59.refs_0_.g_ref), custom_call_target="tpu_custom_call" | custom-call | flops 805306368 | bytes 4194304 | tf_op jit(solution)/shard_map/pallas_call | solution.py:224
  141.1 1.5 collective-permute-start.22
  142.7 1.9 %shard_map.64 = (s16[272,768]{1,0:T(8,128)(2,1)S(1)}, s16[272,768]{1,0:T(8,128)(2,1)S(1)}) custom-call(s32[4]{0:T(128)S(1)} %pad_add_fusion.place_ref, bf16[2048,1024]{1,0:T(8,128)(2,1)S(1)} %shard_map.60.a_ref, bf16[1024,768]{1,0:T(8,128)(2,1)S(1)} %shard_map.59.refs_0_.g_ref), custom_call_target="tpu_custom_call" | custom-call | flops 805306368 | bytes 4194304 | tf_op jit(solution)/shard_map/pallas_call | solution.py:242
  145.5 2.4 %collective-permute-start.25 = (s16[272,768]{1,0:T(8,128)(2,1)S(1)}, s16[272,768]{1,0:T(8,128)(2,1)S(1)}, u32[]{:S(2)}, u32[]{:S(2)}) collective-permute-start(s16[272,768]{1,0:T(8,128)(2,1)S(1)} %get-tuple-element.41), channel_id=1, source_target_pairs={{0,64},{64,128},{128,192},{192,0},{1,65},{65,129},{129,193},{193,1... | collective-permute-start | bytes 1253384 | tf_op jit(solution)/shard_map/ppermute | solution.py:314
  147.9 2.3 %shard_map.61 = (f32[256,768]{1,0:T(8,128)S(1)}, f32[256,768]{1,0:T(8,128)S(1)}, f32[512,768]{1,0:T(8,128)S(1)}) custom-call(s32[4]{0:T(128)S(1)} %pad_add_fusion.place_ref, bf16[2048,1024]{1,0:T(8,128)(2,1)S(1)} %shard_map.60.a_ref, bf16[1024,768]{1,0:T(8,128)(2,1)S(1)} %shard_map.59.refs_0_.g_ref), custom_call_target="tpu_custom_call" | custom-call | flops 1610612736 | bytes 8388608 | tf_op jit(solution)/shard_map/pallas_call | solution.py:262
  150.3 2.9 %collective-permute-done.21.got_up_ref = s16[272,768]{1,0:T(8,128)(2,1)S(1)} collective-permute-done((s16[272,768]{1,0:T(8,128)(2,1)S(1)}, s16[272,768]{1,0:T(8,128)(2,1)S(1)}, u32[]{:S(2)}, u32[]{:S(2)}) %collective-permute-start.21) | collective-permute-done | bytes 417824 | tf_op jit(solution)/shard_map/ppermute | solution.py:314
  153.2 1.7 collective-permute-done.22.got_down_ref
  156.1 1.7 %collective-permute-start.26 = (s16[272,768]{1,0:T(8,128)(2,1)S(1)}, s16[272,768]{1,0:T(8,128)(2,1)S(1)}, u32[]{:S(2)}, u32[]{:S(2)}) collective-permute-start(s16[272,768]{1,0:T(8,128)(2,1)S(1)} %get-tuple-element.42), channel_id=1, source_target_pairs={{0,192},{64,0},{128,64},{192,128},{1,193},{65,1},{129,65},{193,129... | collective-permute-start | bytes 1253384 | tf_op jit(solution)/shard_map/ppermute | solution.py:314
  157.9 6.0 %collective-permute-done.24.top_b_ref = s16[272,768]{1,0:T(8,128)(2,1)S(1)} collective-permute-done((s16[272,768]{1,0:T(8,128)(2,1)S(1)}, s16[272,768]{1,0:T(8,128)(2,1)S(1)}, u32[]{:S(2)}, u32[]{:S(2)}) %collective-permute-start.24) | collective-permute-done | bytes 417824 | tf_op jit(solution)/shard_map/ppermute | solution.py:314
  163.9 5.9 %collective-permute-done.23.top_a_ref = s16[272,768]{1,0:T(8,128)(2,1)S(1)} collective-permute-done((s16[272,768]{1,0:T(8,128)(2,1)S(1)}, s16[272,768]{1,0:T(8,128)(2,1)S(1)}, u32[]{:S(2)}, u32[]{:S(2)}) %collective-permute-start.23) | collective-permute-done | bytes 417824 | tf_op jit(solution)/shard_map/ppermute | solution.py:314
  169.7 1.4 collective-permute-done.26.bottom_b_ref
  171.1 1.7 shard_map.65
  (66 shorter events, 8.5 us)
Async XLA Ops:
  4.8 59.1 %all-to-all-start = ((bf16[8,128,768]{2,1,0:T(8,128)(2,1)}), bf16[8,128,768]{2,1,0:T(8,128)(2,1)S(1)}, u32[]{:S(2)}, u32[]{:S(2)}) async-start(bf16[8,128,768]{2,1,0:T(8,128)(2,1)} %shard_map.56), calls=%async_computation | async-start | bytes 3145728 | tf_op jit(solution)/shard_map/all_to_all | solution.py:318
  11.1 13.4 %collective-permute-start = (bf16[136,1024]{1,0:T(8,128)(2,1)}, bf16[136,1024]{1,0:T(8,128)(2,1)S(1)}, u32[]{:S(2)}, u32[]{:S(2)}) collective-permute-start(bf16[136,1024]{1,0:T(8,128)(2,1)} %get-tuple-element.24.refs_0_), channel_id=1, source_target_pairs={{0,8},{8,16},{16,24},{24,32},{32,40},{40,48},{48,56},{56,0},{1,9},... | collective-permute-start | bytes 835592 | tf_op jit(solution)/shard_map/ppermute | solution.py:314
  13.1 11.5 %collective-permute-start.8 = (bf16[128,1024]{1,0:T(8,128)(2,1)}, bf16[128,1024]{1,0:T(8,128)(2,1)S(1)}, u32[]{:S(2)}, u32[]{:S(2)}) collective-permute-start(bf16[128,1024]{1,0:T(8,128)(2,1)} %get-tuple-element.25.refs_8_), channel_id=1, source_target_pairs={{0,56},{8,0},{16,8},{24,16},{32,24},{40,32},{48,40},{56,48},{1,57}... | collective-permute-start | bytes 786440 | tf_op jit(solution)/shard_map/ppermute | solution.py:314
  17.0 12.9 %collective-permute-start.1 = (bf16[136,1024]{1,0:T(8,128)(2,1)}, bf16[136,1024]{1,0:T(8,128)(2,1)S(1)}, u32[]{:S(2)}, u32[]{:S(2)}) collective-permute-start(bf16[136,1024]{1,0:T(8,128)(2,1)} %get-tuple-element.24.refs_0_), channel_id=1, source_target_pairs={{0,56},{8,0},{16,8},{24,16},{32,24},{40,32},{48,40},{56,48},{1,57}... | collective-permute-start | bytes 835592 | tf_op jit(solution)/shard_map/ppermute | solution.py:314
  24.5 39.4 %copy-start.13 = (bf16[136,1024]{1,0:T(8,128)(2,1)}, bf16[136,1024]{1,0:T(8,128)(2,1)S(1)}, u32[]{:S(2)}) copy-start(bf16[136,1024]{1,0:T(8,128)(2,1)S(1)} %collective-permute-done.refs_1_) | copy-start | bytes 835588
  24.5 10.7 %collective-permute-start.2 = (bf16[136,1024]{1,0:T(8,128)(2,1)S(1)}, bf16[136,1024]{1,0:T(8,128)(2,1)S(1)}, u32[]{:S(2)}, u32[]{:S(2)}) collective-permute-start(bf16[136,1024]{1,0:T(8,128)(2,1)S(1)} %collective-permute-done.refs_1_), channel_id=1, source_target_pairs={{0,8},{8,16},{16,24},{24,32},{32,40},{40,48},{48,56},{56,0},{1,9},... | collective-permute-start | bytes 835592 | tf_op jit(solution)/shard_map/ppermute | solution.py:314
  24.5 16.4 %collective-permute-start.7 = (bf16[128,1024]{1,0:T(8,128)(2,1)}, bf16[128,1024]{1,0:T(8,128)(2,1)S(1)}, u32[]{:S(2)}, u32[]{:S(2)}) collective-permute-start(bf16[128,1024]{1,0:T(8,128)(2,1)} %get-tuple-element.25.refs_8_), channel_id=1, source_target_pairs={{0,8},{8,16},{16,24},{24,32},{32,40},{40,48},{48,56},{56,0},{1,9},... | collective-permute-start | bytes 786440 | tf_op jit(solution)/shard_map/ppermute | solution.py:314
  24.6 16.4 %copy-start.17 = (bf16[128,1024]{1,0:T(8,128)(2,1)}, bf16[128,1024]{1,0:T(8,128)(2,1)S(1)}, u32[]{:S(2)}) copy-start(bf16[128,1024]{1,0:T(8,128)(2,1)S(1)} %collective-permute-done.8.refs_10_) | copy-start | bytes 786436
  24.6 16.3 %collective-permute-start.10 = (bf16[128,1024]{1,0:T(8,128)(2,1)S(1)}, bf16[128,1024]{1,0:T(8,128)(2,1)S(1)}, u32[]{:S(2)}, u32[]{:S(2)}) collective-permute-start(bf16[128,1024]{1,0:T(8,128)(2,1)S(1)} %collective-permute-done.8.refs_10_), channel_id=1, source_target_pairs={{0,56},{8,0},{16,8},{24,16},{32,24},{40,32},{48,40},{56,48},{1,57}... | collective-permute-start | bytes 786440 | tf_op jit(solution)/shard_map/ppermute | solution.py:314
  29.9 34.0 %copy-start.14 = (bf16[136,1024]{1,0:T(8,128)(2,1)}, bf16[136,1024]{1,0:T(8,128)(2,1)S(1)}, u32[]{:S(2)}) copy-start(bf16[136,1024]{1,0:T(8,128)(2,1)S(1)} %collective-permute-done.1.refs_2_) | copy-start | bytes 835588
  29.9 14.3 %collective-permute-start.3 = (bf16[136,1024]{1,0:T(8,128)(2,1)S(1)}, bf16[136,1024]{1,0:T(8,128)(2,1)S(1)}, u32[]{:S(2)}, u32[]{:S(2)}) collective-permute-start(bf16[136,1024]{1,0:T(8,128)(2,1)S(1)} %collective-permute-done.1.refs_2_), channel_id=1, source_target_pairs={{0,56},{8,0},{16,8},{24,16},{32,24},{40,32},{48,40},{56,48},{1,57}... | collective-permute-start | bytes 835592 | tf_op jit(solution)/shard_map/ppermute | solution.py:314
  35.3 27.8 %copy-start.15 = (bf16[136,1024]{1,0:T(8,128)(2,1)}, bf16[136,1024]{1,0:T(8,128)(2,1)S(1)}, u32[]{:S(2)}) copy-start(bf16[136,1024]{1,0:T(8,128)(2,1)S(1)} %collective-permute-done.2.refs_3_) | copy-start | bytes 835588
  35.3 11.6 %collective-permute-start.4 = (bf16[136,1024]{1,0:T(8,128)(2,1)S(1)}, bf16[136,1024]{1,0:T(8,128)(2,1)S(1)}, u32[]{:S(2)}, u32[]{:S(2)}) collective-permute-start(bf16[136,1024]{1,0:T(8,128)(2,1)S(1)} %collective-permute-done.2.refs_3_), channel_id=1, source_target_pairs={{0,8},{8,16},{16,24},{24,32},{32,40},{40,48},{48,56},{56,0},{1,9},... | collective-permute-start | bytes 835592 | tf_op jit(solution)/shard_map/ppermute | solution.py:314
  40.9 6.0 %copy-start.18 = (bf16[128,1024]{1,0:T(8,128)(2,1)}, bf16[128,1024]{1,0:T(8,128)(2,1)S(1)}, u32[]{:S(2)}) copy-start(bf16[128,1024]{1,0:T(8,128)(2,1)S(1)} %collective-permute-done.7.refs_9_) | copy-start | bytes 786436
  40.9 11.6 %collective-permute-start.9 = (bf16[128,1024]{1,0:T(8,128)(2,1)S(1)}, bf16[128,1024]{1,0:T(8,128)(2,1)S(1)}, u32[]{:S(2)}, u32[]{:S(2)}) collective-permute-start(bf16[128,1024]{1,0:T(8,128)(2,1)S(1)} %collective-permute-done.7.refs_9_), channel_id=1, source_target_pairs={{0,8},{8,16},{16,24},{24,32},{32,40},{40,48},{48,56},{56,0},{1,9},... | collective-permute-start | bytes 786440 | tf_op jit(solution)/shard_map/ppermute | solution.py:314
  40.9 22.1 %copy-start.19 = (bf16[128,1024]{1,0:T(8,128)(2,1)}, bf16[128,1024]{1,0:T(8,128)(2,1)S(1)}, u32[]{:S(2)}) copy-start(bf16[128,1024]{1,0:T(8,128)(2,1)S(1)} %collective-permute-done.10.refs_12_) | copy-start | bytes 786436
  40.9 11.6 %collective-permute-start.12 = (bf16[128,1024]{1,0:T(8,128)(2,1)S(1)}, bf16[128,1024]{1,0:T(8,128)(2,1)S(1)}, u32[]{:S(2)}, u32[]{:S(2)}) collective-permute-start(bf16[128,1024]{1,0:T(8,128)(2,1)S(1)} %collective-permute-done.10.refs_12_), channel_id=1, source_target_pairs={{0,56},{8,0},{16,8},{24,16},{32,24},{40,32},{48,40},{56,48},{1,57}... | collective-permute-start | bytes 786440 | tf_op jit(solution)/shard_map/ppermute | solution.py:314
  44.2 18.8 %copy-start.16 = (bf16[136,1024]{1,0:T(8,128)(2,1)}, bf16[136,1024]{1,0:T(8,128)(2,1)S(1)}, u32[]{:S(2)}) copy-start(bf16[136,1024]{1,0:T(8,128)(2,1)S(1)} %collective-permute-done.3.refs_4_) | copy-start | bytes 835588
  44.2 18.8 %collective-permute-start.5 = (bf16[136,1024]{1,0:T(8,128)(2,1)S(1)}, bf16[136,1024]{1,0:T(8,128)(2,1)S(1)}, u32[]{:S(2)}, u32[]{:S(2)}) collective-permute-start(bf16[136,1024]{1,0:T(8,128)(2,1)S(1)} %collective-permute-done.3.refs_4_), channel_id=1, source_target_pairs={{0,56},{8,0},{16,8},{24,16},{32,24},{40,32},{48,40},{56,48},{1,57}... | collective-permute-start | bytes 835592 | tf_op jit(solution)/shard_map/ppermute | solution.py:314
  46.9 17.0 %copy-start.9 = (bf16[136,1024]{1,0:T(8,128)(2,1)}, bf16[136,1024]{1,0:T(8,128)(2,1)S(1)}, u32[]{:S(2)}) copy-start(bf16[136,1024]{1,0:T(8,128)(2,1)S(1)} %collective-permute-done.4.refs_5_.refs_1_) | copy-start | bytes 835588
  46.9 17.0 %collective-permute-start.6 = (bf16[136,1024]{1,0:T(8,128)(2,1)S(1)}, bf16[136,1024]{1,0:T(8,128)(2,1)}, u32[]{:S(2)}, u32[]{:S(2)}) collective-permute-start(bf16[136,1024]{1,0:T(8,128)(2,1)S(1)} %collective-permute-done.4.refs_5_.refs_1_), channel_id=1, source_target_pairs={{0,8},{8,16},{16,24},{24,32},{32,40},{40,48},{48,56},{56,0},{1,9},... | collective-permute-start | bytes 835592 | tf_op jit(solution)/shard_map/ppermute | solution.py:314
  52.5 10.6 %copy-start.20 = (bf16[128,1024]{1,0:T(8,128)(2,1)}, bf16[128,1024]{1,0:T(8,128)(2,1)S(1)}, u32[]{:S(2)}) copy-start(bf16[128,1024]{1,0:T(8,128)(2,1)S(1)} %collective-permute-done.9.refs_11_) | copy-start | bytes 786436
  52.5 10.5 %collective-permute-start.11 = (bf16[128,1024]{1,0:T(8,128)(2,1)S(1)}, bf16[128,1024]{1,0:T(8,128)(2,1)S(1)}, u32[]{:S(2)}, u32[]{:S(2)}) collective-permute-start(bf16[128,1024]{1,0:T(8,128)(2,1)S(1)} %collective-permute-done.9.refs_11_), channel_id=1, source_target_pairs={{0,8},{8,16},{16,24},{24,32},{32,40},{40,48},{48,56},{56,0},{1,9},... | collective-permute-start | bytes 786440 | tf_op jit(solution)/shard_map/ppermute | solution.py:314
  52.5 11.4 %copy-start.11 = (bf16[128,1024]{1,0:T(8,128)(2,1)}, bf16[128,1024]{1,0:T(8,128)(2,1)S(1)}, u32[]{:S(2)}) copy-start(bf16[128,1024]{1,0:T(8,128)(2,1)S(1)} %collective-permute-done.12.refs_14_.refs_4_) | copy-start | bytes 786436
  52.5 10.5 %collective-permute-start.13 = (bf16[128,1024]{1,0:T(8,128)(2,1)S(1)}, bf16[128,1024]{1,0:T(8,128)(2,1)S(1)}, u32[]{:S(2)}, u32[]{:S(2)}) collective-permute-start(bf16[128,1024]{1,0:T(8,128)(2,1)S(1)} %collective-permute-done.12.refs_14_.refs_4_), channel_id=1, source_target_pairs={{0,56},{8,0},{16,8},{24,16},{32,24},{40,32},{48,40},{56,48},{1,57}... | collective-permute-start | bytes 786440 | tf_op jit(solution)/shard_map/ppermute | solution.py:314
  63.0 0.9 copy-start.12
  63.0 0.9 copy-start.10
  63.1 0.8 copy-start.21
  64.0 1.1 copy-start.8
  71.6 54.2 %all-to-all-start.1 = ((bf16[8,128,2048]{2,1,0:T(8,128)(2,1)}), bf16[8,128,2048]{2,1,0:T(8,128)(2,1)}, u32[]{:S(2)}, u32[]{:S(2)}) async-start(bf16[8,128,2048]{2,1,0:T(8,128)(2,1)} %shard_map.57), calls=%async_computation.1 | async-start | bytes 8388608 | tf_op jit(solution)/shard_map/all_to_all | solution.py:318
  76.2 41.5 %copy-start = (bf16[1,768,768]{2,1,0:T(8,128)(2,1)S(1)}, bf16[1,768,768]{2,1,0:T(8,128)(2,1)}, u32[]{:S(2)}) copy-start(bf16[1,768,768]{2,1,0:T(8,128)(2,1)} %refs_8_.1) | copy-start | bytes 3538948
  78.9 9.4 %collective-permute-start.14 = (bf16[128,768]{1,0:T(8,128)(2,1)}, bf16[128,768]{1,0:T(8,128)(2,1)S(1)}, u32[]{:S(2)}, u32[]{:S(2)}) collective-permute-start(bf16[128,768]{1,0:T(8,128)(2,1)} %get-tuple-element.27), channel_id=1, source_target_pairs={{0,8},{8,16},{16,24},{24,32},{32,40},{40,48},{48,56},{56,0},{1,9},... | collective-permute-start | bytes 589832 | tf_op jit(solution)/shard_map/ppermute | solution.py:314
  78.9 13.7 %collective-permute-start.15 = (bf16[128,768]{1,0:T(8,128)(2,1)}, bf16[128,768]{1,0:T(8,128)(2,1)S(1)}, u32[]{:S(2)}, u32[]{:S(2)}) collective-permute-start(bf16[128,768]{1,0:T(8,128)(2,1)} %get-tuple-element.28), channel_id=1, source_target_pairs={{0,56},{8,0},{16,8},{24,16},{32,24},{40,32},{48,40},{56,48},{1,57}... | collective-permute-start | bytes 589832 | tf_op jit(solution)/shard_map/ppermute | solution.py:314
  82.1 16.2 %collective-permute-start.16 = (bf16[128,768]{1,0:T(8,128)(2,1)}, bf16[128,768]{1,0:T(8,128)(2,1)S(1)}, u32[]{:S(2)}, u32[]{:S(2)}) collective-permute-start(bf16[128,768]{1,0:T(8,128)(2,1)} %get-tuple-element.29), channel_id=1, source_target_pairs={{0,16},{8,24},{16,32},{24,40},{32,48},{40,56},{48,0},{56,8},{1,17}... | collective-permute-start | bytes 589832 | tf_op jit(solution)/shard_map/ppermute | solution.py:314
  82.1 17.2 %collective-permute-start.17 = (bf16[128,768]{1,0:T(8,128)(2,1)}, bf16[128,768]{1,0:T(8,128)(2,1)S(1)}, u32[]{:S(2)}, u32[]{:S(2)}) collective-permute-start(bf16[128,768]{1,0:T(8,128)(2,1)} %get-tuple-element.30), channel_id=1, source_target_pairs={{0,48},{8,56},{16,0},{24,8},{32,16},{40,24},{48,32},{56,40},{1,49}... | collective-permute-start | bytes 589832 | tf_op jit(solution)/shard_map/ppermute | solution.py:314
  86.2 22.9 %collective-permute-start.18 = (bf16[128,768]{1,0:T(8,128)(2,1)}, bf16[128,768]{1,0:T(8,128)(2,1)S(1)}, u32[]{:S(2)}, u32[]{:S(2)}) collective-permute-start(bf16[128,768]{1,0:T(8,128)(2,1)} %get-tuple-element.31), channel_id=1, source_target_pairs={{0,24},{8,32},{16,40},{24,48},{32,56},{40,0},{48,8},{56,16},{1,25}... | collective-permute-start | bytes 589832 | tf_op jit(solution)/shard_map/ppermute | solution.py:314
  88.2 28.1 %collective-permute-start.19 = (bf16[128,768]{1,0:T(8,128)(2,1)}, bf16[128,768]{1,0:T(8,128)(2,1)S(1)}, u32[]{:S(2)}, u32[]{:S(2)}) collective-permute-start(bf16[128,768]{1,0:T(8,128)(2,1)} %get-tuple-element.32), channel_id=1, source_target_pairs={{0,40},{8,48},{16,56},{24,0},{32,8},{40,16},{48,24},{56,32},{1,41}... | collective-permute-start | bytes 589832 | tf_op jit(solution)/shard_map/ppermute | solution.py:314
  92.6 24.4 %collective-permute-start.20 = (bf16[128,768]{1,0:T(8,128)(2,1)}, bf16[128,768]{1,0:T(8,128)(2,1)S(1)}, u32[]{:S(2)}, u32[]{:S(2)}) collective-permute-start(bf16[128,768]{1,0:T(8,128)(2,1)} %get-tuple-element.33), channel_id=1, source_target_pairs={{0,32},{8,40},{16,48},{24,56},{32,0},{40,8},{48,16},{56,24},{1,33}... | collective-permute-start | bytes 589832 | tf_op jit(solution)/shard_map/ppermute | solution.py:314
  117.7 0.9 copy-start.1
  118.6 0.9 copy-start.3
  119.5 0.9 copy-start.5
  120.5 0.9 copy-start.7
  140.3 12.9 %collective-permute-start.21 = (s16[272,768]{1,0:T(8,128)(2,1)S(1)}, s16[272,768]{1,0:T(8,128)(2,1)S(1)}, u32[]{:S(2)}, u32[]{:S(2)}) collective-permute-start(s16[272,768]{1,0:T(8,128)(2,1)S(1)} %get-tuple-element.37), channel_id=1, source_target_pairs={{0,64},{64,128},{128,192},{192,0},{1,65},{65,129},{129,193},{193,1... | collective-permute-start | bytes 1253384 | tf_op jit(solution)/shard_map/ppermute | solution.py:314
  141.1 13.8 %collective-permute-start.22 = (s16[272,768]{1,0:T(8,128)(2,1)S(1)}, s16[272,768]{1,0:T(8,128)(2,1)S(1)}, u32[]{:S(2)}, u32[]{:S(2)}) collective-permute-start(s16[272,768]{1,0:T(8,128)(2,1)S(1)} %get-tuple-element.38), channel_id=1, source_target_pairs={{0,192},{64,0},{128,64},{192,128},{1,193},{65,1},{129,65},{193,129... | collective-permute-start | bytes 1253384 | tf_op jit(solution)/shard_map/ppermute | solution.py:314
  144.6 19.2 %collective-permute-start.24 = (s16[272,768]{1,0:T(8,128)(2,1)S(1)}, s16[272,768]{1,0:T(8,128)(2,1)S(1)}, u32[]{:S(2)}, u32[]{:S(2)}) collective-permute-start(s16[272,768]{1,0:T(8,128)(2,1)S(1)} %get-tuple-element.40), channel_id=1, source_target_pairs={{0,192},{64,0},{128,64},{192,128},{1,193},{65,1},{129,65},{193,129... | collective-permute-start | bytes 1253384 | tf_op jit(solution)/shard_map/ppermute | solution.py:314
  145.5 18.3 %collective-permute-start.25 = (s16[272,768]{1,0:T(8,128)(2,1)S(1)}, s16[272,768]{1,0:T(8,128)(2,1)S(1)}, u32[]{:S(2)}, u32[]{:S(2)}) collective-permute-start(s16[272,768]{1,0:T(8,128)(2,1)S(1)} %get-tuple-element.41), channel_id=1, source_target_pairs={{0,64},{64,128},{128,192},{192,0},{1,65},{65,129},{129,193},{193,1... | collective-permute-start | bytes 1253384 | tf_op jit(solution)/shard_map/ppermute | solution.py:314
  155.8 13.9 %collective-permute-start.23 = (s16[272,768]{1,0:T(8,128)(2,1)S(1)}, s16[272,768]{1,0:T(8,128)(2,1)S(1)}, u32[]{:S(2)}, u32[]{:S(2)}) collective-permute-start(s16[272,768]{1,0:T(8,128)(2,1)S(1)} %get-tuple-element.39), channel_id=1, source_target_pairs={{0,64},{64,128},{128,192},{192,0},{1,65},{65,129},{129,193},{193,1... | collective-permute-start | bytes 1253384 | tf_op jit(solution)/shard_map/ppermute | solution.py:314
  156.1 15.0 %collective-permute-start.26 = (s16[272,768]{1,0:T(8,128)(2,1)S(1)}, s16[272,768]{1,0:T(8,128)(2,1)S(1)}, u32[]{:S(2)}, u32[]{:S(2)}) collective-permute-start(s16[272,768]{1,0:T(8,128)(2,1)S(1)} %get-tuple-element.42), channel_id=1, source_target_pairs={{0,192},{64,0},{128,64},{192,128},{1,193},{65,1},{129,65},{193,129... | collective-permute-start | bytes 1253384 | tf_op jit(solution)/shard_map/ppermute | solution.py:314
  (3 other events, 2.0 us)
